TPU v7x, 32 devices: a whole 2x2x4 slice. The times are simulated.
32 devices in a mesh: comp: 2 (over core), tile: 16 (over z, y, x).
Axes of the slice: x: 2, y: 2, z: 4, core: 2. Of those that a mesh axis runs over, the one named last changes fastest.
Arguments:
- state: float32 [2, 256, 256], P('comp', 'tile'), may hold values from -6 to 6
- coeff: float32 [2, 256, 256], P('comp', 'tile'), may hold values from 0.3 to 3
- vertical: int32 [256, 256], P('tile'), may hold values from 0 to 5
- send_cell: int32 [256, 4096], P(('comp', 'tile')), may hold values from 0 to 4095, as said below
- incoming_marine_slot: int32 [256, 4096], P(('comp', 'tile')), may hold values from 0 to 4095, as said below
- remap_weight: float32 [256, 4096], P(('comp', 'tile')), as said below
Outputs:
- exchanged_pair: float32 [2, 256, 256], P('comp', 'tile')
Inputs may be any that keep to these rules, and one draw needn't show every extreme that they name: `send_cell`: rows of ocean partitions (index 128 and above) are 0. Rows d = 3 and d = 5 of every atmosphere partition are full; rows 0 and 1, 2 and 4, 6 and 7 come in pairs whose live slots fill one row together. Live slots lead each row; dead slots hold cell 0. Every atmosphere cell is named by exactly five live slots of its partition. `incoming_marine_slot`: rows of atmosphere partitions are 0. Row (16 + t) * 8 + d names the ocean cell of the slot that send_cell row ((t - d + 4) mod 16) * 8 + d names; dead slots hold 0. `remap_weight`: live slots have weights of at least 0.25; dead slots and rows of ocean partitions 0.
All inputs are finite; a program needn't handle non-finite values.
Results may differ from a plain program's by a relative error of at most 0.00002.
Values sent between devices are 32-bit elements; how exact they have to be, the bound alone decides.
No kernel may reach another device: no remote copies, remote signals or barrier semaphores. Data moves between devices by JAX's collectives and lax.ppermute only.
A program may use at most 64 MiB of HBM per device.

v0:
```python
import jax
import jax.numpy as jnp
from jax import lax
from jax.sharding import PartitionSpec as P

SPAN = 8
SWEEPS = 20


def with_halo(array, sides, width):
    for axis, dim in sides:
        devices, length = (lax.axis_size(axis), array.shape[dim])
        up = [(i, (i + 1) % devices) for i in range(devices)]
        down = [(j, i) for i, j in up]
        last = lax.slice_in_dim(array, length - width, length, axis=dim)
        initial = lax.slice_in_dim(array, 0, width, axis=dim)
        before = lax.ppermute(last, axis, up)
        after = lax.ppermute(initial, axis, down)
        array = jnp.concatenate([before, array, after], axis=dim)
    return array


def shards(state, coeff, vertical, send_cell, incoming_marine_slot, remap_weight):
    mesh_lines = state.shape[1]
    line_length = state.shape[2]
    cells = mesh_lines * line_length
    tiles = lax.axis_size("tile")
    model_index = lax.axis_index("comp")
    tile_index = lax.axis_index("tile")
    middle = SPAN // 2
    mesh_quantity = state[0]
    rate = coeff[0]
    padded = with_halo(mesh_quantity, (("tile", 0),), 1)
    near = padded[:-2] + padded[2:] + jnp.roll(mesh_quantity, 1, 1) + jnp.roll(mesh_quantity, -1, 1)
    air_flux = (rate * (mesh_quantity + 0.2 * (near - 4.0 * mesh_quantity))).reshape(-1)
    offsets = jnp.arange(SPAN, dtype=jnp.int32)
    ahead_rows = tiles + (tile_index + offsets - middle) % tiles
    behind_rows = (tile_index - offsets + middle) % tiles
    zeros_flat = jnp.zeros((cells,), jnp.float32)
    outgoing = remap_weight * jnp.take(air_flux, send_cell)
    buffer = jnp.zeros((2 * tiles, cells), jnp.float32).at[ahead_rows].set(outgoing)
    arrived = lax.all_to_all(buffer, ("comp", "tile"), split_axis=0, concat_axis=0, tiled=True)
    incoming = arrived[behind_rows]
    ocean_source = zeros_flat.at[incoming_marine_slot.reshape(-1)].add(incoming.reshape(-1))
    source_mesh = ocean_source.reshape(mesh_lines, line_length)
    rhs = source_mesh + mesh_quantity
    diag = rate + 3.0
    col_ids = jnp.arange(line_length, dtype=jnp.int32)[None, :]
    zeros_grid = jnp.zeros((mesh_lines, line_length), jnp.float32)
    row_ids = jnp.arange(mesh_lines, dtype=jnp.int32)[:, None]
    up_down = vertical // 3
    sideways = vertical % 3 - 1
    index = (row_ids + 2 * up_down) * line_length + (col_ids + sideways) % line_length

    def sweep_once(step, skin_quantity):
        extended = with_halo(skin_quantity, (("tile", 0),), 1)
        beside_all = (
            jnp.roll(skin_quantity, 1, 1)
            + jnp.roll(skin_quantity, -1, 1)
            + jnp.take(extended.reshape(-1), index)
        )
        return (rhs + beside_all) / diag

    skin_quantity = lax.fori_loop(0, SWEEPS, sweep_once, zeros_grid)
    linear_skin_heat = (mesh_quantity + 0.5 * skin_quantity - 0.25 * source_mesh).reshape(-1)
    share_accumulated = zeros_flat.at[send_cell.reshape(-1)].add(remap_weight.reshape(-1))
    backward_transfers = jnp.take(linear_skin_heat, incoming_marine_slot)
    buffer_back = jnp.zeros((2 * tiles, cells), jnp.float32).at[behind_rows].set(backward_transfers)
    arrived_back = lax.all_to_all(
        buffer_back, ("comp", "tile"), split_axis=0, concat_axis=0, tiled=True
    )
    incoming_back = arrived_back[ahead_rows]
    overall_quantity = zeros_flat.at[send_cell.reshape(-1)].add(
        (remap_weight * incoming_back).reshape(-1)
    )
    safe_share_total = share_accumulated + (model_index != 0).astype(jnp.float32)
    measured_skin_heat = (overall_quantity / safe_share_total).reshape(mesh_lines, line_length)
    exchanged_pair = jnp.where(model_index == 0, measured_skin_heat, skin_quantity)
    return exchanged_pair[None]


def solution(mesh):
    in_specs = (
        P("comp", "tile", None),
        P("comp", "tile", None),
        P("tile", None),
        P(("comp", "tile"), None),
        P(("comp", "tile"), None),
        P(("comp", "tile"), None),
    )
    out_specs = P("comp", "tile", None)
    return jax.shard_map(shards, mesh=mesh, in_specs=in_specs, out_specs=out_specs, check_vma=False)
```

profile of v0, /device:TPU:0, one launch (start us, length us, event | category | flops | bytes accessed | tf_op | source)
XLA Modules:
  0.0 1667.0 jit_solution(16128943397865568365)
XLA Ops:
  3.7 4.0 collective-permute-start.3
  12.2 180.5 %gather_fusion.3 = f32[32768]{0:T(1024)S(1)} fusion(f32[4096]{0:T(1024)S(1)} %bitcast.64, s32[32768]{0:T(1024)S(1)} %broadcast_clamp_fusion.2), kind=kCustom, calls=%fused_computation.clone | custom fusion | bytes 393216 | tf_op jit(solution)/shard_map/jit(_take)/gather | solution.py:40
  199.3 16.6 all-to-all-done
  216.8 226.3 %scatter_custom_fusion.1 = f32[4096]{0:T(1024)S(1)} fusion(s32[32768]{0:T(1024)S(1)} %bitcast.81, f32[32768]{0:T(1024)S(1)} %bitcast.85, f32[]{:T(128)} %constant.102.clone.1), kind=kCustom, calls=%fused_computation.83 | custom fusion | flops 32768 | bytes 16388 | tf_op jit(solution)/shard_map/scatter-add | solution.py:44
  443.2 609.9 %while.11 = (s32[]{:T(128)}, f32[16,256]{1,0:T(8,128)S(1)}, s32[16,256]{1,0:T(8,128)S(1)}, f32[16,256]{1,0:T(8,128)S(1)}, f32[16,256]{1,0:T(8,128)S(1)}, /*index=5*/s32[]{:T(128)}, s32[]{:T(128)}) while((s32[]{:T(128)}, f32[16,256]{1,0:T(8,128)S(1)}, s32[16,256]{1,0:T(8,128)S(1)}, f32[16,256]{1,0:T(8,128)S(1)}, ...), condition=%wide.region_3.5_spmd.clone, body=%wide.region_2.4_spmd.clone.sunk | while | flops 82947 | bytes 479399 | solution.py:64
  446.8 4.4 collective-permute-done.1
  451.2 23.0 %gather_fusion = f32[4096]{0:T(1024)S(1)} fusion(f32[4608]{0:T(1024)S(1)} %reshape.349, s32[4096]{0:T(1024)S(1)} %broadcast_clamp_fusion.4), kind=kCustom, calls=%fused_computation.1.clone.clone.1 | custom fusion | bytes 49152 | tf_op jit(solution)/shard_map/while/body/eval_jaxpr/jit(_take)/gather | solution.py:60
  478.0 3.7 collective-permute-done.1
  481.7 23.0 %gather_fusion = f32[4096]{0:T(1024)S(1)} fusion(f32[4608]{0:T(1024)S(1)} %reshape.349, s32[4096]{0:T(1024)S(1)} %broadcast_clamp_fusion.4), kind=kCustom, calls=%fused_computation.1.clone.clone.1 | custom fusion | bytes 49152 | tf_op jit(solution)/shard_map/while/body/eval_jaxpr/jit(_take)/gather | solution.py:60
  508.5 3.7 collective-permute-done.1
  512.1 23.0 %gather_fusion = f32[4096]{0:T(1024)S(1)} fusion(f32[4608]{0:T(1024)S(1)} %reshape.349, s32[4096]{0:T(1024)S(1)} %broadcast_clamp_fusion.4), kind=kCustom, calls=%fused_computation.1.clone.clone.1 | custom fusion | bytes 49152 | tf_op jit(solution)/shard_map/while/body/eval_jaxpr/jit(_take)/gather | solution.py:60
  538.9 3.7 collective-permute-done.1
  542.6 23.0 %gather_fusion = f32[4096]{0:T(1024)S(1)} fusion(f32[4608]{0:T(1024)S(1)} %reshape.349, s32[4096]{0:T(1024)S(1)} %broadcast_clamp_fusion.4), kind=kCustom, calls=%fused_computation.1.clone.clone.1 | custom fusion | bytes 49152 | tf_op jit(solution)/shard_map/while/body/eval_jaxpr/jit(_take)/gather | solution.py:60
  569.4 3.7 collective-permute-done.1
  573.1 23.0 %gather_fusion = f32[4096]{0:T(1024)S(1)} fusion(f32[4608]{0:T(1024)S(1)} %reshape.349, s32[4096]{0:T(1024)S(1)} %broadcast_clamp_fusion.4), kind=kCustom, calls=%fused_computation.1.clone.clone.1 | custom fusion | bytes 49152 | tf_op jit(solution)/shard_map/while/body/eval_jaxpr/jit(_take)/gather | solution.py:60
  599.8 3.7 collective-permute-done.1
  603.5 23.0 %gather_fusion = f32[4096]{0:T(1024)S(1)} fusion(f32[4608]{0:T(1024)S(1)} %reshape.349, s32[4096]{0:T(1024)S(1)} %broadcast_clamp_fusion.4), kind=kCustom, calls=%fused_computation.1.clone.clone.1 | custom fusion | bytes 49152 | tf_op jit(solution)/shard_map/while/body/eval_jaxpr/jit(_take)/gather | solution.py:60
  630.3 3.7 collective-permute-done.1
  634.0 23.0 %gather_fusion = f32[4096]{0:T(1024)S(1)} fusion(f32[4608]{0:T(1024)S(1)} %reshape.349, s32[4096]{0:T(1024)S(1)} %broadcast_clamp_fusion.4), kind=kCustom, calls=%fused_computation.1.clone.clone.1 | custom fusion | bytes 49152 | tf_op jit(solution)/shard_map/while/body/eval_jaxpr/jit(_take)/gather | solution.py:60
  660.8 3.7 collective-permute-done.1
  664.4 23.0 %gather_fusion = f32[4096]{0:T(1024)S(1)} fusion(f32[4608]{0:T(1024)S(1)} %reshape.349, s32[4096]{0:T(1024)S(1)} %broadcast_clamp_fusion.4), kind=kCustom, calls=%fused_computation.1.clone.clone.1 | custom fusion | bytes 49152 | tf_op jit(solution)/shard_map/while/body/eval_jaxpr/jit(_take)/gather | solution.py:60
  691.2 3.7 collective-permute-done.1
  694.9 23.0 %gather_fusion = f32[4096]{0:T(1024)S(1)} fusion(f32[4608]{0:T(1024)S(1)} %reshape.349, s32[4096]{0:T(1024)S(1)} %broadcast_clamp_fusion.4), kind=kCustom, calls=%fused_computation.1.clone.clone.1 | custom fusion | bytes 49152 | tf_op jit(solution)/shard_map/while/body/eval_jaxpr/jit(_take)/gather | solution.py:60
  721.7 3.7 collective-permute-done.1
  725.3 23.0 %gather_fusion = f32[4096]{0:T(1024)S(1)} fusion(f32[4608]{0:T(1024)S(1)} %reshape.349, s32[4096]{0:T(1024)S(1)} %broadcast_clamp_fusion.4), kind=kCustom, calls=%fused_computation.1.clone.clone.1 | custom fusion | bytes 49152 | tf_op jit(solution)/shard_map/while/body/eval_jaxpr/jit(_take)/gather | solution.py:60
  752.1 3.7 collective-permute-done.1
  755.8 23.0 %gather_fusion = f32[4096]{0:T(1024)S(1)} fusion(f32[4608]{0:T(1024)S(1)} %reshape.349, s32[4096]{0:T(1024)S(1)} %broadcast_clamp_fusion.4), kind=kCustom, calls=%fused_computation.1.clone.clone.1 | custom fusion | bytes 49152 | tf_op jit(solution)/shard_map/while/body/eval_jaxpr/jit(_take)/gather | solution.py:60
  782.6 3.7 collective-permute-done.1
  786.3 23.0 %gather_fusion = f32[4096]{0:T(1024)S(1)} fusion(f32[4608]{0:T(1024)S(1)} %reshape.349, s32[4096]{0:T(1024)S(1)} %broadcast_clamp_fusion.4), kind=kCustom, calls=%fused_computation.1.clone.clone.1 | custom fusion | bytes 49152 | tf_op jit(solution)/shard_map/while/body/eval_jaxpr/jit(_take)/gather | solution.py:60
  813.0 3.7 collective-permute-done.1
  816.7 23.0 %gather_fusion = f32[4096]{0:T(1024)S(1)} fusion(f32[4608]{0:T(1024)S(1)} %reshape.349, s32[4096]{0:T(1024)S(1)} %broadcast_clamp_fusion.4), kind=kCustom, calls=%fused_computation.1.clone.clone.1 | custom fusion | bytes 49152 | tf_op jit(solution)/shard_map/while/body/eval_jaxpr/jit(_take)/gather | solution.py:60
  843.5 3.7 collective-permute-done.1
  847.2 23.0 %gather_fusion = f32[4096]{0:T(1024)S(1)} fusion(f32[4608]{0:T(1024)S(1)} %reshape.349, s32[4096]{0:T(1024)S(1)} %broadcast_clamp_fusion.4), kind=kCustom, calls=%fused_computation.1.clone.clone.1 | custom fusion | bytes 49152 | tf_op jit(solution)/shard_map/while/body/eval_jaxpr/jit(_take)/gather | solution.py:60
  874.0 3.7 collective-permute-done.1
  877.6 23.0 %gather_fusion = f32[4096]{0:T(1024)S(1)} fusion(f32[4608]{0:T(1024)S(1)} %reshape.349, s32[4096]{0:T(1024)S(1)} %broadcast_clamp_fusion.4), kind=kCustom, calls=%fused_computation.1.clone.clone.1 | custom fusion | bytes 49152 | tf_op jit(solution)/shard_map/while/body/eval_jaxpr/jit(_take)/gather | solution.py:60
  904.4 3.7 collective-permute-done.1
  908.1 23.0 %gather_fusion = f32[4096]{0:T(1024)S(1)} fusion(f32[4608]{0:T(1024)S(1)} %reshape.349, s32[4096]{0:T(1024)S(1)} %broadcast_clamp_fusion.4), kind=kCustom, calls=%fused_computation.1.clone.clone.1 | custom fusion | bytes 49152 | tf_op jit(solution)/shard_map/while/body/eval_jaxpr/jit(_take)/gather | solution.py:60
  934.9 3.7 collective-permute-done.1
  938.6 23.0 %gather_fusion = f32[4096]{0:T(1024)S(1)} fusion(f32[4608]{0:T(1024)S(1)} %reshape.349, s32[4096]{0:T(1024)S(1)} %broadcast_clamp_fusion.4), kind=kCustom, calls=%fused_computation.1.clone.clone.1 | custom fusion | bytes 49152 | tf_op jit(solution)/shard_map/while/body/eval_jaxpr/jit(_take)/gather | solution.py:60
  965.3 3.7 collective-permute-done.1
  969.0 23.0 %gather_fusion = f32[4096]{0:T(1024)S(1)} fusion(f32[4608]{0:T(1024)S(1)} %reshape.349, s32[4096]{0:T(1024)S(1)} %broadcast_clamp_fusion.4), kind=kCustom, calls=%fused_computation.1.clone.clone.1 | custom fusion | bytes 49152 | tf_op jit(solution)/shard_map/while/body/eval_jaxpr/jit(_take)/gather | solution.py:60
  995.8 3.7 collective-permute-done.1
  999.5 23.0 %gather_fusion = f32[4096]{0:T(1024)S(1)} fusion(f32[4608]{0:T(1024)S(1)} %reshape.349, s32[4096]{0:T(1024)S(1)} %broadcast_clamp_fusion.4), kind=kCustom, calls=%fused_computation.1.clone.clone.1 | custom fusion | bytes 49152 | tf_op jit(solution)/shard_map/while/body/eval_jaxpr/jit(_take)/gather | solution.py:60
  1026.2 3.7 collective-permute-done.1
  1029.9 23.0 %gather_fusion = f32[4096]{0:T(1024)S(1)} fusion(f32[4608]{0:T(1024)S(1)} %reshape.349, s32[4096]{0:T(1024)S(1)} %broadcast_clamp_fusion.4), kind=kCustom, calls=%fused_computation.1.clone.clone.1 | custom fusion | bytes 49152 | tf_op jit(solution)/shard_map/while/body/eval_jaxpr/jit(_take)/gather | solution.py:60
  1053.1 180.5 %gather_fusion.4 = f32[32768]{0:T(1024)S(1)} fusion(f32[4096]{0:T(1024)S(1)} %bitcast.65, s32[32768]{0:T(1024)S(1)} %broadcast_clamp_fusion.1), kind=kCustom, calls=%fused_computation.2.clone | custom fusion | bytes 393216 | tf_op jit(solution)/shard_map/jit(_take)/gather | solution.py:67
  1238.7 213.3 %scatter_custom_fusion.4 = f32[4096]{0:T(1024)S(1)} fusion(s32[32768]{0:T(1024)S(1)} %bitcast.82, f32[32768]{0:T(1024)S(1)} %bitcast.86, f32[]{:T(128)S(6)} %convert_element_type.3), kind=kCustom, calls=%fused_computation.79 | custom fusion | flops 32768 | bytes 16388 | tf_op jit(solution)/shard_map/scatter-add | solution.py:66
  1453.0 213.3 %scatter_custom_fusion.3 = f32[4096]{0:T(1024)S(1)} fusion(s32[32768]{0:T(1024)S(1)} %bitcast.83, f32[32768]{0:T(1024)S(1)} %bitcast.84, f32[]{:T(128)} %constant.102.clone.1), kind=kCustom, calls=%fused_computation.81 | custom fusion | flops 32768 | bytes 16388 | tf_op jit(solution)/shard_map/scatter-add | solution.py:73
  (340 shorter events, 96.5 us)
Async XLA Ops:
  0.7 10.7 collective-permute-start.2
  3.7 7.8 collective-permute-start.3
  7.7 0.9 copy-start.3
  9.6 0.9 copy-start.2
  192.8 0.9 copy-start
  192.8 1.0 copy-start.1
  195.9 19.9 %all-to-all-start = ((f32[32,1,4096]{2,1,0:T(1,128)}), f32[32,1,4096]{2,1,0:T(1,128)S(1)}, u32[]{:S(2)}, u32[]{:S(2)}) async-start(f32[32,1,4096]{2,1,0:T(1,128)} %all_to_all.16), calls=%async_computation | async-start | bytes 1048576 | tf_op jit(solution)/shard_map/all_to_all | solution.py:42
  443.2 3.6 collective-permute-start
  444.0 7.2 collective-permute-start.1
  474.4 3.6 collective-permute-start
  474.4 7.2 collective-permute-start.1
  504.8 3.6 collective-permute-start
  504.9 7.2 collective-permute-start.1
  535.3 3.6 collective-permute-start
  535.4 7.2 collective-permute-start.1
  565.8 3.6 collective-permute-start
  565.8 7.2 collective-permute-start.1
  596.2 3.6 collective-permute-start
  596.3 7.2 collective-permute-start.1
  626.7 3.6 collective-permute-start
  626.7 7.2 collective-permute-start.1
  657.1 3.6 collective-permute-start
  657.2 7.2 collective-permute-start.1
  687.6 3.6 collective-permute-start
  687.7 7.2 collective-permute-start.1
  718.0 3.6 collective-permute-start
  718.1 7.2 collective-permute-start.1
  748.5 3.6 collective-permute-start
  748.6 7.2 collective-permute-start.1
  779.0 3.6 collective-permute-start
  779.0 7.2 collective-permute-start.1
  809.4 3.6 collective-permute-start
  809.5 7.2 collective-permute-start.1
  839.9 3.6 collective-permute-start
  839.9 7.2 collective-permute-start.1
  870.3 3.6 collective-permute-start
  870.4 7.2 collective-permute-start.1
  900.8 3.6 collective-permute-start
  900.9 7.2 collective-permute-start.1
  931.3 3.6 collective-permute-start
  931.3 7.2 collective-permute-start.1
  961.7 3.6 collective-permute-start
  961.8 7.2 collective-permute-start.1
  992.2 3.6 collective-permute-start
  992.2 7.2 collective-permute-start.1
  1022.6 3.6 collective-permute-start
  1022.7 7.2 collective-permute-start.1
  1235.9 216.1 %all-to-all-start.1 = ((f32[32,1,4096]{2,1,0:T(1,128)}), f32[32,1,4096]{2,1,0:T(1,128)S(1)}, u32[]{:S(2)}, u32[]{:S(2)}) async-start(f32[32,1,4096]{2,1,0:T(1,128)} %copy.7), calls=%async_computation.1 | async-start | bytes 1048576 | tf_op jit(solution)/shard_map/all_to_all | solution.py:69
  (2 other events, 1.4 us)
where the time goes:
time: 1690 us; the launch traced here: 1670 us
  local copies, waits for them, and re-layouts  835 us (49%)
  other arithmetic  659 us (39%)
  waiting for transfers between devices  118 us (7%)
  starting transfers between devices  54.1 us (3%)
    gather x40, local copies, waits for them, and re-layouts, sweep_once(): jnp.take(extended.reshape(-1), index)  461 us
    scatter-add x1, other arithmetic, shards(): zeros_flat.at[incoming_marine_slot.reshape(-1)].add(incoming.reshape(-1))  226 us
    scatter-add x1, other arithmetic, shards(): zeros_flat.at[send_cell.reshape(-1)].add(remap_weight.reshape(-1))  213 us
    scatter-add x1, other arithmetic, shards(): zeros_flat.at[send_cell.reshape(-1)]  213 us
    gather x2, local copies, waits for them, and re-layouts, shards(): backward_transfers = jnp.take(linear_skin_heat, incoming_marine_slot)  181 us
    gather x2, local copies, waits for them, and re-layouts, shards(): outgoing = remap_weight * jnp.take(air_flux, send_cell)  181 us
    ppermute x21, waiting for transfers between devices, with_halo(): before = lax.ppermute(last, axis, up)  73.9 us
    ppermute x21, starting transfers between devices, with_halo(): before = lax.ppermute(last, axis, up)  42.4 us
  transfers between devices with their start and end apart: 44, of which 41 were waited for; matrix products, arithmetic and copies ran while one was open for 13% of the time, Pallas kernels for 0%

commit v1 on v0

v1 whole, which is shorter than its diff:
```python
import jax
import jax.experimental.pallas as pl
import jax.experimental.pallas.tpu as pltpu
import jax.numpy as jnp
from jax import lax
from jax.sharding import PartitionSpec as P

SPAN = 8
SWEEPS = 20
MIDDLE = SPAN // 2
F32 = jnp.float32
BF16 = jnp.bfloat16
I32 = jnp.int32
CONTRACT_LANES = (((1,), (1,)), ((), ()))
GRID = ("comp", "tile")


def call(kernel, shapes, *operands, scratch=()):
    out = [jax.ShapeDtypeStruct(shape, F32) for shape in shapes]
    return pl.pallas_call(
        kernel,
        out_shape=out,
        in_specs=[pl.BlockSpec(memory_space=pltpu.VMEM)] * len(operands),
        out_specs=[pl.BlockSpec(memory_space=pltpu.VMEM)] * len(out),
        scratch_shapes=scratch,
        compiler_params=pltpu.CompilerParams(vmem_limit_bytes=32 * 1024 * 1024),
    )(*operands)


def on_each_component(atmosphere, ocean):
    comp = lax.axis_index("comp")
    pl.when(comp == 0)(atmosphere)
    pl.when(comp != 0)(ocean)


def fold_row(source, row, target, first):
    width = target.shape[1]
    for j in range(source.shape[1] // width):
        piece = source[row : row + 1, j * width : (j + 1) * width]
        target[first + j : first + j + 1, :] = piece.astype(F32)


def gather_cells(table, index):
    rows, width = index.shape
    tiles = [(r, h) for r in range(0, rows, 8) for h in range(0, width, 128)]
    pieces = [index[r : r + 8, h : h + 128] for r, h in tiles]
    high = [lax.shift_right_logical(p, 7) for p in pieces]
    low = [p & 127 for p in pieces]
    found = [jnp.zeros((8, 128), F32) for _ in tiles]
    for i in range(rows * width // 128):
        r, h = divmod(i * 128, width)
        line = jnp.broadcast_to(table[r : r + 1, h : h + 128], (8, 128))
        for k in range(len(tiles)):
            picked = jnp.take_along_axis(line, low[k], axis=1, mode="promise_in_bounds")
            found[k] = jnp.where(high[k] == i, picked, found[k])
    across = width // 128
    return jnp.concatenate(
        [jnp.concatenate(found[k : k + across], 1) for k in range(0, len(found), across)], 0
    )


def scatter_add(total, values, index):
    rows, width = index.shape
    place = lax.broadcasted_iota(I32, (64, width), 0)
    for r in range(rows):
        cell = index[r : r + 1, :]
        value = values[r : r + 1, :]
        head = value.astype(BF16).astype(F32)
        tail = value - head
        row_here = place == lax.shift_right_logical(cell, 6)
        column_here = place == (cell & 63)
        spread = jnp.concatenate(
            [
                jnp.where(row_here, head, 0.0).astype(BF16),
                jnp.where(row_here, tail, 0.0).astype(BF16),
            ],
            0,
        )
        chosen = jnp.where(column_here, 1.0, 0.0).astype(BF16)
        total = total + lax.dot_general(
            spread, chosen, CONTRACT_LANES, preferred_element_type=F32
        )
    return total


def as_rows(total):
    both = total[:64] + total[64:]
    cells = both.reshape(16, 4, 64)
    return jnp.concatenate([cells[:, q, :] for q in range(4)], 1)


def pack_kernel(
    cells, weights, slots, state, coeff, cells_sw, weights_sw, slots_sw, state_sw, coeff_sw, vertical,
    m0, m1, m2, m3, edge, n0, n1, n2, n3,
):
    forward = (m0, m1, m2, m3)
    static = (n0, n1, n2, n3)

    def fill(cells, weights, slots, state0, coeff0, state1, coeff1, rows, rows_back):
        for j in range(4):
            fold_row(cells, rows[j], forward[j], 0)
            fold_row(weights, rows[j], forward[j], 16)
            forward[j][32:48, :] = state0[0]
            forward[j][48:64, :] = coeff0[0]
            fold_row(slots, rows_back[j], static[j], 0)
            static[j][16:32, :] = coeff1[0]
            static[j][32:48, :] = vertical[...].astype(F32)
            static[j][48:64, :] = state1[0]
        edge[...] = state0[0, 0:8, :]

    on_each_component(
        lambda: fill(cells, weights, slots_sw, state, coeff, state_sw, coeff_sw, (3, 2, 1, 0), (5, 6, 7, 4)),
        lambda: fill(cells_sw, weights_sw, slots, state_sw, coeff_sw, state, coeff, (4, 5, 6, 7), (3, 2, 1, 0)),
    )


def local_kernel(cells, weights, slots, cells_sw, weights_sw, slots_sw, near_slots, far_cells, far_weights, inverse):
    def fill(cells, weights, slots, rows, rows_back):
        for j in range(4):
            fold_row(slots, rows[j], near_slots, 16 * j)
            fold_row(cells, rows_back[j], far_cells, 16 * j)
            fold_row(weights, rows_back[j], far_weights, 16 * j)

    def atmosphere():
        fill(cells, weights, slots_sw, (3, 2, 1, 0), (4, 5, 6, 7))
        total = jnp.zeros((128, 64), F32)
        for d in range(SPAN):
            for j in range(0, cells.shape[1], 256):
                total = scatter_add(total, weights[d : d + 1, j : j + 256], cells[d : d + 1, j : j + 256])
        inverse[...] = 1.0 / as_rows(total)

    def ocean():
        fill(cells_sw, weights_sw, slots, (4, 5, 6, 7), (0, 1, 2, 3))
        inverse[...] = jnp.ones_like(inverse)

    on_each_component(atmosphere, ocean)


def flux_kernel(own, r0, r1, r2, r3, edge, near_slots, partial):
    atmosphere = lax.axis_index("comp") == 0
    first = jnp.where(atmosphere, r0[...], own[...])
    blocks = (first, r1[...], r2[...], r3[...])
    air = [b[32:48] for b in blocks]
    top = [a[0:1] for a in air]
    bottom = [a[15:16] for a in air]
    beyond = edge[0:1]
    total = jnp.zeros((128, 64), F32)
    for j in range(4):
        if j == 0:
            before = jnp.where(atmosphere, own[47:48], bottom[1])
        elif j < 3:
            before = jnp.where(atmosphere, bottom[j - 1], bottom[j + 1])
        else:
            before = jnp.where(atmosphere, bottom[2], r0[47:48])
        if j == 0:
            after = jnp.where(atmosphere, top[1], beyond)
        elif j < 3:
            after = jnp.where(atmosphere, top[j + 1], top[j - 1])
        else:
            after = jnp.where(atmosphere, beyond, top[2])
        s = air[j]
        near = jnp.concatenate([before, s[:-1]], 0) + jnp.concatenate([s[1:], after], 0)
        near = near + pltpu.roll(s, 1, 1) + pltpu.roll(s, s.shape[1] - 1, 1)
        flux = blocks[j][48:64] * (s + 0.2 * (near - 4.0 * s))
        picked = gather_cells(flux, blocks[j][0:16].astype(I32))
        slot = near_slots[16 * j : 16 * j + 16].astype(I32)
        total = scatter_add(total, blocks[j][16:32] * picked, slot)
    partial[...] = as_rows(total)


def source_kernel(partial, partial_sw, own, rhs, back, low, high):
    total = partial[...] + partial_sw[...] + own[48:64]
    rhs[...] = total
    back[0:16, :] = total
    back[16:48, :] = own[16:48]
    for k, rows in enumerate((total, own[16:32], own[32:48])):
        low[8 * k : 8 * k + 8, :] = rows[8:16]
        high[8 * k : 8 * k + 8, :] = rows[0:8]


def trace_kernel(
    rhs_own, p0, p1, p2, p3, p4, p5, p6, n_own, n0, n1, n2, n3, far_cells, far_weights,
    send, keep, rhs, inv, code, eta, left, right,
):
    rows = rhs.shape[0]
    pad = 8
    inner = rows

    def place(parts):
        at = 0
        for r, c, v in parts:
            size = r.shape[0]
            rhs[at : at + size, :] = r[...]
            inv[at : at + size, :] = 1.0 / (c[...] + 3.0)
            code[at : at + size, :] = v[...]
            at += size

    lo = (p5.at[0:8], p5.at[8:16], p5.at[16:24])
    hi = (p6.at[0:8], p6.at[8:16], p6.at[16:24])
    back = (p4.at[0:16], p4.at[16:32], p4.at[32:48])
    own = (rhs_own, n_own.at[16:32], n_own.at[32:48])
    near = [(p, n.at[16:32], n.at[32:48]) for p, n in zip((p0, p1, p2, p3), (n0, n1, n2, n3))]
    on_each_component(
        lambda: place([lo, back, own, *near, hi]),
        lambda: place([lo, back, *near[::-1], own, hi]),
    )
    zero = jnp.zeros((inner + 2 * pad, rhs.shape[1]), F32)
    eta[...] = zero
    left[...] = zero
    right[...] = zero
    width = rhs.shape[1]

    def sweep(step, carry):
        for b in range(0, inner, 16):
            here = eta[pad + b : pad + b + 16, :]
            left[pad + b : pad + b + 16, :] = pltpu.roll(here, 1, 1)
            right[pad + b : pad + b + 16, :] = pltpu.roll(here, width - 1, 1)
        fresh = []
        for b in range(0, inner, 16):
            v = code[b : b + 16, :]
            down = v >= 3.0
            side = jnp.where(down, v - 3.0, v)
            third = []
            for ref in (left, eta, right):
                above = ref[pad + b - 1 : pad + b + 15, :]
                below = ref[pad + b + 1 : pad + b + 17, :]
                third.append(jnp.where(down, below, above))
            picked = jnp.where(side == 0.0, third[0], jnp.where(side == 1.0, third[1], third[2]))
            beside = left[pad + b : pad + b + 16, :] + right[pad + b : pad + b + 16, :] + picked
            fresh.append((rhs[b : b + 16, :] + beside) * inv[b : b + 16, :])
        for k, b in enumerate(range(0, inner, 16)):
            eta[pad + b : pad + b + 16, :] = fresh[k]
        return carry

    lax.fori_loop(0, SWEEPS, sweep, 0)

    atmosphere = lax.axis_index("comp") == 0
    surface = [jnp.where(atmosphere, n_own[48:64], n3[48:64])]
    slots = [jnp.where(atmosphere, n_own[0:16], n3[0:16])]
    for i, (up, down) in enumerate(((n0, n2), (n1, n1), (n2, n0))):
        surface.append(jnp.where(atmosphere, up[48:64], down[48:64]))
        slots.append(jnp.where(atmosphere, up[0:16], down[0:16]))
    total = jnp.zeros((128, 64), F32)
    for i in range(4):
        at = 24 + 16 * i
        sst = 1.25 * surface[i] + 0.5 * eta[pad + at : pad + at + 16, :] - 0.25 * rhs[at : at + 16, :]
        picked = gather_cells(sst, slots[i].astype(I32))
        cell = far_cells[16 * i : 16 * i + 16].astype(I32)
        total = scatter_add(total, far_weights[16 * i : 16 * i + 16] * picked, cell)
    part = as_rows(total)
    send[...] = jnp.where(atmosphere, eta[pad + 24 : pad + 40, :], part)
    keep[...] = jnp.where(atmosphere, part, 0.0)


def shards(state, coeff, vertical, send_cell, incoming_marine_slot, remap_weight):
    tiles = lax.axis_size("tile")
    block = state.shape[1:]

    def swap(x):
        return lax.ppermute(x, "comp", [(0, 1), (1, 0)])

    def move(x, atmosphere_from, ocean_from):
        pairs = [((t + atmosphere_from) % tiles, t) for t in range(tiles)]
        pairs += [(tiles + (t + ocean_from) % tiles, tiles + t) for t in range(tiles)]
        return lax.ppermute(x, GRID, pairs)

    cells_sw, weights_sw, slots_sw = swap(send_cell), swap(remap_weight), swap(incoming_marine_slot)
    state_sw, coeff_sw = swap(state), swap(coeff)
    lines, width = block
    packed = call(
        pack_kernel,
        [(4 * lines, width)] * 4 + [(8, width)] + [(4 * lines, width)] * 4,
        send_cell, remap_weight, incoming_marine_slot, state, coeff,
        cells_sw, weights_sw, slots_sw, state_sw, coeff_sw, vertical,
    )
    forward, edge, static = packed[:4], packed[4], packed[5:]
    edge_in = move(edge, 5, 1)
    forward_in = [move(forward[j], 1 + j, -j if j else -4) for j in (3, 2, 1, 0)][::-1]
    static_in = [move(static[j], 1 + j, -1 - j) for j in range(4)]
    near_slots, far_cells, far_weights, inverse = call(
        local_kernel,
        [(4 * lines, width)] * 3 + [block],
        send_cell, remap_weight, incoming_marine_slot, cells_sw, weights_sw, slots_sw,
    )
    (partial,) = call(flux_kernel, [block], forward[0], *forward_in, edge_in, near_slots)
    rhs, back, low, high = call(
        source_kernel, [block, (3 * lines, width), (24, width), (24, width)], partial, swap(partial), static[3]
    )
    rhs_in = [move(rhs, 1 + j, -1 - j) for j in range(4)]
    rhs_in += [move(back, -1, -5), move(low, -2, -6), move(high, 5, 1)]
    window = 6 * lines + 16
    send, keep = call(
        trace_kernel, [block, block], rhs, *rhs_in, static[3], *static_in, far_cells, far_weights,
        scratch=[pltpu.VMEM((window, width), F32)] * 3 + [pltpu.VMEM((window + 16, width), F32)] * 3,
    )
    return ((keep + swap(send)) * inverse)[None]


def solution(mesh):
    table = P(GRID, None)
    grid = P("comp", "tile", None)
    return jax.shard_map(
        shards,
        mesh=mesh,
        in_specs=(grid, grid, P("tile", None), table, table, table),
        out_specs=grid,
        check_vma=False,
    )
```

time: 1690 us -> 58.6 us (0.03); the launches traced: 1670 us -> 58.2 us
  local copies, waits for them, and re-layouts: 835 us -> 4.86 us
  other arithmetic: 659 us -> 0.61 us
  waiting for transfers between devices: 118 us -> 9.09 us
  starting transfers between devices: 54.1 us -> 32.2 us
    gather x46 -> x0, local copies, waits for them, and re-layouts: 823 us -> none  [the longest x40 461 us: sweep_once(): jnp.take(extended.reshape(-1), index)]
    scatter-add x3 -> x0, other arithmetic: 653 us -> none  [the longest x1 226 us: shards(): zeros_flat.at[incoming_marine_slot.reshape(-1)].add(incoming.reshape(-1))]
    ppermute x42 -> x23, waiting for transfers between devices: 101 us -> 9.09 us  [the longest x16 6.03 us: move(): return lax.ppermute(x, GRID, pairs)]
    ppermute x42 -> x23, starting transfers between devices: 48.4 us -> 32.2 us  [the longest x16 28 us: move(): return lax.ppermute(x, GRID, pairs)]
  transfers between devices with their start and end apart: 44 -> 23, of which waited for: 41 -> 6; matrix products, arithmetic and copies ran while one was open for 13% -> 0% of each run, Pallas kernels for 0% -> 8%
where the time goes in v1:
time: 58.6 us; the launch traced here: 58.2 us
  starting transfers between devices  32.2 us (55%)
  Pallas kernels  11.3 us (19%)
  waiting for transfers between devices  9.09 us (16%)
  local copies, waits for them, and re-layouts  4.86 us (8%)
  other arithmetic  0.61 us (1%)
    ppermute x16, starting transfers between devices, move(): return lax.ppermute(x, GRID, pairs)  28 us
    pallas_call x5, Pallas kernels, call(): pl.pallas_call(kernel, out_shape=out, in_specs=[pl.BlockSpec(memory_space...  11.3 us
    ppermute x16, waiting for transfers between devices, move(): return lax.ppermute(x, GRID, pairs)  6.03 us
    unnamed x12, local copies, waits for them, and re-layouts  4.86 us
    ppermute x7, starting transfers between devices, swap(): return lax.ppermute(x, 'comp', [(0, 1), (1, 0)])  4.21 us
    ppermute x7, waiting for transfers between devices, swap(): return lax.ppermute(x, 'comp', [(0, 1), (1, 0)])  3.07 us
  transfers between devices with their start and end apart: 23, of which 6 were waited for; matrix products, arithmetic and copies ran while one was open for 0% of the time, Pallas kernels for 8%

profile of v1, /device:TPU:0, one launch (start us, length us, event | category | flops | bytes accessed | tf_op | source)
XLA Modules:
  0.0 58.2 jit_solution(4778493881697934463)
XLA Ops:
  0.0 0.5 collective-permute-start
  0.5 0.1 collective-permute-start.2
  0.5 0.5 collective-permute-start.1
  1.0 0.1 collective-permute-start.3
  1.0 0.5 collective-permute-start.4
  1.5 0.9 %collective-permute-done.3.state_sw = f32[1,16,256]{2,1,0:T(8,128)S(1)} collective-permute-done((f32[1,16,256]{2,1,0:T(8,128)}, f32[1,16,256]{2,1,0:T(8,128)S(1)}, u32[]{:S(2)}, u32[]{:S(2)}) %collective-permute-start.3) | collective-permute-done | bytes 16416 | tf_op jit(solution)/shard_map/ppermute | solution.py:260
  2.4 0.2 collective-permute-done.4.coeff_sw
  2.5 0.0 collective-permute-done.cells_sw
  2.5 0.0 collective-permute-done.2.slots_sw
  2.5 0.0 collective-permute-done.1.weights_sw
  2.5 0.9 %copy-done = s32[8,4096]{1,0:T(8,128)S(1)} copy-done((s32[8,4096]{1,0:T(8,128)S(1)}, s32[8,4096]{1,0:T(8,128)}, u32[]{:S(2)}) %copy-start) | copy-done | bytes 131096
  3.4 0.9 %copy-done.1 = f32[8,4096]{1,0:T(8,128)S(1)} copy-done((f32[8,4096]{1,0:T(8,128)S(1)}, f32[8,4096]{1,0:T(8,128)}, u32[]{:S(2)}) %copy-start.1) | copy-done | bytes 131096
  4.4 0.9 %copy-done.2 = s32[8,4096]{1,0:T(8,128)S(1)} copy-done((s32[8,4096]{1,0:T(8,128)S(1)}, s32[8,4096]{1,0:T(8,128)}, u32[]{:S(2)}) %copy-start.2) | copy-done | bytes 131096
  5.3 0.7 %copy-done.3 = f32[1,16,256]{2,1,0:T(8,128)S(1)} copy-done((f32[1,16,256]{2,1,0:T(8,128)S(1)}, f32[1,16,256]{2,1,0:T(8,128)}, u32[]{:S(2)}) %copy-start.3) | copy-done | bytes 16408
  6.0 0.7 %copy-done.4 = f32[1,16,256]{2,1,0:T(8,128)S(1)} copy-done((f32[1,16,256]{2,1,0:T(8,128)S(1)}, f32[1,16,256]{2,1,0:T(8,128)}, u32[]{:S(2)}) %copy-start.4) | copy-done | bytes 16408
  6.7 0.7 %copy-done.5 = s32[16,256]{1,0:T(8,128)S(1)} copy-done((s32[16,256]{1,0:T(8,128)S(1)}, s32[16,256]{1,0:T(8,128)}, u32[]{:S(2)}) %copy-start.5) | copy-done | bytes 16408
  7.4 0.1 shard_map.64
  7.5 6.0 %collective-permute-start.6 = (f32[64,256]{1,0:T(8,128)S(1)}, f32[64,256]{1,0:T(8,128)S(1)}, u32[]{:S(2)}, u32[]{:S(2)}) collective-permute-start(f32[64,256]{1,0:T(8,128)S(1)} %get-tuple-element.25), channel_id=1, source_target_pairs={{2,0},{3,1},{4,2},{5,3},{6,4},{7,5},{8,6},{9,7},{10,8},{11,9},{12,... | collective-permute-start | bytes 196616 | tf_op jit(solution)/shard_map/ppermute | solution.py:265
  13.5 1.4 %collective-permute-start.7 = (f32[64,256]{1,0:T(8,128)S(1)}, f32[64,256]{1,0:T(8,128)S(1)}, u32[]{:S(2)}, u32[]{:S(2)}) collective-permute-start(f32[64,256]{1,0:T(8,128)S(1)} %get-tuple-element.26), channel_id=1, source_target_pairs={{3,0},{4,1},{5,2},{6,3},{7,4},{8,5},{9,6},{10,7},{11,8},{12,9},{13... | collective-permute-start | bytes 196616 | tf_op jit(solution)/shard_map/ppermute | solution.py:265
  14.9 0.4 collective-permute-start.8
  15.3 1.4 %collective-permute-start.5 = (f32[64,256]{1,0:T(8,128)S(1)}, f32[64,256]{1,0:T(8,128)S(1)}, u32[]{:S(2)}, u32[]{:S(2)}) collective-permute-start(f32[64,256]{1,0:T(8,128)S(1)} %get-tuple-element.24.own), channel_id=1, source_target_pairs={{1,0},{2,1},{3,2},{4,3},{5,4},{6,5},{7,6},{8,7},{9,8},{10,9},{11,1... | collective-permute-start | bytes 196616 | tf_op jit(solution)/shard_map/ppermute | solution.py:265
  16.7 4.5 %collective-permute-done.9.edge = f32[8,256]{1,0:T(8,128)S(1)} collective-permute-done((f32[8,256]{1,0:T(8,128)S(1)}, f32[8,256]{1,0:T(8,128)S(1)}, u32[]{:S(2)}, u32[]{:S(2)}) %collective-permute-start.9) | collective-permute-done | bytes 8224 | tf_op jit(solution)/shard_map/ppermute | solution.py:265
  21.3 3.6 %collective-permute-start.18 = (f32[64,256]{1,0:T(8,128)S(1)}, f32[64,256]{1,0:T(8,128)S(1)}, u32[]{:S(2)}, u32[]{:S(2)}) collective-permute-start(f32[64,256]{1,0:T(8,128)S(1)} %get-tuple-element.35), channel_id=1, source_target_pairs={{1,0},{2,1},{3,2},{4,3},{5,4},{6,5},{7,6},{8,7},{9,8},{10,9},{11,1... | collective-permute-start | bytes 196616 | tf_op jit(solution)/shard_map/ppermute | solution.py:265
  24.9 0.0 collective-permute-done.6.r1
  24.9 1.1 %collective-permute-start.19 = (f32[64,256]{1,0:T(8,128)S(1)}, f32[64,256]{1,0:T(8,128)S(1)}, u32[]{:S(2)}, u32[]{:S(2)}) collective-permute-start(f32[64,256]{1,0:T(8,128)S(1)} %get-tuple-element.36), channel_id=1, source_target_pairs={{2,0},{3,1},{4,2},{5,3},{6,4},{7,5},{8,6},{9,7},{10,8},{11,9},{12,... | collective-permute-start | bytes 196616 | tf_op jit(solution)/shard_map/ppermute | solution.py:265
  25.9 0.0 collective-permute-done.7.r2
  25.9 2.0 %collective-permute-start.21 = (f32[64,256]{1,0:T(8,128)S(1)}, f32[64,256]{1,0:T(8,128)S(1)}, u32[]{:S(2)}, u32[]{:S(2)}) collective-permute-start(f32[64,256]{1,0:T(8,128)S(1)} %get-tuple-element.30.own.n_own), channel_id=1, source_target_pairs={{4,0},{5,1},{6,2},{7,3},{8,4},{9,5},{10,6},{11,7},{12,8},{13,9},{1... | collective-permute-start | bytes 196616 | tf_op jit(solution)/shard_map/ppermute | solution.py:265
  27.9 2.5 %shard_map.65 = (f32[64,256]{1,0:T(8,128)S(1)}, f32[64,256]{1,0:T(8,128)S(1)}, f32[64,256]{1,0:T(8,128)S(1)}, f32[16,256]{1,0:T(8,128)S(1)}) custom-call(s32[8,4096]{1,0:T(8,128)S(1)} %copy-done, f32[8,4096]{1,0:T(8,128)S(1)} %copy-done.1, s32[8,4096]{1,0:T(8,128)S(1)} %copy-done.2, s32[8,4096]{1,0:T(8,128)S(1)} %collective-permute-done.cells_sw, ...), custom_call_target="tpu_custom_call" | custom-call | tf_op jit(solution)/shard_map/pallas_call | solution.py:20
  30.5 0.0 collective-permute-done.5.r0
  30.5 2.3 %shard_map.66.partial = f32[16,256]{1,0:T(8,128)S(1)} custom-call(f32[64,256]{1,0:T(8,128)S(1)} %get-tuple-element.24.own, f32[64,256]{1,0:T(8,128)S(1)} %collective-permute-done.5.r0, f32[64,256]{1,0:T(8,128)S(1)} %collective-permute-done.6.r1, f32[64,256]{1,0:T(8,128)S(1)} %collective-permute-done.7.r2, f32[64,256]{1,0:T(8,128)S(1)} %collective-permute-done.8.r3, ...), custom_call_target="tpu_custom_call" | custom-call | tf_op jit(solution)/shard_map/pallas_call | solution.py:20
  32.8 0.0 collective-permute-start.10
  32.8 1.2 %collective-permute-done.10.partial_sw = f32[16,256]{1,0:T(8,128)S(1)} collective-permute-done((f32[16,256]{1,0:T(8,128)S(1)}, f32[16,256]{1,0:T(8,128)S(1)}, u32[]{:S(2)}, u32[]{:S(2)}) %collective-permute-start.10) | collective-permute-done | bytes 16416 | tf_op jit(solution)/shard_map/ppermute | solution.py:260
  34.0 2.7 %collective-permute-start.15 = (f32[48,256]{1,0:T(8,128)S(1)}, f32[48,256]{1,0:T(8,128)S(1)}, u32[]{:S(2)}, u32[]{:S(2)}) collective-permute-start(f32[48,256]{1,0:T(8,128)S(1)} %get-tuple-element.32), channel_id=1, source_target_pairs={{15,0},{0,1},{1,2},{2,3},{3,4},{4,5},{5,6},{6,7},{7,8},{8,9},{9,10... | collective-permute-start | bytes 147464 | tf_op jit(solution)/shard_map/ppermute | solution.py:265
  36.7 0.8 %collective-permute-start.14 = (f32[16,256]{1,0:T(8,128)S(1)}, f32[16,256]{1,0:T(8,128)S(1)}, u32[]{:S(2)}, u32[]{:S(2)}) collective-permute-start(f32[16,256]{1,0:T(8,128)S(1)} %get-tuple-element.31.rhs_own), channel_id=1, source_target_pairs={{4,0},{5,1},{6,2},{7,3},{8,4},{9,5},{10,6},{11,7},{12,8},{13,9},{1... | collective-permute-start | bytes 49160 | tf_op jit(solution)/shard_map/ppermute | solution.py:265
  37.5 0.0 collective-permute-done.19.n1
  37.5 0.8 %collective-permute-start.13 = (f32[16,256]{1,0:T(8,128)S(1)}, f32[16,256]{1,0:T(8,128)S(1)}, u32[]{:S(2)}, u32[]{:S(2)}) collective-permute-start(f32[16,256]{1,0:T(8,128)S(1)} %get-tuple-element.31.rhs_own), channel_id=1, source_target_pairs={{3,0},{4,1},{5,2},{6,3},{7,4},{8,5},{9,6},{10,7},{11,8},{12,9},{13... | collective-permute-start | bytes 49160 | tf_op jit(solution)/shard_map/ppermute | solution.py:265
  38.3 0.0 collective-permute-done.20.n2
  38.3 1.9 %collective-permute-start.16 = (f32[24,256]{1,0:T(8,128)S(1)}, f32[24,256]{1,0:T(8,128)S(1)}, u32[]{:S(2)}, u32[]{:S(2)}) collective-permute-start(f32[24,256]{1,0:T(8,128)S(1)} %get-tuple-element.33), channel_id=1, source_target_pairs={{14,0},{15,1},{0,2},{1,3},{2,4},{3,5},{4,6},{5,7},{6,8},{7,9},{8,1... | collective-permute-start | bytes 73736 | tf_op jit(solution)/shard_map/ppermute | solution.py:265
  40.3 0.0 collective-permute-done.21.n3
  40.3 2.0 %collective-permute-start.17 = (f32[24,256]{1,0:T(8,128)S(1)}, f32[24,256]{1,0:T(8,128)S(1)}, u32[]{:S(2)}, u32[]{:S(2)}) collective-permute-start(f32[24,256]{1,0:T(8,128)S(1)} %get-tuple-element.34), channel_id=1, source_target_pairs={{5,0},{6,1},{7,2},{8,3},{9,4},{10,5},{11,6},{12,7},{13,8},{14,9},{... | collective-permute-start | bytes 73736 | tf_op jit(solution)/shard_map/ppermute | solution.py:265
  42.3 0.0 collective-permute-done.14.p3
  42.3 1.4 %collective-permute-start.12 = (f32[16,256]{1,0:T(8,128)S(1)}, f32[16,256]{1,0:T(8,128)S(1)}, u32[]{:S(2)}, u32[]{:S(2)}) collective-permute-start(f32[16,256]{1,0:T(8,128)S(1)} %get-tuple-element.31.rhs_own), channel_id=1, source_target_pairs={{2,0},{3,1},{4,2},{5,3},{6,4},{7,5},{8,6},{9,7},{10,8},{11,9},{12,... | collective-permute-start | bytes 49160 | tf_op jit(solution)/shard_map/ppermute | solution.py:265
  43.7 2.4 %collective-permute-start.11 = (f32[16,256]{1,0:T(8,128)S(1)}, f32[16,256]{1,0:T(8,128)S(1)}, u32[]{:S(2)}, u32[]{:S(2)}) collective-permute-start(f32[16,256]{1,0:T(8,128)S(1)} %get-tuple-element.31.rhs_own), channel_id=1, source_target_pairs={{1,0},{2,1},{3,2},{4,3},{5,4},{6,5},{7,6},{8,7},{9,8},{10,9},{11,1... | collective-permute-start | bytes 49160 | tf_op jit(solution)/shard_map/ppermute | solution.py:265
  46.1 1.4 %collective-permute-done.11.p0 = f32[16,256]{1,0:T(8,128)S(1)} collective-permute-done((f32[16,256]{1,0:T(8,128)S(1)}, f32[16,256]{1,0:T(8,128)S(1)}, u32[]{:S(2)}, u32[]{:S(2)}) %collective-permute-start.11) | collective-permute-done | bytes 16416 | tf_op jit(solution)/shard_map/ppermute | solution.py:265
  47.6 6.4 %shard_map.68 = (f32[16,256]{1,0:T(8,128)S(1)}, f32[16,256]{1,0:T(8,128)S(1)}) custom-call(f32[16,256]{1,0:T(8,128)S(1)} %get-tuple-element.31.rhs_own, f32[16,256]{1,0:T(8,128)S(1)} %collective-permute-done.11.p0, f32[16,256]{1,0:T(8,128)S(1)} %collective-permute-done.12.p1, f32[16,256]{1,0:T(8,128)S(1)} %collective-permute-done.13.p2, ...), custom_call_target="tpu_custom_call" | custom-call | tf_op jit(solution)/shard_map/pallas_call | solution.py:20
  54.0 2.7 %collective-permute-start.22 = (f32[16,256]{1,0:T(8,128)S(1)}, f32[16,256]{1,0:T(8,128)S(1)}, u32[]{:S(2)}, u32[]{:S(2)}) collective-permute-start(f32[16,256]{1,0:T(8,128)S(1)} %get-tuple-element.41), channel_id=1, source_target_pairs={{0,16},{16,0},{1,17},{17,1},{2,18},{18,2},{3,19},{19,3},{4,20},{20... | collective-permute-start | bytes 49160 | tf_op jit(solution)/shard_map/ppermute | solution.py:260
  56.7 0.8 %collective-permute-done.22 = f32[16,256]{1,0:T(8,128)S(1)} collective-permute-done((f32[16,256]{1,0:T(8,128)S(1)}, f32[16,256]{1,0:T(8,128)S(1)}, u32[]{:S(2)}, u32[]{:S(2)}) %collective-permute-start.22) | collective-permute-done | bytes 16416 | tf_op jit(solution)/shard_map/ppermute | solution.py:260
  57.6 0.6 %multiply_bitcast_fusion = f32[1,16,256]{2,1,0:T(8,128)} fusion(f32[16,256]{1,0:T(8,128)S(1)} %get-tuple-element.42, f32[16,256]{1,0:T(8,128)S(1)} %get-tuple-element.40, f32[16,256]{1,0:T(8,128)S(1)} %collective-permute-done.22), kind=kLoop, calls=%fused_computation | loop fusion | flops 8192 | bytes 65536 | tf_op jit(solution)/shard_map/broadcast_in_dim | solution.py:296
  (16 shorter events, 0.0 us)
Async XLA Ops:
  0.0 2.5 %collective-permute-start = (s32[8,4096]{1,0:T(8,128)}, s32[8,4096]{1,0:T(8,128)S(1)}, u32[]{:S(2)}, u32[]{:S(2)}) collective-permute-start(s32[8,4096]{1,0:T(8,128)} %cells.3), channel_id=1, source_target_pairs={{0,16},{16,0},{1,17},{17,1},{2,18},{18,2},{3,19},{19,3},{4,20},{20... | collective-permute-start | bytes 393224 | tf_op jit(solution)/shard_map/ppermute | solution.py:260
  0.5 2.1 %collective-permute-start.2 = (s32[8,4096]{1,0:T(8,128)}, s32[8,4096]{1,0:T(8,128)S(1)}, u32[]{:S(2)}, u32[]{:S(2)}) collective-permute-start(s32[8,4096]{1,0:T(8,128)} %slots.3), channel_id=1, source_target_pairs={{0,16},{16,0},{1,17},{17,1},{2,18},{18,2},{3,19},{19,3},{4,20},{20... | collective-permute-start | bytes 393224 | tf_op jit(solution)/shard_map/ppermute | solution.py:260
  0.5 2.0 %collective-permute-start.1 = (f32[8,4096]{1,0:T(8,128)}, f32[8,4096]{1,0:T(8,128)S(1)}, u32[]{:S(2)}, u32[]{:S(2)}) collective-permute-start(f32[8,4096]{1,0:T(8,128)} %weights.3), channel_id=1, source_target_pairs={{0,16},{16,0},{1,17},{17,1},{2,18},{18,2},{3,19},{19,3},{4,20},{20... | collective-permute-start | bytes 393224 | tf_op jit(solution)/shard_map/ppermute | solution.py:260
  1.0 1.4 %collective-permute-start.3 = (f32[1,16,256]{2,1,0:T(8,128)}, f32[1,16,256]{2,1,0:T(8,128)S(1)}, u32[]{:S(2)}, u32[]{:S(2)}) collective-permute-start(f32[1,16,256]{2,1,0:T(8,128)} %state.1), channel_id=1, source_target_pairs={{0,16},{16,0},{1,17},{17,1},{2,18},{18,2},{3,19},{19,3},{4,20},{20... | collective-permute-start | bytes 49160 | tf_op jit(solution)/shard_map/ppermute | solution.py:260
  1.0 1.5 %collective-permute-start.4 = (f32[1,16,256]{2,1,0:T(8,128)}, f32[1,16,256]{2,1,0:T(8,128)S(1)}, u32[]{:S(2)}, u32[]{:S(2)}) collective-permute-start(f32[1,16,256]{2,1,0:T(8,128)} %coeff.1), channel_id=1, source_target_pairs={{0,16},{16,0},{1,17},{17,1},{2,18},{18,2},{3,19},{19,3},{4,20},{20... | collective-permute-start | bytes 49160 | tf_op jit(solution)/shard_map/ppermute | solution.py:260
  2.5 0.9 %copy-start = (s32[8,4096]{1,0:T(8,128)S(1)}, s32[8,4096]{1,0:T(8,128)}, u32[]{:S(2)}) copy-start(s32[8,4096]{1,0:T(8,128)} %cells.3) | copy-start | bytes 393220
  3.4 0.9 %copy-start.1 = (f32[8,4096]{1,0:T(8,128)S(1)}, f32[8,4096]{1,0:T(8,128)}, u32[]{:S(2)}) copy-start(f32[8,4096]{1,0:T(8,128)} %weights.3) | copy-start | bytes 393220
  4.3 0.9 %copy-start.2 = (s32[8,4096]{1,0:T(8,128)S(1)}, s32[8,4096]{1,0:T(8,128)}, u32[]{:S(2)}) copy-start(s32[8,4096]{1,0:T(8,128)} %slots.3) | copy-start | bytes 393220
  5.3 0.7 %copy-start.3 = (f32[1,16,256]{2,1,0:T(8,128)S(1)}, f32[1,16,256]{2,1,0:T(8,128)}, u32[]{:S(2)}) copy-start(f32[1,16,256]{2,1,0:T(8,128)} %state.1) | copy-start | bytes 49156
  6.0 0.7 %copy-start.4 = (f32[1,16,256]{2,1,0:T(8,128)S(1)}, f32[1,16,256]{2,1,0:T(8,128)}, u32[]{:S(2)}) copy-start(f32[1,16,256]{2,1,0:T(8,128)} %coeff.1) | copy-start | bytes 49156
  6.7 0.7 %copy-start.5 = (s32[16,256]{1,0:T(8,128)S(1)}, s32[16,256]{1,0:T(8,128)}, u32[]{:S(2)}) copy-start(s32[16,256]{1,0:T(8,128)} %vertical.1) | copy-start | bytes 49156
  7.5 17.3 %collective-permute-start.6 = (f32[64,256]{1,0:T(8,128)S(1)}, f32[64,256]{1,0:T(8,128)S(1)}, u32[]{:S(2)}, u32[]{:S(2)}) collective-permute-start(f32[64,256]{1,0:T(8,128)S(1)} %get-tuple-element.25), channel_id=1, source_target_pairs={{2,0},{3,1},{4,2},{5,3},{6,4},{7,5},{8,6},{9,7},{10,8},{11,9},{12,... | collective-permute-start | bytes 196616 | tf_op jit(solution)/shard_map/ppermute | solution.py:265
  13.5 12.5 %collective-permute-start.7 = (f32[64,256]{1,0:T(8,128)S(1)}, f32[64,256]{1,0:T(8,128)S(1)}, u32[]{:S(2)}, u32[]{:S(2)}) collective-permute-start(f32[64,256]{1,0:T(8,128)S(1)} %get-tuple-element.26), channel_id=1, source_target_pairs={{3,0},{4,1},{5,2},{6,3},{7,4},{8,5},{9,6},{10,7},{11,8},{12,9},{13... | collective-permute-start | bytes 196616 | tf_op jit(solution)/shard_map/ppermute | solution.py:265
  14.9 11.1 %collective-permute-start.8 = (f32[64,256]{1,0:T(8,128)S(1)}, f32[64,256]{1,0:T(8,128)S(1)}, u32[]{:S(2)}, u32[]{:S(2)}) collective-permute-start(f32[64,256]{1,0:T(8,128)S(1)} %get-tuple-element.27), channel_id=1, source_target_pairs={{4,0},{5,1},{6,2},{7,3},{8,4},{9,5},{10,6},{11,7},{12,8},{13,9},{1... | collective-permute-start | bytes 196616 | tf_op jit(solution)/shard_map/ppermute | solution.py:265
  15.3 15.2 %collective-permute-start.5 = (f32[64,256]{1,0:T(8,128)S(1)}, f32[64,256]{1,0:T(8,128)S(1)}, u32[]{:S(2)}, u32[]{:S(2)}) collective-permute-start(f32[64,256]{1,0:T(8,128)S(1)} %get-tuple-element.24.own), channel_id=1, source_target_pairs={{1,0},{2,1},{3,2},{4,3},{5,4},{6,5},{7,6},{8,7},{9,8},{10,9},{11,1... | collective-permute-start | bytes 196616 | tf_op jit(solution)/shard_map/ppermute | solution.py:265
  16.7 4.5 %collective-permute-start.9 = (f32[8,256]{1,0:T(8,128)S(1)}, f32[8,256]{1,0:T(8,128)S(1)}, u32[]{:S(2)}, u32[]{:S(2)}) collective-permute-start(f32[8,256]{1,0:T(8,128)S(1)} %get-tuple-element.28), channel_id=1, source_target_pairs={{5,0},{6,1},{7,2},{8,3},{9,4},{10,5},{11,6},{12,7},{13,8},{14,9},{... | collective-permute-start | bytes 24584 | tf_op jit(solution)/shard_map/ppermute | solution.py:265
  21.3 15.4 %collective-permute-start.18 = (f32[64,256]{1,0:T(8,128)S(1)}, f32[64,256]{1,0:T(8,128)S(1)}, u32[]{:S(2)}, u32[]{:S(2)}) collective-permute-start(f32[64,256]{1,0:T(8,128)S(1)} %get-tuple-element.35), channel_id=1, source_target_pairs={{1,0},{2,1},{3,2},{4,3},{5,4},{6,5},{7,6},{8,7},{9,8},{10,9},{11,1... | collective-permute-start | bytes 196616 | tf_op jit(solution)/shard_map/ppermute | solution.py:265
  24.9 12.6 %collective-permute-start.19 = (f32[64,256]{1,0:T(8,128)S(1)}, f32[64,256]{1,0:T(8,128)S(1)}, u32[]{:S(2)}, u32[]{:S(2)}) collective-permute-start(f32[64,256]{1,0:T(8,128)S(1)} %get-tuple-element.36), channel_id=1, source_target_pairs={{2,0},{3,1},{4,2},{5,3},{6,4},{7,5},{8,6},{9,7},{10,8},{11,9},{12,... | collective-permute-start | bytes 196616 | tf_op jit(solution)/shard_map/ppermute | solution.py:265
  25.9 12.4 %collective-permute-start.20 = (f32[64,256]{1,0:T(8,128)S(1)}, f32[64,256]{1,0:T(8,128)S(1)}, u32[]{:S(2)}, u32[]{:S(2)}) collective-permute-start(f32[64,256]{1,0:T(8,128)S(1)} %get-tuple-element.37), channel_id=1, source_target_pairs={{3,0},{4,1},{5,2},{6,3},{7,4},{8,5},{9,6},{10,7},{11,8},{12,9},{13... | collective-permute-start | bytes 196616 | tf_op jit(solution)/shard_map/ppermute | solution.py:265
  25.9 14.3 %collective-permute-start.21 = (f32[64,256]{1,0:T(8,128)S(1)}, f32[64,256]{1,0:T(8,128)S(1)}, u32[]{:S(2)}, u32[]{:S(2)}) collective-permute-start(f32[64,256]{1,0:T(8,128)S(1)} %get-tuple-element.30.own.n_own), channel_id=1, source_target_pairs={{4,0},{5,1},{6,2},{7,3},{8,4},{9,5},{10,6},{11,7},{12,8},{13,9},{1... | collective-permute-start | bytes 196616 | tf_op jit(solution)/shard_map/ppermute | solution.py:265
  32.8 1.2 %collective-permute-start.10 = (f32[16,256]{1,0:T(8,128)S(1)}, f32[16,256]{1,0:T(8,128)S(1)}, u32[]{:S(2)}, u32[]{:S(2)}) collective-permute-start(f32[16,256]{1,0:T(8,128)S(1)} %shard_map.66.partial), channel_id=1, source_target_pairs={{0,16},{16,0},{1,17},{17,1},{2,18},{18,2},{3,19},{19,3},{4,20},{20... | collective-permute-start | bytes 49160 | tf_op jit(solution)/shard_map/ppermute | solution.py:260
  34.0 13.6 %collective-permute-start.15 = (f32[48,256]{1,0:T(8,128)S(1)}, f32[48,256]{1,0:T(8,128)S(1)}, u32[]{:S(2)}, u32[]{:S(2)}) collective-permute-start(f32[48,256]{1,0:T(8,128)S(1)} %get-tuple-element.32), channel_id=1, source_target_pairs={{15,0},{0,1},{1,2},{2,3},{3,4},{4,5},{5,6},{6,7},{7,8},{8,9},{9,10... | collective-permute-start | bytes 147464 | tf_op jit(solution)/shard_map/ppermute | solution.py:265
  36.7 5.6 %collective-permute-start.14 = (f32[16,256]{1,0:T(8,128)S(1)}, f32[16,256]{1,0:T(8,128)S(1)}, u32[]{:S(2)}, u32[]{:S(2)}) collective-permute-start(f32[16,256]{1,0:T(8,128)S(1)} %get-tuple-element.31.rhs_own), channel_id=1, source_target_pairs={{4,0},{5,1},{6,2},{7,3},{8,4},{9,5},{10,6},{11,7},{12,8},{13,9},{1... | collective-permute-start | bytes 49160 | tf_op jit(solution)/shard_map/ppermute | solution.py:265
  37.5 6.2 %collective-permute-start.13 = (f32[16,256]{1,0:T(8,128)S(1)}, f32[16,256]{1,0:T(8,128)S(1)}, u32[]{:S(2)}, u32[]{:S(2)}) collective-permute-start(f32[16,256]{1,0:T(8,128)S(1)} %get-tuple-element.31.rhs_own), channel_id=1, source_target_pairs={{3,0},{4,1},{5,2},{6,3},{7,4},{8,5},{9,6},{10,7},{11,8},{12,9},{13... | collective-permute-start | bytes 49160 | tf_op jit(solution)/shard_map/ppermute | solution.py:265
  38.3 9.2 %collective-permute-start.16 = (f32[24,256]{1,0:T(8,128)S(1)}, f32[24,256]{1,0:T(8,128)S(1)}, u32[]{:S(2)}, u32[]{:S(2)}) collective-permute-start(f32[24,256]{1,0:T(8,128)S(1)} %get-tuple-element.33), channel_id=1, source_target_pairs={{14,0},{15,1},{0,2},{1,3},{2,4},{3,5},{4,6},{5,7},{6,8},{7,9},{8,1... | collective-permute-start | bytes 73736 | tf_op jit(solution)/shard_map/ppermute | solution.py:265
  40.3 7.3 %collective-permute-start.17 = (f32[24,256]{1,0:T(8,128)S(1)}, f32[24,256]{1,0:T(8,128)S(1)}, u32[]{:S(2)}, u32[]{:S(2)}) collective-permute-start(f32[24,256]{1,0:T(8,128)S(1)} %get-tuple-element.34), channel_id=1, source_target_pairs={{5,0},{6,1},{7,2},{8,3},{9,4},{10,5},{11,6},{12,7},{13,8},{14,9},{... | collective-permute-start | bytes 73736 | tf_op jit(solution)/shard_map/ppermute | solution.py:265
  42.3 3.9 %collective-permute-start.12 = (f32[16,256]{1,0:T(8,128)S(1)}, f32[16,256]{1,0:T(8,128)S(1)}, u32[]{:S(2)}, u32[]{:S(2)}) collective-permute-start(f32[16,256]{1,0:T(8,128)S(1)} %get-tuple-element.31.rhs_own), channel_id=1, source_target_pairs={{2,0},{3,1},{4,2},{5,3},{6,4},{7,5},{8,6},{9,7},{10,8},{11,9},{12,... | collective-permute-start | bytes 49160 | tf_op jit(solution)/shard_map/ppermute | solution.py:265
  43.7 3.9 %collective-permute-start.11 = (f32[16,256]{1,0:T(8,128)S(1)}, f32[16,256]{1,0:T(8,128)S(1)}, u32[]{:S(2)}, u32[]{:S(2)}) collective-permute-start(f32[16,256]{1,0:T(8,128)S(1)} %get-tuple-element.31.rhs_own), channel_id=1, source_target_pairs={{1,0},{2,1},{3,2},{4,3},{5,4},{6,5},{7,6},{8,7},{9,8},{10,9},{11,1... | collective-permute-start | bytes 49160 | tf_op jit(solution)/shard_map/ppermute | solution.py:265
  54.0 3.6 %collective-permute-start.22 = (f32[16,256]{1,0:T(8,128)S(1)}, f32[16,256]{1,0:T(8,128)S(1)}, u32[]{:S(2)}, u32[]{:S(2)}) collective-permute-start(f32[16,256]{1,0:T(8,128)S(1)} %get-tuple-element.41), channel_id=1, source_target_pairs={{0,16},{16,0},{1,17},{17,1},{2,18},{18,2},{3,19},{19,3},{4,20},{20... | collective-permute-start | bytes 49160 | tf_op jit(solution)/shard_map/ppermute | solution.py:260

commit v2 on v1

v2 whole, which is shorter than its diff:
```python
import jax
import jax.experimental.pallas as pl
import jax.experimental.pallas.tpu as pltpu
import jax.numpy as jnp
from jax import lax
from jax.sharding import PartitionSpec as P

SPAN = 8
SWEEPS = 20
MIDDLE = SPAN // 2
F32 = jnp.float32
BF16 = jnp.bfloat16
I32 = jnp.int32
CONTRACT_LANES = (((1,), (1,)), ((), ()))
GRID = ("comp", "tile")


def call(kernel, shapes, *operands, scratch=(), where=pltpu.VMEM, flops=None):
    out = [jax.ShapeDtypeStruct(shape, F32) for shape in shapes]
    cost = None
    if flops is not None:
        cost = pl.CostEstimate(flops=flops, bytes_accessed=0, transcendentals=0)
    return pl.pallas_call(
        kernel,
        out_shape=out,
        in_specs=[pl.BlockSpec(memory_space=where)] * len(operands),
        out_specs=[pl.BlockSpec(memory_space=pltpu.VMEM)] * len(out),
        scratch_shapes=scratch,
        cost_estimate=cost,
        compiler_params=pltpu.CompilerParams(vmem_limit_bytes=32 * 1024 * 1024),
    )(*operands)


def on_each_component(atmosphere, ocean):
    comp = lax.axis_index("comp")
    pl.when(comp == 0)(atmosphere)
    pl.when(comp != 0)(ocean)


def fold(source, target, first):
    width = target.shape[1]
    lines = source.shape[1] // width
    for row in range(SPAN):
        for j in range(lines):
            piece = source[row : row + 1, j * width : (j + 1) * width]
            at = first + row * lines + j
            target[at : at + 1, :] = piece.astype(F32)


def gather_cells(table, index):
    rows, width = index.shape
    tiles = [(r, h) for r in range(0, rows, 8) for h in range(0, width, 128)]
    pieces = [index[r : r + 8, h : h + 128] for r, h in tiles]
    high = [lax.shift_right_logical(p, 7) for p in pieces]
    low = [p & 127 for p in pieces]
    found = [jnp.zeros((8, 128), F32) for _ in tiles]
    for i in range(rows * width // 128):
        r, h = divmod(i * 128, width)
        line = jnp.broadcast_to(table[r : r + 1, h : h + 128], (8, 128))
        for k in range(len(tiles)):
            picked = jnp.take_along_axis(line, low[k], axis=1, mode="promise_in_bounds")
            found[k] = jnp.where(high[k] == i, picked, found[k])
    across = width // 128
    return jnp.concatenate(
        [jnp.concatenate(found[k : k + across], 1) for k in range(0, len(found), across)], 0
    )


def scatter_add(total, values, index):
    rows, width = index.shape
    place = lax.broadcasted_iota(I32, (64, width), 0)
    for r in range(rows):
        cell = index[r : r + 1, :]
        value = values[r : r + 1, :]
        head = value.astype(BF16).astype(F32)
        tail = value - head
        row_here = place == lax.shift_right_logical(cell, 6)
        column_here = place == (cell & 63)
        spread = jnp.concatenate(
            [
                jnp.where(row_here, head, 0.0).astype(BF16),
                jnp.where(row_here, tail, 0.0).astype(BF16),
            ],
            0,
        )
        chosen = jnp.where(column_here, 1.0, 0.0).astype(BF16)
        total = total + lax.dot_general(
            spread, chosen, CONTRACT_LANES, preferred_element_type=F32
        )
    return total


def as_rows(total):
    both = total[:64] + total[64:]
    cells = both.reshape(16, 4, 64)
    return jnp.concatenate([cells[:, q, :] for q in range(4)], 1)


def pack_kernel(cells, weights, slots, state, coeff, vertical, pack, code, ints, reals, codes, sems):
    copies = [
        pltpu.make_async_copy(state.at[0], pack.at[256:272], sems.at[0]),
        pltpu.make_async_copy(coeff.at[0], pack.at[272:288], sems.at[1]),
        pltpu.make_async_copy(vertical, codes, sems.at[2]),
    ]
    for copy in copies:
        copy.start()

    def atmosphere():
        first = pltpu.make_async_copy(cells, ints, sems.at[3])
        second = pltpu.make_async_copy(weights, reals, sems.at[4])
        first.start()
        second.start()
        first.wait()
        fold(ints, pack, 0)
        second.wait()
        fold(reals, pack, 128)

    def ocean():
        first = pltpu.make_async_copy(slots, ints, sems.at[3])
        first.start()
        pack[128:256, :] = jnp.zeros((128, pack.shape[1]), F32)
        first.wait()
        fold(ints, pack, 0)

    on_each_component(atmosphere, ocean)
    for copy in copies:
        copy.wait()
    code[...] = codes[...].astype(F32)


def block_of(ref, k):
    return ref[16 * k : 16 * k + 16, :]


def message_kernel(pack, other, code, m1, m2, m3, m4, edge):
    def fill(air, sea, rows, rows_back):
        for j, m in enumerate((m1, m2, m3)):
            m[0:16, :] = block_of(air, rows[j])
            m[16:32, :] = block_of(air, 8 + rows[j])
            m[32:64, :] = air[256:288, :]
            m[64:80, :] = block_of(sea, rows_back[j])
            m[80:96, :] = sea[272:288, :]
            m[96:112, :] = code[...]
            m[112:128, :] = sea[256:272, :]
        m4[32:64, :] = air[256:288, :]
        m4[64:80, :] = sea[272:288, :]
        m4[80:96, :] = code[...]
        edge[...] = air[256:264, :]

    def atmosphere():
        fill(pack, other, (3, 2, 1), (5, 6, 7))
        m4[0:16, :] = block_of(pack, 0)
        m4[16:32, :] = block_of(pack, 8)

    def ocean():
        fill(other, pack, (5, 6, 7), (3, 2, 1))
        m4[0:16, :] = block_of(pack, 0)
        m4[16:32, :] = pack[256:272, :]

    on_each_component(atmosphere, ocean)


def share_kernel(pack, inverse):
    def atmosphere():
        total = jnp.zeros((128, 64), F32)
        for d in range(SPAN):
            total = scatter_add(total, block_of(pack, 8 + d), block_of(pack, d).astype(I32))
        inverse[...] = 1.0 / as_rows(total)

    def ocean():
        inverse[...] = jnp.ones_like(inverse)

    on_each_component(atmosphere, ocean)


def flux_kernel(edge, m1, m3, m2, m4, pack, other, partial):
    atmosphere = lax.axis_index("comp") == 0

    def part(k):
        rows = slice(16 * k, 16 * k + 16)
        local = block_of(other, (4, 12, 16, 17)[k])
        return [
            jnp.where(atmosphere, a[rows, :], b)
            for a, b in ((m1, local), (m2, m1[rows, :]), (m3, m2[rows, :]), (m4, m3[rows, :]))
        ]

    cells, weights, air, coeff = (part(k) for k in range(4))
    top = [a[0:1] for a in air]
    bottom = [a[15:16] for a in air]
    beyond = edge[0:1]
    total = jnp.zeros((128, 64), F32)
    for j in range(4):
        before = jnp.where(
            atmosphere,
            bottom[j - 1] if j else pack[271:272, :],
            bottom[j + 1] if j < 3 else m4[47:48, :],
        )
        after = jnp.where(atmosphere, top[j + 1] if j < 3 else beyond, top[j - 1] if j else beyond)
        s = air[j]
        near = jnp.concatenate([before, s[:-1]], 0) + jnp.concatenate([s[1:], after], 0)
        near = near + pltpu.roll(s, 1, 1) + pltpu.roll(s, s.shape[1] - 1, 1)
        flux = coeff[j] * (s + 0.2 * (near - 4.0 * s))
        picked = gather_cells(flux, cells[j].astype(I32))
        slot = jnp.where(atmosphere, block_of(other, 3 - j), block_of(pack, 4 + j)).astype(I32)
        total = scatter_add(total, weights[j] * picked, slot)
    partial[...] = as_rows(total)


def source_kernel(partial, partial_sw, pack, other, code, rhs, fifth, sixth):
    atmosphere = lax.axis_index("comp") == 0
    sea = jnp.where(atmosphere, other[256:272, :], pack[256:272, :])
    diagonal = jnp.where(atmosphere, other[272:288, :], pack[272:288, :])
    total = partial[...] + partial_sw[...] + sea
    rhs[...] = total
    for k, part in enumerate((total, diagonal, code[...])):
        fifth[16 * k : 16 * k + 16, :] = part
        sixth[8 * k : 8 * k + 8, :] = part[8:16]


def near_kernel(p1, p2, m1, m2, out):
    for k, (right, rows) in enumerate(((p1, slice(0, 16)), (m1, slice(80, 96)), (m1, slice(96, 112)))):
        out[16 * k : 16 * k + 16, :] = right[rows, :]
    for k, (right, rows) in enumerate(((p2, slice(8, 16)), (m2, slice(88, 96)), (m2, slice(104, 112)))):
        out[48 + 8 * k : 56 + 8 * k, :] = right[rows, :]


def edge_kernel(edge, out):
    out[...] = edge[...]


def trace_kernel(
    pack, other, inverse, own, near, fifth, sixth, p1, p2, p3, p4, m1, m2, m3, m4,
    send, keep, rhs, inv, code, code_up, code_down, eta,
):
    rows, width = rhs.shape
    groups = rows // 8

    def place(parts):
        at = 0
        for right, diagonal, face in parts:
            size = right.shape[0]
            rhs[at : at + size, :] = right[...]
            inv[at : at + size, :] = 1.0 / (diagonal[...] + 3.0)
            code[at : at + size, :] = face[...]
            at += size

    def thirds(ref, first, step, size):
        return [ref.at[first + k * step : first + k * step + size] for k in range(3)]

    others = [(p, m.at[80:96], m.at[96:112]) for p, m in ((p1, m1), (p2, m2), (p3, m3))]
    others.append((p4, m4.at[64:80], m4.at[80:96]))
    here = thirds(own, 0, 16, 16)
    on_each_component(
        lambda: place(
            [thirds(near, 48, 8, 8), thirds(near, 0, 16, 16), here, *others, thirds(fifth, 0, 16, 8)]
        ),
        lambda: place(
            [thirds(sixth, 0, 8, 8), thirds(fifth, 0, 16, 16), *others[::-1], here, thirds(near, 0, 16, 8)]
        ),
    )
    line = lax.broadcasted_iota(I32, (8, width), 0)

    def group(ref, g):
        return ref[8 * g : 8 * g + 8, :]

    def from_above(here, above):
        return jnp.where(line == 0, above, here)

    def from_below(here, below):
        return jnp.where(line == 7, below, here)

    downward = [pltpu.roll(group(code, g), 1, 0) for g in range(groups)]
    for g in range(groups):
        code_down[8 * g : 8 * g + 8, :] = from_above(downward[g], downward[max(g - 1, 0)])
    upward = [pltpu.roll(group(code, g), 7, 0) for g in range(groups)]
    for g in range(groups):
        code_up[8 * g : 8 * g + 8, :] = from_below(upward[g], upward[min(g + 1, groups - 1)])
    for g in range(groups):
        eta[8 * g : 8 * g + 8, :] = group(rhs, g) * group(inv, g)

    def sweep(step, carry):
        beside, above, below = {}, {}, {}

        def read(g):
            here = group(eta, g)
            left = pltpu.roll(here, 1, 1)
            right = pltpu.roll(here, width - 1, 1)
            beside[g] = left + right
            u, d = group(code_up, g), group(code_down, g)
            above[g] = pltpu.roll(jnp.where(u == 0.0, left, jnp.where(u == 1.0, here, right)), 1, 0)
            below[g] = pltpu.roll(jnp.where(d == 3.0, left, jnp.where(d == 4.0, here, right)), 7, 0)

        def write(g):
            up = from_above(above[g], above[max(g - 1, 0)])
            down = from_below(below[g], below[min(g + 1, groups - 1)])
            third = jnp.where(group(code, g) >= 3.0, down, up)
            eta[8 * g : 8 * g + 8, :] = (group(rhs, g) + (beside[g] + third)) * group(inv, g)

        for g in range(groups):
            read(g)
            if g:
                write(g - 1)
        write(groups - 1)
        return carry

    lax.fori_loop(1, SWEEPS, sweep, 0)

    atmosphere = lax.axis_index("comp") == 0
    sea = [jnp.where(atmosphere, other[256:272, :], m4[16:32, :])]
    slots = [jnp.where(atmosphere, block_of(other, 4), m4[0:16, :])]
    for a, b in ((m1, m3), (m2, m2), (m3, m1)):
        sea.append(jnp.where(atmosphere, a[112:128, :], b[112:128, :]))
        slots.append(jnp.where(atmosphere, a[64:80, :], b[64:80, :]))
    total = jnp.zeros((128, 64), F32)
    for i in range(4):
        at = 24 + 16 * i
        sst = 1.25 * sea[i] + 0.5 * eta[at : at + 16, :] - 0.25 * rhs[at : at + 16, :]
        picked = gather_cells(sst, slots[i].astype(I32))
        cell = jnp.where(atmosphere, block_of(pack, 4 + i), block_of(other, i)).astype(I32)
        weight = jnp.where(atmosphere, block_of(pack, 12 + i), block_of(other, 8 + i))
        total = scatter_add(total, weight * picked, cell)
    part = as_rows(total)
    send[...] = jnp.where(atmosphere, eta[24:40, :], part)
    keep[...] = jnp.where(atmosphere, part * inverse[...], 0.0)


def shards(state, coeff, vertical, send_cell, incoming_marine_slot, remap_weight):
    tiles = lax.axis_size("tile")
    block = state.shape[1:]
    lines, width = block

    def swap(x):
        return lax.ppermute(x, "comp", [(0, 1), (1, 0)])

    def move(x, atmosphere_from, ocean_from):
        pairs = [((t + atmosphere_from) % tiles, t) for t in range(tiles)]
        pairs += [(tiles + (t + ocean_from) % tiles, tiles + t) for t in range(tiles)]
        return lax.ppermute(x, GRID, pairs)

    arguments = (send_cell, remap_weight, incoming_marine_slot, state, coeff, vertical)
    pack, code = call(
        pack_kernel, [(18 * lines, width), block],
        *[pltpu.with_memory_space_constraint(x, pltpu.HBM) for x in arguments],
        scratch=[
            pltpu.VMEM(send_cell.shape, I32),
            pltpu.VMEM(send_cell.shape, F32),
            pltpu.VMEM(block, I32),
            pltpu.SemaphoreType.DMA((5,)),
        ],
        where=pltpu.HBM,
    )
    other = swap(pack)
    *messages, edge = call(
        message_kernel, [(8 * lines, width)] * 3 + [(6 * lines, width), (8, width)], pack, other, code
    )
    edge_in = move(edge, 5, 1)
    messages_in = [move(m, j, -j) for j, m in enumerate(messages, 1)]
    m1_in, m2_in, m3_in, m4_in = messages_in
    (inverse,) = call(share_kernel, [block], pack, flops=10**9)
    (edge_in,) = call(edge_kernel, [(8, width)], edge_in, flops=10**9)
    (partial,) = call(flux_kernel, [block], edge_in, m1_in, m3_in, m2_in, m4_in, pack, other)
    rhs, fifth, sixth = call(
        source_kernel, [block, (3 * lines, width), (24, width)], partial, swap(partial), pack, other, code
    )
    p1_in, p2_in, p3_in, p4_in = (move(rhs, j, -j) for j in range(1, 5))
    fifth_in = move(fifth, 5, -5)
    sixth_in = lax.ppermute(sixth, GRID, [(tiles + t, tiles + (t + 6) % tiles) for t in range(tiles)])
    (near,) = call(near_kernel, [(72, width)], p1_in, p2_in, m1_in, m2_in)
    window = (6 * lines + 16, width)
    send, keep = call(
        trace_kernel, [block, block],
        pack, other, inverse, fifth, swap(near), fifth_in, sixth_in, p1_in, p2_in, p3_in, p4_in, *messages_in,
        scratch=[pltpu.VMEM(window, F32)] * 6,
    )
    return (keep + swap(send) * inverse)[None]


def solution(mesh):
    table = P(GRID, None)
    grid = P("comp", "tile", None)
    return jax.shard_map(
        shards,
        mesh=mesh,
        in_specs=(grid, grid, P("tile", None), table, table, table),
        out_specs=grid,
        check_vma=False,
    )
```

time: 58.6 us -> 41.7 us (0.71)
  starting transfers between devices: 32.2 us -> 21.5 us
  local copies, waits for them, and re-layouts: 4.86 us -> 0 us
  waiting for transfers between devices: 9.09 us -> 7.65 us
    ppermute x16 -> x10, starting transfers between devices: 28 us -> 19 us  [move(): return lax.ppermute(x, GRID, pairs)]
    unnamed x12 -> x0, local copies, waits for them, and re-layouts: 4.86 us -> none
    ppermute x7 -> x4, starting transfers between devices: 4.21 us -> 1.79 us  [swap(): return lax.ppermute(x, 'comp', [(0, 1), (1, 0)])]
    ppermute x16 -> x10, waiting for transfers between devices: 6.03 us -> 4.43 us  [move(): return lax.ppermute(x, GRID, pairs)]
    ppermute x0 -> x1, starting transfers between devices: none -> 0.65 us  [shards(): lax.ppermute(sixth, GRID, [(tiles + t, tiles + (t + 6) % tiles) for t in...]
    ppermute x7 -> x4, waiting for transfers between devices: 3.07 us -> 3.22 us  [swap(): return lax.ppermute(x, 'comp', [(0, 1), (1, 0)])]
    pallas_call x5 -> x8, Pallas kernels: 11.3 us -> 11.3 us  [call(): pl.pallas_call(kernel, out_shape=out, in_specs=[pl.BlockSpec(memory_space...]
  transfers between devices with their start and end apart: 23 -> 15, of which waited for: 6 -> 4; matrix products, arithmetic and copies ran while one was open for 0% -> 0% of each run, Pallas kernels for 8% -> 6%
where the time goes in v2:
time: 41.7 us; the launch traced here: 41.2 us
  starting transfers between devices  21.5 us (52%)
  Pallas kernels  11.3 us (27%)
  waiting for transfers between devices  7.65 us (18%)
  other arithmetic  0.61 us (1%)
    ppermute x10, starting transfers between devices, move(): return lax.ppermute(x, GRID, pairs)  19 us
    pallas_call x8, Pallas kernels, call(): pl.pallas_call(kernel, out_shape=out, in_specs=[pl.BlockSpec(memory_space...  11.3 us
    ppermute x10, waiting for transfers between devices, move(): return lax.ppermute(x, GRID, pairs)  4.43 us
    ppermute x4, waiting for transfers between devices, swap(): return lax.ppermute(x, 'comp', [(0, 1), (1, 0)])  3.22 us
    ppermute x4, starting transfers between devices, swap(): return lax.ppermute(x, 'comp', [(0, 1), (1, 0)])  1.79 us
  transfers between devices with their start and end apart: 15, of which 4 were waited for; matrix products, arithmetic and copies ran while one was open for 0% of the time, Pallas kernels for 6%

profile of v2, /device:TPU:0, one launch (start us, length us, event | category | flops | bytes accessed | tf_op | source)
XLA Modules:
  0.0 41.2 jit_solution(3262103657562321586)
XLA Ops:
  0.0 1.1 %shard_map.64 = (f32[288,256]{1,0:T(8,128)S(1)}, f32[16,256]{1,0:T(8,128)S(1)}) custom-call(s32[8,4096]{1,0:T(8,128)} %cells.1, f32[8,4096]{1,0:T(8,128)} %weights.1, s32[8,4096]{1,0:T(8,128)} %slots.1, f32[1,16,256]{2,1,0:T(8,128)} %state.1, f32[1,16,256]{2,1,0:T(8,128)} %coeff.1, s32[16,256]{1,0:T(8,128)} %vertical.1), custom_call_target="tpu_custom_call" | custom-call | tf_op jit(solution)/shard_map/pallas_call | solution.py:23
  1.2 0.4 %collective-permute-start = (f32[288,256]{1,0:T(8,128)S(1)}, f32[288,256]{1,0:T(8,128)S(1)}, u32[]{:S(2)}, u32[]{:S(2)}) collective-permute-start(f32[288,256]{1,0:T(8,128)S(1)} %get-tuple-element.17.pack), channel_id=1, source_target_pairs={{0,16},{16,0},{1,17},{17,1},{2,18},{18,2},{3,19},{19,3},{4,20},{20... | collective-permute-start | bytes 884744 | tf_op jit(solution)/shard_map/ppermute | solution.py:333
  1.6 1.2 %collective-permute-done.other = f32[288,256]{1,0:T(8,128)S(1)} collective-permute-done((f32[288,256]{1,0:T(8,128)S(1)}, f32[288,256]{1,0:T(8,128)S(1)}, u32[]{:S(2)}, u32[]{:S(2)}) %collective-permute-start) | collective-permute-done | bytes 294944 | tf_op jit(solution)/shard_map/ppermute | solution.py:333
  2.9 7.0 %collective-permute-start.2 = (f32[128,256]{1,0:T(8,128)S(1)}, f32[128,256]{1,0:T(8,128)S(1)}, u32[]{:S(2)}, u32[]{:S(2)}) collective-permute-start(f32[128,256]{1,0:T(8,128)S(1)} %get-tuple-element.20), channel_id=1, source_target_pairs={{1,0},{2,1},{3,2},{4,3},{5,4},{6,5},{7,6},{8,7},{9,8},{10,9},{11,1... | collective-permute-start | bytes 393224 | tf_op jit(solution)/shard_map/ppermute | solution.py:338
  9.8 0.5 %collective-permute-start.4 = (f32[128,256]{1,0:T(8,128)S(1)}, f32[128,256]{1,0:T(8,128)S(1)}, u32[]{:S(2)}, u32[]{:S(2)}) collective-permute-start(f32[128,256]{1,0:T(8,128)S(1)} %get-tuple-element.22), channel_id=1, source_target_pairs={{2,0},{3,1},{4,2},{5,3},{6,4},{7,5},{8,6},{9,7},{10,8},{11,9},{12,... | collective-permute-start | bytes 393224 | tf_op jit(solution)/shard_map/ppermute | solution.py:338
  10.3 0.5 %collective-permute-start.3 = (f32[128,256]{1,0:T(8,128)S(1)}, f32[128,256]{1,0:T(8,128)S(1)}, u32[]{:S(2)}, u32[]{:S(2)}) collective-permute-start(f32[128,256]{1,0:T(8,128)S(1)} %get-tuple-element.21), channel_id=1, source_target_pairs={{3,0},{4,1},{5,2},{6,3},{7,4},{8,5},{9,6},{10,7},{11,8},{12,9},{13... | collective-permute-start | bytes 393224 | tf_op jit(solution)/shard_map/ppermute | solution.py:338
  10.8 1.3 %collective-permute-start.1 = (f32[8,256]{1,0:T(8,128)S(1)}, f32[8,256]{1,0:T(8,128)S(1)}, u32[]{:S(2)}, u32[]{:S(2)}) collective-permute-start(f32[8,256]{1,0:T(8,128)S(1)} %get-tuple-element.19), channel_id=1, source_target_pairs={{5,0},{6,1},{7,2},{8,3},{9,4},{10,5},{11,6},{12,7},{13,8},{14,9},{... | collective-permute-start | bytes 24584 | tf_op jit(solution)/shard_map/ppermute | solution.py:338
  12.1 1.3 %collective-permute-start.5 = (f32[96,256]{1,0:T(8,128)S(1)}, f32[96,256]{1,0:T(8,128)S(1)}, u32[]{:S(2)}, u32[]{:S(2)}) collective-permute-start(f32[96,256]{1,0:T(8,128)S(1)} %get-tuple-element.23), channel_id=1, source_target_pairs={{4,0},{5,1},{6,2},{7,3},{8,4},{9,5},{10,6},{11,7},{12,8},{13,9},{1... | collective-permute-start | bytes 294920 | tf_op jit(solution)/shard_map/ppermute | solution.py:338
  13.5 4.4 %collective-permute-done.1.edge = f32[8,256]{1,0:T(8,128)S(1)} collective-permute-done((f32[8,256]{1,0:T(8,128)S(1)}, f32[8,256]{1,0:T(8,128)S(1)}, u32[]{:S(2)}, u32[]{:S(2)}) %collective-permute-start.1) | collective-permute-done | bytes 8224 | tf_op jit(solution)/shard_map/ppermute | solution.py:338
  17.9 0.0 collective-permute-done.5.m4
  17.9 0.0 collective-permute-done.2.m1
  17.9 0.0 collective-permute-done.4.m2
  17.9 0.0 collective-permute-done.3.m3
  17.9 2.3 %shard_map.68.partial = f32[16,256]{1,0:T(8,128)S(1)} custom-call(f32[8,256]{1,0:T(8,128)S(1)} %shard_map.67.edge, f32[128,256]{1,0:T(8,128)S(1)} %collective-permute-done.2.m1, f32[128,256]{1,0:T(8,128)S(1)} %collective-permute-done.3.m3, f32[128,256]{1,0:T(8,128)S(1)} %collective-permute-done.4.m2, f32[96,256]{1,0:T(8,128)S(1)} %collective-permute-done.5.m4, ...), custom_call_target="tpu_custom_call" | custom-call | tf_op jit(solution)/shard_map/pallas_call | solution.py:23
  20.2 0.0 collective-permute-start.6
  20.2 1.2 %collective-permute-done.6.partial_sw = f32[16,256]{1,0:T(8,128)S(1)} collective-permute-done((f32[16,256]{1,0:T(8,128)S(1)}, f32[16,256]{1,0:T(8,128)S(1)}, u32[]{:S(2)}, u32[]{:S(2)}) %collective-permute-start.6) | collective-permute-done | bytes 16416 | tf_op jit(solution)/shard_map/ppermute | solution.py:333
  21.4 2.0 %collective-permute-start.7 = (f32[16,256]{1,0:T(8,128)S(1)}, f32[16,256]{1,0:T(8,128)S(1)}, u32[]{:S(2)}, u32[]{:S(2)}) collective-permute-start(f32[16,256]{1,0:T(8,128)S(1)} %get-tuple-element.25), channel_id=1, source_target_pairs={{1,0},{2,1},{3,2},{4,3},{5,4},{6,5},{7,6},{8,7},{9,8},{10,9},{11,1... | collective-permute-start | bytes 49160 | tf_op jit(solution)/shard_map/ppermute | solution.py:338
  23.4 3.1 %collective-permute-start.8 = (f32[16,256]{1,0:T(8,128)S(1)}, f32[16,256]{1,0:T(8,128)S(1)}, u32[]{:S(2)}, u32[]{:S(2)}) collective-permute-start(f32[16,256]{1,0:T(8,128)S(1)} %get-tuple-element.25), channel_id=1, source_target_pairs={{2,0},{3,1},{4,2},{5,3},{6,4},{7,5},{8,6},{9,7},{10,8},{11,9},{12,... | collective-permute-start | bytes 49160 | tf_op jit(solution)/shard_map/ppermute | solution.py:338
  26.6 1.1 %collective-permute-start.12 = (f32[16,256]{1,0:T(8,128)S(1)}, f32[16,256]{1,0:T(8,128)S(1)}, u32[]{:S(2)}, u32[]{:S(2)}) collective-permute-start(f32[16,256]{1,0:T(8,128)S(1)} %get-tuple-element.25), channel_id=1, source_target_pairs={{3,0},{4,1},{5,2},{6,3},{7,4},{8,5},{9,6},{10,7},{11,8},{12,9},{13... | collective-permute-start | bytes 49160 | tf_op jit(solution)/shard_map/ppermute | solution.py:338
  27.7 0.4 %collective-permute-start.13 = (f32[16,256]{1,0:T(8,128)S(1)}, f32[16,256]{1,0:T(8,128)S(1)}, u32[]{:S(2)}, u32[]{:S(2)}) collective-permute-start(f32[16,256]{1,0:T(8,128)S(1)} %get-tuple-element.25), channel_id=1, source_target_pairs={{4,0},{5,1},{6,2},{7,3},{8,4},{9,5},{10,6},{11,7},{12,8},{13,9},{1... | collective-permute-start | bytes 49160 | tf_op jit(solution)/shard_map/ppermute | solution.py:338
  28.1 1.7 %collective-permute-start.10 = (f32[48,256]{1,0:T(8,128)S(1)}, f32[48,256]{1,0:T(8,128)S(1)}, u32[]{:S(2)}, u32[]{:S(2)}) collective-permute-start(f32[48,256]{1,0:T(8,128)S(1)} %get-tuple-element.24.own), channel_id=1, source_target_pairs={{5,0},{6,1},{7,2},{8,3},{9,4},{10,5},{11,6},{12,7},{13,8},{14,9},{... | collective-permute-start | bytes 147464 | tf_op jit(solution)/shard_map/ppermute | solution.py:338
  29.8 0.0 collective-permute-done.7.p1
  29.8 0.7 %collective-permute-start.11 = (f32[24,256]{1,0:T(8,128)S(1)}, f32[24,256]{1,0:T(8,128)S(1)}, u32[]{:S(2)}, u32[]{:S(2)}) collective-permute-start(f32[24,256]{1,0:T(8,128)S(1)} %get-tuple-element.26), channel_id=1, source_target_pairs={{16,22},{17,23},{18,24},{19,25},{20,26},{21,27},{22,28},{23,29},{2... | collective-permute-start | bytes 73736 | tf_op jit(solution)/shard_map/ppermute | solution.py:367
  30.5 0.0 collective-permute-done.8.p2
  30.5 0.6 %collective-permute-start.9 = (f32[72,256]{1,0:T(8,128)S(1)}, f32[72,256]{1,0:T(8,128)S(1)}, u32[]{:S(2)}, u32[]{:S(2)}) collective-permute-start(f32[72,256]{1,0:T(8,128)S(1)} %shard_map.70), channel_id=1, source_target_pairs={{0,16},{16,0},{1,17},{17,1},{2,18},{18,2},{3,19},{19,3},{4,20},{20... | collective-permute-start | bytes 221192 | tf_op jit(solution)/shard_map/ppermute | solution.py:333
  31.1 2.4 %shard_map.65.inverse = f32[16,256]{1,0:T(8,128)S(1)} custom-call(f32[288,256]{1,0:T(8,128)S(1)} %get-tuple-element.17.pack), custom_call_target="tpu_custom_call" | custom-call | flops 1000000000 | tf_op jit(solution)/shard_map/pallas_call | solution.py:23
  33.5 0.0 collective-permute-done.12.p3
  33.5 0.0 collective-permute-done.13.p4
  33.5 0.0 collective-permute-done.11.sixth
  33.5 0.0 collective-permute-done.10.fifth
  33.5 0.0 collective-permute-done.9.near
  33.5 5.4 %shard_map.71 = (f32[16,256]{1,0:T(8,128)S(1)}, f32[16,256]{1,0:T(8,128)S(1)}) custom-call(f32[288,256]{1,0:T(8,128)S(1)} %get-tuple-element.17.pack, f32[288,256]{1,0:T(8,128)S(1)} %collective-permute-done.other, f32[16,256]{1,0:T(8,128)S(1)} %shard_map.65.inverse, f32[48,256]{1,0:T(8,128)S(1)} %get-tuple-element.24.own, ...), custom_call_target="tpu_custom_call" | custom-call | tf_op jit(solution)/shard_map/pallas_call | solution.py:23
  39.0 0.8 %collective-permute-start.14 = (f32[16,256]{1,0:T(8,128)S(1)}, f32[16,256]{1,0:T(8,128)S(1)}, u32[]{:S(2)}, u32[]{:S(2)}) collective-permute-start(f32[16,256]{1,0:T(8,128)S(1)} %get-tuple-element.28), channel_id=1, source_target_pairs={{0,16},{16,0},{1,17},{17,1},{2,18},{18,2},{3,19},{19,3},{4,20},{20... | collective-permute-start | bytes 49160 | tf_op jit(solution)/shard_map/ppermute | solution.py:333
  39.7 0.8 %collective-permute-done.14 = f32[16,256]{1,0:T(8,128)S(1)} collective-permute-done((f32[16,256]{1,0:T(8,128)S(1)}, f32[16,256]{1,0:T(8,128)S(1)}, u32[]{:S(2)}, u32[]{:S(2)}) %collective-permute-start.14) | collective-permute-done | bytes 16416 | tf_op jit(solution)/shard_map/ppermute | solution.py:333
  40.6 0.6 %add_bitcast_fusion = f32[1,16,256]{2,1,0:T(8,128)} fusion(f32[16,256]{1,0:T(8,128)S(1)} %get-tuple-element.27, f32[16,256]{1,0:T(8,128)S(1)} %collective-permute-done.14, f32[16,256]{1,0:T(8,128)S(1)} %shard_map.65.inverse), kind=kLoop, calls=%fused_computation | loop fusion | flops 8192 | bytes 65536 | tf_op jit(solution)/shard_map/broadcast_in_dim | solution.py:375
  (4 shorter events, 0.1 us)
Async XLA Ops:
  1.2 1.7 %collective-permute-start = (f32[288,256]{1,0:T(8,128)S(1)}, f32[288,256]{1,0:T(8,128)S(1)}, u32[]{:S(2)}, u32[]{:S(2)}) collective-permute-start(f32[288,256]{1,0:T(8,128)S(1)} %get-tuple-element.17.pack), channel_id=1, source_target_pairs={{0,16},{16,0},{1,17},{17,1},{2,18},{18,2},{3,19},{19,3},{4,20},{20... | collective-permute-start | bytes 884744 | tf_op jit(solution)/shard_map/ppermute | solution.py:333
  2.9 15.0 %collective-permute-start.2 = (f32[128,256]{1,0:T(8,128)S(1)}, f32[128,256]{1,0:T(8,128)S(1)}, u32[]{:S(2)}, u32[]{:S(2)}) collective-permute-start(f32[128,256]{1,0:T(8,128)S(1)} %get-tuple-element.20), channel_id=1, source_target_pairs={{1,0},{2,1},{3,2},{4,3},{5,4},{6,5},{7,6},{8,7},{9,8},{10,9},{11,1... | collective-permute-start | bytes 393224 | tf_op jit(solution)/shard_map/ppermute | solution.py:338
  9.8 8.1 %collective-permute-start.4 = (f32[128,256]{1,0:T(8,128)S(1)}, f32[128,256]{1,0:T(8,128)S(1)}, u32[]{:S(2)}, u32[]{:S(2)}) collective-permute-start(f32[128,256]{1,0:T(8,128)S(1)} %get-tuple-element.22), channel_id=1, source_target_pairs={{2,0},{3,1},{4,2},{5,3},{6,4},{7,5},{8,6},{9,7},{10,8},{11,9},{12,... | collective-permute-start | bytes 393224 | tf_op jit(solution)/shard_map/ppermute | solution.py:338
  10.3 7.6 %collective-permute-start.3 = (f32[128,256]{1,0:T(8,128)S(1)}, f32[128,256]{1,0:T(8,128)S(1)}, u32[]{:S(2)}, u32[]{:S(2)}) collective-permute-start(f32[128,256]{1,0:T(8,128)S(1)} %get-tuple-element.21), channel_id=1, source_target_pairs={{3,0},{4,1},{5,2},{6,3},{7,4},{8,5},{9,6},{10,7},{11,8},{12,9},{13... | collective-permute-start | bytes 393224 | tf_op jit(solution)/shard_map/ppermute | solution.py:338
  10.8 7.1 %collective-permute-start.1 = (f32[8,256]{1,0:T(8,128)S(1)}, f32[8,256]{1,0:T(8,128)S(1)}, u32[]{:S(2)}, u32[]{:S(2)}) collective-permute-start(f32[8,256]{1,0:T(8,128)S(1)} %get-tuple-element.19), channel_id=1, source_target_pairs={{5,0},{6,1},{7,2},{8,3},{9,4},{10,5},{11,6},{12,7},{13,8},{14,9},{... | collective-permute-start | bytes 24584 | tf_op jit(solution)/shard_map/ppermute | solution.py:338
  12.1 5.8 %collective-permute-start.5 = (f32[96,256]{1,0:T(8,128)S(1)}, f32[96,256]{1,0:T(8,128)S(1)}, u32[]{:S(2)}, u32[]{:S(2)}) collective-permute-start(f32[96,256]{1,0:T(8,128)S(1)} %get-tuple-element.23), channel_id=1, source_target_pairs={{4,0},{5,1},{6,2},{7,3},{8,4},{9,5},{10,6},{11,7},{12,8},{13,9},{1... | collective-permute-start | bytes 294920 | tf_op jit(solution)/shard_map/ppermute | solution.py:338
  20.2 1.2 %collective-permute-start.6 = (f32[16,256]{1,0:T(8,128)S(1)}, f32[16,256]{1,0:T(8,128)S(1)}, u32[]{:S(2)}, u32[]{:S(2)}) collective-permute-start(f32[16,256]{1,0:T(8,128)S(1)} %shard_map.68.partial), channel_id=1, source_target_pairs={{0,16},{16,0},{1,17},{17,1},{2,18},{18,2},{3,19},{19,3},{4,20},{20... | collective-permute-start | bytes 49160 | tf_op jit(solution)/shard_map/ppermute | solution.py:333
  21.4 8.4 %collective-permute-start.7 = (f32[16,256]{1,0:T(8,128)S(1)}, f32[16,256]{1,0:T(8,128)S(1)}, u32[]{:S(2)}, u32[]{:S(2)}) collective-permute-start(f32[16,256]{1,0:T(8,128)S(1)} %get-tuple-element.25), channel_id=1, source_target_pairs={{1,0},{2,1},{3,2},{4,3},{5,4},{6,5},{7,6},{8,7},{9,8},{10,9},{11,1... | collective-permute-start | bytes 49160 | tf_op jit(solution)/shard_map/ppermute | solution.py:338
  23.4 7.0 %collective-permute-start.8 = (f32[16,256]{1,0:T(8,128)S(1)}, f32[16,256]{1,0:T(8,128)S(1)}, u32[]{:S(2)}, u32[]{:S(2)}) collective-permute-start(f32[16,256]{1,0:T(8,128)S(1)} %get-tuple-element.25), channel_id=1, source_target_pairs={{2,0},{3,1},{4,2},{5,3},{6,4},{7,5},{8,6},{9,7},{10,8},{11,9},{12,... | collective-permute-start | bytes 49160 | tf_op jit(solution)/shard_map/ppermute | solution.py:338
  26.6 6.9 %collective-permute-start.12 = (f32[16,256]{1,0:T(8,128)S(1)}, f32[16,256]{1,0:T(8,128)S(1)}, u32[]{:S(2)}, u32[]{:S(2)}) collective-permute-start(f32[16,256]{1,0:T(8,128)S(1)} %get-tuple-element.25), channel_id=1, source_target_pairs={{3,0},{4,1},{5,2},{6,3},{7,4},{8,5},{9,6},{10,7},{11,8},{12,9},{13... | collective-permute-start | bytes 49160 | tf_op jit(solution)/shard_map/ppermute | solution.py:338
  27.7 5.8 %collective-permute-start.13 = (f32[16,256]{1,0:T(8,128)S(1)}, f32[16,256]{1,0:T(8,128)S(1)}, u32[]{:S(2)}, u32[]{:S(2)}) collective-permute-start(f32[16,256]{1,0:T(8,128)S(1)} %get-tuple-element.25), channel_id=1, source_target_pairs={{4,0},{5,1},{6,2},{7,3},{8,4},{9,5},{10,6},{11,7},{12,8},{13,9},{1... | collective-permute-start | bytes 49160 | tf_op jit(solution)/shard_map/ppermute | solution.py:338
  28.1 5.4 %collective-permute-start.10 = (f32[48,256]{1,0:T(8,128)S(1)}, f32[48,256]{1,0:T(8,128)S(1)}, u32[]{:S(2)}, u32[]{:S(2)}) collective-permute-start(f32[48,256]{1,0:T(8,128)S(1)} %get-tuple-element.24.own), channel_id=1, source_target_pairs={{5,0},{6,1},{7,2},{8,3},{9,4},{10,5},{11,6},{12,7},{13,8},{14,9},{... | collective-permute-start | bytes 147464 | tf_op jit(solution)/shard_map/ppermute | solution.py:338
  29.8 3.7 %collective-permute-start.11 = (f32[24,256]{1,0:T(8,128)S(1)}, f32[24,256]{1,0:T(8,128)S(1)}, u32[]{:S(2)}, u32[]{:S(2)}) collective-permute-start(f32[24,256]{1,0:T(8,128)S(1)} %get-tuple-element.26), channel_id=1, source_target_pairs={{16,22},{17,23},{18,24},{19,25},{20,26},{21,27},{22,28},{23,29},{2... | collective-permute-start | bytes 73736 | tf_op jit(solution)/shard_map/ppermute | solution.py:367
  30.5 3.0 %collective-permute-start.9 = (f32[72,256]{1,0:T(8,128)S(1)}, f32[72,256]{1,0:T(8,128)S(1)}, u32[]{:S(2)}, u32[]{:S(2)}) collective-permute-start(f32[72,256]{1,0:T(8,128)S(1)} %shard_map.70), channel_id=1, source_target_pairs={{0,16},{16,0},{1,17},{17,1},{2,18},{18,2},{3,19},{19,3},{4,20},{20... | collective-permute-start | bytes 221192 | tf_op jit(solution)/shard_map/ppermute | solution.py:333
  39.0 1.6 %collective-permute-start.14 = (f32[16,256]{1,0:T(8,128)S(1)}, f32[16,256]{1,0:T(8,128)S(1)}, u32[]{:S(2)}, u32[]{:S(2)}) collective-permute-start(f32[16,256]{1,0:T(8,128)S(1)} %get-tuple-element.28), channel_id=1, source_target_pairs={{0,16},{16,0},{1,17},{17,1},{2,18},{18,2},{3,19},{19,3},{4,20},{20... | collective-permute-start | bytes 49160 | tf_op jit(solution)/shard_map/ppermute | solution.py:333

commit v3 on v2

--- a/solution.py
+++ b/solution.py
@@ -129,23 +129,32 @@
 
 
 def block_of(ref, k):
-    return ref[16 * k : 16 * k + 16, :]
+    return ref[16 * k : 16 * k + 16]
 
 
 def message_kernel(pack, other, code, m1, m2, m3, m4, edge):
     def fill(air, sea, rows, rows_back):
+        s = air[256:272, :]
+        coeff = air[272:288, :]
+        none = jnp.zeros_like(s[0:1])
+        near = jnp.concatenate([none, s[:-1]], 0) + jnp.concatenate([s[1:], none], 0)
+        near = near + pltpu.roll(s, 1, 1) + pltpu.roll(s, s.shape[1] - 1, 1)
+        flux = coeff * (s + 0.2 * (near - 4.0 * s))
+        ends = jnp.concatenate([coeff[0:1], coeff[15:16], s[0:1], s[15:16], none, none, none, none], 0)
         for j, m in enumerate((m1, m2, m3)):
             m[0:16, :] = block_of(air, rows[j])
             m[16:32, :] = block_of(air, 8 + rows[j])
-            m[32:64, :] = air[256:288, :]
-            m[64:80, :] = block_of(sea, rows_back[j])
-            m[80:96, :] = sea[272:288, :]
-            m[96:112, :] = code[...]
-            m[112:128, :] = sea[256:272, :]
-        m4[32:64, :] = air[256:288, :]
-        m4[64:80, :] = sea[272:288, :]
-        m4[80:96, :] = code[...]
-        edge[...] = air[256:264, :]
+            m[32:48, :] = flux
+            m[48:64, :] = block_of(sea, rows_back[j])
+            m[64:72, :] = ends
+            m[72:88, :] = sea[272:288, :]
+            m[88:104, :] = code[...]
+            m[104:120, :] = sea[256:272, :]
+        m4[32:48, :] = flux
+        m4[48:56, :] = ends
+        m4[56:72, :] = sea[272:288, :]
+        m4[72:88, :] = code[...]
+        edge[...] = s[0:8]
 
     def atmosphere():
         fill(pack, other, (3, 2, 1), (5, 6, 7))
@@ -173,37 +182,43 @@
     on_each_component(atmosphere, ocean)
 
 
-def flux_kernel(edge, m1, m3, m2, m4, pack, other, partial):
+def edge_kernel(edge, out):
+    out[...] = edge[...]
+
+
+def add_fluxes(total, cells, weights, flux, ends, before, after, slots):
+    first = flux[0:1] + ends[0:1] * (0.2 * before)
+    last = flux[15:16] + ends[1:2] * (0.2 * after)
+    flux = jnp.concatenate([first, flux[1:15], last], 0)
+    return scatter_add(total, weights * gather_cells(flux, cells.astype(I32)), slots.astype(I32))
+
+
+def flux_kernel(edge, m1, m2, m3, m4, own, pack, other, partial):
     atmosphere = lax.axis_index("comp") == 0
 
-    def part(k):
-        rows = slice(16 * k, 16 * k + 16)
-        local = block_of(other, (4, 12, 16, 17)[k])
-        return [
-            jnp.where(atmosphere, a[rows, :], b)
-            for a, b in ((m1, local), (m2, m1[rows, :]), (m3, m2[rows, :]), (m4, m3[rows, :]))
-        ]
-
-    cells, weights, air, coeff = (part(k) for k in range(4))
-    top = [a[0:1] for a in air]
-    bottom = [a[15:16] for a in air]
-    beyond = edge[0:1]
+    def either(a, b):
+        return jnp.where(atmosphere, a, b)
+
+    def part(m):
+        return m[0:16, :], m[16:32, :], m[32:48, :], m[64:72, :]
+
     total = jnp.zeros((128, 64), F32)
-    for j in range(4):
-        before = jnp.where(
-            atmosphere,
-            bottom[j - 1] if j else pack[271:272, :],
-            bottom[j + 1] if j < 3 else m4[47:48, :],
-        )
-        after = jnp.where(atmosphere, top[j + 1] if j < 3 else beyond, top[j - 1] if j else beyond)
-        s = air[j]
-        near = jnp.concatenate([before, s[:-1]], 0) + jnp.concatenate([s[1:], after], 0)
-        near = near + pltpu.roll(s, 1, 1) + pltpu.roll(s, s.shape[1] - 1, 1)
-        flux = coeff[j] * (s + 0.2 * (near - 4.0 * s))
-        picked = gather_cells(flux, cells[j].astype(I32))
-        slot = jnp.where(atmosphere, block_of(other, 3 - j), block_of(pack, 4 + j)).astype(I32)
-        total = scatter_add(total, weights[j] * picked, slot)
-    partial[...] = as_rows(total)
+    before = either(pack[271:272, :], m2[67:68, :])
+    after = either(m2[66:67, :], other[256:257, :])
+    total = add_fluxes(total, *part(m1), before, after, either(block_of(other, 3), block_of(pack, 5)))
+    before = either(m1[67:68, :], m3[67:68, :])
+    after = either(m3[66:67, :], m1[66:67, :])
+    total = add_fluxes(total, *part(m2), before, after, either(block_of(other, 2), block_of(pack, 6)))
+    before = either(m2[67:68, :], m4[51:52, :])
+    after = either(m4[50:51, :], m2[66:67, :])
+    total = add_fluxes(total, *part(m3), before, after, either(block_of(other, 1), block_of(pack, 7)))
+    before = either(m3[67:68, :], m1[67:68, :])
+    cells = either(m4[0:16, :], block_of(other, 4))
+    weights = either(m4[16:32, :], block_of(other, 12))
+    flux = either(m4[32:48, :], own[32:48, :])
+    ends = either(m4[48:56, :], own[64:72, :])
+    slots = either(block_of(other, 0), block_of(pack, 4))
+    partial[...] = as_rows(add_fluxes(total, cells, weights, flux, ends, before, edge[0:1, :], slots))
 
 
 def source_kernel(partial, partial_sw, pack, other, code, rhs, fifth, sixth):
@@ -218,14 +233,11 @@
 
 
 def near_kernel(p1, p2, m1, m2, out):
-    for k, (right, rows) in enumerate(((p1, slice(0, 16)), (m1, slice(80, 96)), (m1, slice(96, 112)))):
-        out[16 * k : 16 * k + 16, :] = right[rows, :]
-    for k, (right, rows) in enumerate(((p2, slice(8, 16)), (m2, slice(88, 96)), (m2, slice(104, 112)))):
-        out[48 + 8 * k : 56 + 8 * k, :] = right[rows, :]
-
-
-def edge_kernel(edge, out):
-    out[...] = edge[...]
+    out[0:16, :] = p1[...]
+    out[16:48, :] = m1[72:104, :]
+    out[48:56, :] = p2[8:16, :]
+    out[56:64, :] = m2[80:88, :]
+    out[64:72, :] = m2[96:104, :]
 
 
 def trace_kernel(
@@ -247,8 +259,8 @@
     def thirds(ref, first, step, size):
         return [ref.at[first + k * step : first + k * step + size] for k in range(3)]
 
-    others = [(p, m.at[80:96], m.at[96:112]) for p, m in ((p1, m1), (p2, m2), (p3, m3))]
-    others.append((p4, m4.at[64:80], m4.at[80:96]))
+    others = [(p, m.at[72:88], m.at[88:104]) for p, m in ((p1, m1), (p2, m2), (p3, m3))]
+    others.append((p4, m4.at[56:72], m4.at[72:88]))
     here = thirds(own, 0, 16, 16)
     on_each_component(
         lambda: place(
@@ -278,7 +290,7 @@
     for g in range(groups):
         eta[8 * g : 8 * g + 8, :] = group(rhs, g) * group(inv, g)
 
-    def sweep(step, carry):
+    def sweep(first, last):
         beside, above, below = {}, {}, {}
 
         def read(g):
@@ -291,26 +303,41 @@
             below[g] = pltpu.roll(jnp.where(d == 3.0, left, jnp.where(d == 4.0, here, right)), 7, 0)
 
         def write(g):
-            up = from_above(above[g], above[max(g - 1, 0)])
-            down = from_below(below[g], below[min(g + 1, groups - 1)])
+            up = from_above(above[g], above[max(g - 1, first)])
+            down = from_below(below[g], below[min(g + 1, last - 1)])
             third = jnp.where(group(code, g) >= 3.0, down, up)
             eta[8 * g : 8 * g + 8, :] = (group(rhs, g) + (beside[g] + third)) * group(inv, g)
 
-        for g in range(groups):
+        for g in range(first, last):
             read(g)
-            if g:
+            if g > first:
                 write(g - 1)
-        write(groups - 1)
-        return carry
-
-    lax.fori_loop(1, SWEEPS, sweep, 0)
+        write(last - 1)
+
+    def repeat(count, skip):
+        def several(_, carry):
+            for _ in range(4):
+                sweep(skip, groups - skip)
+            return carry
+
+        for _ in range(count % 4):
+            sweep(skip, groups - skip)
+        if count >= 4:
+            lax.fori_loop(0, count // 4, several, 0)
+
+    done = 1
+    for skip in range(3):
+        until = min(SWEEPS, SWEEPS - 16 + 8 * skip)
+        repeat(until - done, skip)
+        done = until
 
     atmosphere = lax.axis_index("comp") == 0
+    states = [m[104:120, :] for m in (m1, m2, m3)]
     sea = [jnp.where(atmosphere, other[256:272, :], m4[16:32, :])]
+    sea += [jnp.where(atmosphere, states[i], states[2 - i]) for i in range(3)]
     slots = [jnp.where(atmosphere, block_of(other, 4), m4[0:16, :])]
     for a, b in ((m1, m3), (m2, m2), (m3, m1)):
-        sea.append(jnp.where(atmosphere, a[112:128, :], b[112:128, :]))
-        slots.append(jnp.where(atmosphere, a[64:80, :], b[64:80, :]))
+        slots.append(jnp.where(atmosphere, a[48:64, :], b[48:64, :]))
     total = jnp.zeros((128, 64), F32)
     for i in range(4):
         at = 24 + 16 * i
@@ -350,15 +377,16 @@
         where=pltpu.HBM,
     )
     other = swap(pack)
+    tall = 4 * lines + 8
     *messages, edge = call(
-        message_kernel, [(8 * lines, width)] * 3 + [(6 * lines, width), (8, width)], pack, other, code
-    )
-    edge_in = move(edge, 5, 1)
-    messages_in = [move(m, j, -j) for j, m in enumerate(messages, 1)]
-    m1_in, m2_in, m3_in, m4_in = messages_in
+        message_kernel,
+        [(tall + 3 * lines, width)] * 3 + [(tall + lines, width), (8, width)],
+        pack, other, code,
+    )
+    (edge_in,) = call(edge_kernel, [(8, width)], move(edge, 5, 1), flops=10**9)
+    m1_in, m2_in, m3_in, m4_in = messages_in = [move(m, j, -j) for j, m in enumerate(messages, 1)]
     (inverse,) = call(share_kernel, [block], pack, flops=10**9)
-    (edge_in,) = call(edge_kernel, [(8, width)], edge_in, flops=10**9)
-    (partial,) = call(flux_kernel, [block], edge_in, m1_in, m3_in, m2_in, m4_in, pack, other)
+    (partial,) = call(flux_kernel, [block], edge_in, *messages_in, messages[1], pack, other, flops=10**9)
     rhs, fifth, sixth = call(
         source_kernel, [block, (3 * lines, width), (24, width)], partial, swap(partial), pack, other, code
     )

time: 41.7 us -> 40.6 us (0.974)
  Pallas kernels: 11.3 us -> 10.4 us
    pallas_call x8, Pallas kernels: 11.3 us -> 10.4 us  [call(): pl.pallas_call(kernel, out_shape=out, in_specs=[pl.BlockSpec(memory_space...]
  transfers between devices with their start and end apart: 15 -> 15, of which waited for: 4 -> 6; matrix products, arithmetic and copies ran while one was open for 0% -> 0% of each run, Pallas kernels for 6% -> 6%
where the time goes in v3:
time: 40.6 us; the launch traced here: 40.3 us
  starting transfers between devices  21.6 us (53%)
  Pallas kernels  10.4 us (26%)
  waiting for transfers between devices  7.53 us (19%)
  other arithmetic  0.61 us (2%)
    ppermute x10, starting transfers between devices, move(): return lax.ppermute(x, GRID, pairs)  18.8 us
    pallas_call x8, Pallas kernels, call(): pl.pallas_call(kernel, out_shape=out, in_specs=[pl.BlockSpec(memory_space...  10.4 us
    ppermute x10, waiting for transfers between devices, move(): return lax.ppermute(x, GRID, pairs)  4.31 us
    ppermute x4, waiting for transfers between devices, swap(): return lax.ppermute(x, 'comp', [(0, 1), (1, 0)])  3.22 us
    ppermute x4, starting transfers between devices, swap(): return lax.ppermute(x, 'comp', [(0, 1), (1, 0)])  2.16 us
  transfers between devices with their start and end apart: 15, of which 6 were waited for; matrix products, arithmetic and copies ran while one was open for 0% of the time, Pallas kernels for 6%

profile of v3, /device:TPU:0, one launch (start us, length us, event | category | flops | bytes accessed | tf_op | source)
XLA Modules:
  0.0 40.3 jit_solution(1430595570312283122)
XLA Ops:
  0.0 1.1 %shard_map.64 = (f32[288,256]{1,0:T(8,128)S(1)}, f32[16,256]{1,0:T(8,128)S(1)}) custom-call(s32[8,4096]{1,0:T(8,128)} %cells.1, f32[8,4096]{1,0:T(8,128)} %weights.1, s32[8,4096]{1,0:T(8,128)} %slots.1, f32[1,16,256]{2,1,0:T(8,128)} %state.1, f32[1,16,256]{2,1,0:T(8,128)} %coeff.1, s32[16,256]{1,0:T(8,128)} %vertical.1), custom_call_target="tpu_custom_call" | custom-call | tf_op jit(solution)/shard_map/pallas_call | solution.py:23
  1.2 0.4 %collective-permute-start = (f32[288,256]{1,0:T(8,128)S(1)}, f32[288,256]{1,0:T(8,128)S(1)}, u32[]{:S(2)}, u32[]{:S(2)}) collective-permute-start(f32[288,256]{1,0:T(8,128)S(1)} %get-tuple-element.17.pack), channel_id=1, source_target_pairs={{0,16},{16,0},{1,17},{17,1},{2,18},{18,2},{3,19},{19,3},{4,20},{20... | collective-permute-start | bytes 884744 | tf_op jit(solution)/shard_map/ppermute | solution.py:360
  1.6 1.2 %collective-permute-done.other = f32[288,256]{1,0:T(8,128)S(1)} collective-permute-done((f32[288,256]{1,0:T(8,128)S(1)}, f32[288,256]{1,0:T(8,128)S(1)}, u32[]{:S(2)}, u32[]{:S(2)}) %collective-permute-start) | collective-permute-done | bytes 294944 | tf_op jit(solution)/shard_map/ppermute | solution.py:360
  2.8 0.1 shard_map.66
  2.9 6.0 %collective-permute-start.3 = (f32[120,256]{1,0:T(8,128)S(1)}, f32[120,256]{1,0:T(8,128)S(1)}, u32[]{:S(2)}, u32[]{:S(2)}) collective-permute-start(f32[120,256]{1,0:T(8,128)S(1)} %get-tuple-element.21.own), channel_id=1, source_target_pairs={{2,0},{3,1},{4,2},{5,3},{6,4},{7,5},{8,6},{9,7},{10,8},{11,9},{12,... | collective-permute-start | bytes 368648 | tf_op jit(solution)/shard_map/ppermute | solution.py:365
  8.9 1.4 %collective-permute-start.2 = (f32[120,256]{1,0:T(8,128)S(1)}, f32[120,256]{1,0:T(8,128)S(1)}, u32[]{:S(2)}, u32[]{:S(2)}) collective-permute-start(f32[120,256]{1,0:T(8,128)S(1)} %get-tuple-element.20), channel_id=1, source_target_pairs={{1,0},{2,1},{3,2},{4,3},{5,4},{6,5},{7,6},{8,7},{9,8},{10,9},{11,1... | collective-permute-start | bytes 368648 | tf_op jit(solution)/shard_map/ppermute | solution.py:365
  10.4 0.5 %collective-permute-start.4 = (f32[120,256]{1,0:T(8,128)S(1)}, f32[120,256]{1,0:T(8,128)S(1)}, u32[]{:S(2)}, u32[]{:S(2)}) collective-permute-start(f32[120,256]{1,0:T(8,128)S(1)} %get-tuple-element.22), channel_id=1, source_target_pairs={{3,0},{4,1},{5,2},{6,3},{7,4},{8,5},{9,6},{10,7},{11,8},{12,9},{13... | collective-permute-start | bytes 368648 | tf_op jit(solution)/shard_map/ppermute | solution.py:365
  10.9 1.3 %collective-permute-start.1 = (f32[8,256]{1,0:T(8,128)S(1)}, f32[8,256]{1,0:T(8,128)S(1)}, u32[]{:S(2)}, u32[]{:S(2)}) collective-permute-start(f32[8,256]{1,0:T(8,128)S(1)} %get-tuple-element.19), channel_id=1, source_target_pairs={{5,0},{6,1},{7,2},{8,3},{9,4},{10,5},{11,6},{12,7},{13,8},{14,9},{... | collective-permute-start | bytes 24584 | tf_op jit(solution)/shard_map/ppermute | solution.py:365
  12.2 1.3 %collective-permute-start.5 = (f32[88,256]{1,0:T(8,128)S(1)}, f32[88,256]{1,0:T(8,128)S(1)}, u32[]{:S(2)}, u32[]{:S(2)}) collective-permute-start(f32[88,256]{1,0:T(8,128)S(1)} %get-tuple-element.23), channel_id=1, source_target_pairs={{4,0},{5,1},{6,2},{7,3},{8,4},{9,5},{10,6},{11,7},{12,8},{13,9},{1... | collective-permute-start | bytes 270344 | tf_op jit(solution)/shard_map/ppermute | solution.py:365
  13.5 4.1 %collective-permute-done.1.edge = f32[8,256]{1,0:T(8,128)S(1)} collective-permute-done((f32[8,256]{1,0:T(8,128)S(1)}, f32[8,256]{1,0:T(8,128)S(1)}, u32[]{:S(2)}, u32[]{:S(2)}) %collective-permute-start.1) | collective-permute-done | bytes 8224 | tf_op jit(solution)/shard_map/ppermute | solution.py:365
  17.6 0.1 collective-permute-done.5.m4
  17.8 0.0 collective-permute-done.3.m2
  17.8 0.0 collective-permute-done.2.m1
  17.8 0.0 collective-permute-done.4.m3
  17.8 2.1 %shard_map.68.partial = f32[16,256]{1,0:T(8,128)S(1)} custom-call(f32[8,256]{1,0:T(8,128)S(1)} %shard_map.67.edge, f32[120,256]{1,0:T(8,128)S(1)} %collective-permute-done.2.m1, f32[120,256]{1,0:T(8,128)S(1)} %collective-permute-done.3.m2, f32[120,256]{1,0:T(8,128)S(1)} %collective-permute-done.4.m3, f32[88,256]{1,0:T(8,128)S(1)} %collective-permute-done.5.m4, ...), custom_call_target="tpu_custom_call" | custom-call | flops 1000000000 | tf_op jit(solution)/shard_map/pallas_call | solution.py:23
  19.9 0.0 collective-permute-start.6
  19.9 1.2 %collective-permute-done.6.partial_sw = f32[16,256]{1,0:T(8,128)S(1)} collective-permute-done((f32[16,256]{1,0:T(8,128)S(1)}, f32[16,256]{1,0:T(8,128)S(1)}, u32[]{:S(2)}, u32[]{:S(2)}) %collective-permute-start.6) | collective-permute-done | bytes 16416 | tf_op jit(solution)/shard_map/ppermute | solution.py:360
  21.1 2.2 %collective-permute-start.7 = (f32[16,256]{1,0:T(8,128)S(1)}, f32[16,256]{1,0:T(8,128)S(1)}, u32[]{:S(2)}, u32[]{:S(2)}) collective-permute-start(f32[16,256]{1,0:T(8,128)S(1)} %get-tuple-element.25), channel_id=1, source_target_pairs={{1,0},{2,1},{3,2},{4,3},{5,4},{6,5},{7,6},{8,7},{9,8},{10,9},{11,1... | collective-permute-start | bytes 49160 | tf_op jit(solution)/shard_map/ppermute | solution.py:365
  23.3 2.0 %collective-permute-start.8 = (f32[16,256]{1,0:T(8,128)S(1)}, f32[16,256]{1,0:T(8,128)S(1)}, u32[]{:S(2)}, u32[]{:S(2)}) collective-permute-start(f32[16,256]{1,0:T(8,128)S(1)} %get-tuple-element.25), channel_id=1, source_target_pairs={{2,0},{3,1},{4,2},{5,3},{6,4},{7,5},{8,6},{9,7},{10,8},{11,9},{12,... | collective-permute-start | bytes 49160 | tf_op jit(solution)/shard_map/ppermute | solution.py:365
  25.3 2.2 %collective-permute-start.12 = (f32[16,256]{1,0:T(8,128)S(1)}, f32[16,256]{1,0:T(8,128)S(1)}, u32[]{:S(2)}, u32[]{:S(2)}) collective-permute-start(f32[16,256]{1,0:T(8,128)S(1)} %get-tuple-element.25), channel_id=1, source_target_pairs={{3,0},{4,1},{5,2},{6,3},{7,4},{8,5},{9,6},{10,7},{11,8},{12,9},{13... | collective-permute-start | bytes 49160 | tf_op jit(solution)/shard_map/ppermute | solution.py:365
  27.5 0.4 %collective-permute-start.13 = (f32[16,256]{1,0:T(8,128)S(1)}, f32[16,256]{1,0:T(8,128)S(1)}, u32[]{:S(2)}, u32[]{:S(2)}) collective-permute-start(f32[16,256]{1,0:T(8,128)S(1)} %get-tuple-element.25), channel_id=1, source_target_pairs={{4,0},{5,1},{6,2},{7,3},{8,4},{9,5},{10,6},{11,7},{12,8},{13,9},{1... | collective-permute-start | bytes 49160 | tf_op jit(solution)/shard_map/ppermute | solution.py:365
  27.9 1.4 %collective-permute-start.10 = (f32[48,256]{1,0:T(8,128)S(1)}, f32[48,256]{1,0:T(8,128)S(1)}, u32[]{:S(2)}, u32[]{:S(2)}) collective-permute-start(f32[48,256]{1,0:T(8,128)S(1)} %get-tuple-element.24.own), channel_id=1, source_target_pairs={{5,0},{6,1},{7,2},{8,3},{9,4},{10,5},{11,6},{12,7},{13,8},{14,9},{... | collective-permute-start | bytes 147464 | tf_op jit(solution)/shard_map/ppermute | solution.py:365
  29.3 0.0 collective-permute-done.7.p1
  29.3 0.7 %collective-permute-start.11 = (f32[24,256]{1,0:T(8,128)S(1)}, f32[24,256]{1,0:T(8,128)S(1)}, u32[]{:S(2)}, u32[]{:S(2)}) collective-permute-start(f32[24,256]{1,0:T(8,128)S(1)} %get-tuple-element.26), channel_id=1, source_target_pairs={{16,22},{17,23},{18,24},{19,25},{20,26},{21,27},{22,28},{23,29},{2... | collective-permute-start | bytes 73736 | tf_op jit(solution)/shard_map/ppermute | solution.py:395
  30.0 0.0 collective-permute-done.8.p2
  30.0 0.9 %collective-permute-start.9 = (f32[72,256]{1,0:T(8,128)S(1)}, f32[72,256]{1,0:T(8,128)S(1)}, u32[]{:S(2)}, u32[]{:S(2)}) collective-permute-start(f32[72,256]{1,0:T(8,128)S(1)} %shard_map.70), channel_id=1, source_target_pairs={{0,16},{16,0},{1,17},{17,1},{2,18},{18,2},{3,19},{19,3},{4,20},{20... | collective-permute-start | bytes 221192 | tf_op jit(solution)/shard_map/ppermute | solution.py:360
  30.9 2.4 %shard_map.65.inverse = f32[16,256]{1,0:T(8,128)S(1)} custom-call(f32[288,256]{1,0:T(8,128)S(1)} %get-tuple-element.17.pack), custom_call_target="tpu_custom_call" | custom-call | flops 1000000000 | tf_op jit(solution)/shard_map/pallas_call | solution.py:23
  33.4 0.0 collective-permute-done.12.p3
  33.4 0.0 collective-permute-done.13.p4
  33.4 0.0 collective-permute-done.11.sixth
  33.4 0.1 collective-permute-done.10.fifth
  33.5 0.0 collective-permute-done.9.near
  33.5 4.6 %shard_map.71 = (f32[16,256]{1,0:T(8,128)S(1)}, f32[16,256]{1,0:T(8,128)S(1)}) custom-call(f32[288,256]{1,0:T(8,128)S(1)} %get-tuple-element.17.pack, f32[288,256]{1,0:T(8,128)S(1)} %collective-permute-done.other, f32[16,256]{1,0:T(8,128)S(1)} %shard_map.65.inverse, f32[48,256]{1,0:T(8,128)S(1)} %get-tuple-element.24.own, ...), custom_call_target="tpu_custom_call" | custom-call | tf_op jit(solution)/shard_map/pallas_call | solution.py:23
  38.1 0.8 %collective-permute-start.14 = (f32[16,256]{1,0:T(8,128)S(1)}, f32[16,256]{1,0:T(8,128)S(1)}, u32[]{:S(2)}, u32[]{:S(2)}) collective-permute-start(f32[16,256]{1,0:T(8,128)S(1)} %get-tuple-element.28), channel_id=1, source_target_pairs={{0,16},{16,0},{1,17},{17,1},{2,18},{18,2},{3,19},{19,3},{4,20},{20... | collective-permute-start | bytes 49160 | tf_op jit(solution)/shard_map/ppermute | solution.py:360
  38.8 0.8 %collective-permute-done.14 = f32[16,256]{1,0:T(8,128)S(1)} collective-permute-done((f32[16,256]{1,0:T(8,128)S(1)}, f32[16,256]{1,0:T(8,128)S(1)}, u32[]{:S(2)}, u32[]{:S(2)}) %collective-permute-start.14) | collective-permute-done | bytes 16416 | tf_op jit(solution)/shard_map/ppermute | solution.py:360
  39.7 0.6 %add_bitcast_fusion = f32[1,16,256]{2,1,0:T(8,128)} fusion(f32[16,256]{1,0:T(8,128)S(1)} %get-tuple-element.27, f32[16,256]{1,0:T(8,128)S(1)} %collective-permute-done.14, f32[16,256]{1,0:T(8,128)S(1)} %shard_map.65.inverse), kind=kLoop, calls=%fused_computation | loop fusion | flops 8192 | bytes 65536 | tf_op jit(solution)/shard_map/broadcast_in_dim | solution.py:403
  (3 shorter events, 0.0 us)
Async XLA Ops:
  1.2 1.7 %collective-permute-start = (f32[288,256]{1,0:T(8,128)S(1)}, f32[288,256]{1,0:T(8,128)S(1)}, u32[]{:S(2)}, u32[]{:S(2)}) collective-permute-start(f32[288,256]{1,0:T(8,128)S(1)} %get-tuple-element.17.pack), channel_id=1, source_target_pairs={{0,16},{16,0},{1,17},{17,1},{2,18},{18,2},{3,19},{19,3},{4,20},{20... | collective-permute-start | bytes 884744 | tf_op jit(solution)/shard_map/ppermute | solution.py:360
  2.9 14.9 %collective-permute-start.3 = (f32[120,256]{1,0:T(8,128)S(1)}, f32[120,256]{1,0:T(8,128)S(1)}, u32[]{:S(2)}, u32[]{:S(2)}) collective-permute-start(f32[120,256]{1,0:T(8,128)S(1)} %get-tuple-element.21.own), channel_id=1, source_target_pairs={{2,0},{3,1},{4,2},{5,3},{6,4},{7,5},{8,6},{9,7},{10,8},{11,9},{12,... | collective-permute-start | bytes 368648 | tf_op jit(solution)/shard_map/ppermute | solution.py:365
  8.9 8.8 %collective-permute-start.2 = (f32[120,256]{1,0:T(8,128)S(1)}, f32[120,256]{1,0:T(8,128)S(1)}, u32[]{:S(2)}, u32[]{:S(2)}) collective-permute-start(f32[120,256]{1,0:T(8,128)S(1)} %get-tuple-element.20), channel_id=1, source_target_pairs={{1,0},{2,1},{3,2},{4,3},{5,4},{6,5},{7,6},{8,7},{9,8},{10,9},{11,1... | collective-permute-start | bytes 368648 | tf_op jit(solution)/shard_map/ppermute | solution.py:365
  10.4 7.4 %collective-permute-start.4 = (f32[120,256]{1,0:T(8,128)S(1)}, f32[120,256]{1,0:T(8,128)S(1)}, u32[]{:S(2)}, u32[]{:S(2)}) collective-permute-start(f32[120,256]{1,0:T(8,128)S(1)} %get-tuple-element.22), channel_id=1, source_target_pairs={{3,0},{4,1},{5,2},{6,3},{7,4},{8,5},{9,6},{10,7},{11,8},{12,9},{13... | collective-permute-start | bytes 368648 | tf_op jit(solution)/shard_map/ppermute | solution.py:365
  10.9 6.8 %collective-permute-start.1 = (f32[8,256]{1,0:T(8,128)S(1)}, f32[8,256]{1,0:T(8,128)S(1)}, u32[]{:S(2)}, u32[]{:S(2)}) collective-permute-start(f32[8,256]{1,0:T(8,128)S(1)} %get-tuple-element.19), channel_id=1, source_target_pairs={{5,0},{6,1},{7,2},{8,3},{9,4},{10,5},{11,6},{12,7},{13,8},{14,9},{... | collective-permute-start | bytes 24584 | tf_op jit(solution)/shard_map/ppermute | solution.py:365
  12.2 5.6 %collective-permute-start.5 = (f32[88,256]{1,0:T(8,128)S(1)}, f32[88,256]{1,0:T(8,128)S(1)}, u32[]{:S(2)}, u32[]{:S(2)}) collective-permute-start(f32[88,256]{1,0:T(8,128)S(1)} %get-tuple-element.23), channel_id=1, source_target_pairs={{4,0},{5,1},{6,2},{7,3},{8,4},{9,5},{10,6},{11,7},{12,8},{13,9},{1... | collective-permute-start | bytes 270344 | tf_op jit(solution)/shard_map/ppermute | solution.py:365
  19.9 1.2 %collective-permute-start.6 = (f32[16,256]{1,0:T(8,128)S(1)}, f32[16,256]{1,0:T(8,128)S(1)}, u32[]{:S(2)}, u32[]{:S(2)}) collective-permute-start(f32[16,256]{1,0:T(8,128)S(1)} %shard_map.68.partial), channel_id=1, source_target_pairs={{0,16},{16,0},{1,17},{17,1},{2,18},{18,2},{3,19},{19,3},{4,20},{20... | collective-permute-start | bytes 49160 | tf_op jit(solution)/shard_map/ppermute | solution.py:360
  21.1 8.2 %collective-permute-start.7 = (f32[16,256]{1,0:T(8,128)S(1)}, f32[16,256]{1,0:T(8,128)S(1)}, u32[]{:S(2)}, u32[]{:S(2)}) collective-permute-start(f32[16,256]{1,0:T(8,128)S(1)} %get-tuple-element.25), channel_id=1, source_target_pairs={{1,0},{2,1},{3,2},{4,3},{5,4},{6,5},{7,6},{8,7},{9,8},{10,9},{11,1... | collective-permute-start | bytes 49160 | tf_op jit(solution)/shard_map/ppermute | solution.py:365
  23.3 6.7 %collective-permute-start.8 = (f32[16,256]{1,0:T(8,128)S(1)}, f32[16,256]{1,0:T(8,128)S(1)}, u32[]{:S(2)}, u32[]{:S(2)}) collective-permute-start(f32[16,256]{1,0:T(8,128)S(1)} %get-tuple-element.25), channel_id=1, source_target_pairs={{2,0},{3,1},{4,2},{5,3},{6,4},{7,5},{8,6},{9,7},{10,8},{11,9},{12,... | collective-permute-start | bytes 49160 | tf_op jit(solution)/shard_map/ppermute | solution.py:365
  25.3 8.1 %collective-permute-start.12 = (f32[16,256]{1,0:T(8,128)S(1)}, f32[16,256]{1,0:T(8,128)S(1)}, u32[]{:S(2)}, u32[]{:S(2)}) collective-permute-start(f32[16,256]{1,0:T(8,128)S(1)} %get-tuple-element.25), channel_id=1, source_target_pairs={{3,0},{4,1},{5,2},{6,3},{7,4},{8,5},{9,6},{10,7},{11,8},{12,9},{13... | collective-permute-start | bytes 49160 | tf_op jit(solution)/shard_map/ppermute | solution.py:365
  27.5 5.9 %collective-permute-start.13 = (f32[16,256]{1,0:T(8,128)S(1)}, f32[16,256]{1,0:T(8,128)S(1)}, u32[]{:S(2)}, u32[]{:S(2)}) collective-permute-start(f32[16,256]{1,0:T(8,128)S(1)} %get-tuple-element.25), channel_id=1, source_target_pairs={{4,0},{5,1},{6,2},{7,3},{8,4},{9,5},{10,6},{11,7},{12,8},{13,9},{1... | collective-permute-start | bytes 49160 | tf_op jit(solution)/shard_map/ppermute | solution.py:365
  27.9 5.5 %collective-permute-start.10 = (f32[48,256]{1,0:T(8,128)S(1)}, f32[48,256]{1,0:T(8,128)S(1)}, u32[]{:S(2)}, u32[]{:S(2)}) collective-permute-start(f32[48,256]{1,0:T(8,128)S(1)} %get-tuple-element.24.own), channel_id=1, source_target_pairs={{5,0},{6,1},{7,2},{8,3},{9,4},{10,5},{11,6},{12,7},{13,8},{14,9},{... | collective-permute-start | bytes 147464 | tf_op jit(solution)/shard_map/ppermute | solution.py:365
  29.3 4.1 %collective-permute-start.11 = (f32[24,256]{1,0:T(8,128)S(1)}, f32[24,256]{1,0:T(8,128)S(1)}, u32[]{:S(2)}, u32[]{:S(2)}) collective-permute-start(f32[24,256]{1,0:T(8,128)S(1)} %get-tuple-element.26), channel_id=1, source_target_pairs={{16,22},{17,23},{18,24},{19,25},{20,26},{21,27},{22,28},{23,29},{2... | collective-permute-start | bytes 73736 | tf_op jit(solution)/shard_map/ppermute | solution.py:395
  30.0 3.5 %collective-permute-start.9 = (f32[72,256]{1,0:T(8,128)S(1)}, f32[72,256]{1,0:T(8,128)S(1)}, u32[]{:S(2)}, u32[]{:S(2)}) collective-permute-start(f32[72,256]{1,0:T(8,128)S(1)} %shard_map.70), channel_id=1, source_target_pairs={{0,16},{16,0},{1,17},{17,1},{2,18},{18,2},{3,19},{19,3},{4,20},{20... | collective-permute-start | bytes 221192 | tf_op jit(solution)/shard_map/ppermute | solution.py:360
  38.1 1.6 %collective-permute-start.14 = (f32[16,256]{1,0:T(8,128)S(1)}, f32[16,256]{1,0:T(8,128)S(1)}, u32[]{:S(2)}, u32[]{:S(2)}) collective-permute-start(f32[16,256]{1,0:T(8,128)S(1)} %get-tuple-element.28), channel_id=1, source_target_pairs={{0,16},{16,0},{1,17},{17,1},{2,18},{18,2},{3,19},{19,3},{4,20},{20... | collective-permute-start | bytes 49160 | tf_op jit(solution)/shard_map/ppermute | solution.py:360

commit v4 on v3

--- a/solution.py
+++ b/solution.py
@@ -120,12 +120,49 @@
         first.start()
         pack[128:256, :] = jnp.zeros((128, pack.shape[1]), F32)
         first.wait()
+        ints[...] = renumbered(ints[...])
         fold(ints, pack, 0)
 
     on_each_component(atmosphere, ocean)
     for copy in copies:
         copy.wait()
-    code[...] = codes[...].astype(F32)
+    code[...] = halved(codes[...].astype(F32))
+
+    @pl.when(lax.axis_index("comp") != 0)
+    def _():
+        pack[256:272, :] = halved(pack[256:272, :])
+        pack[272:288, :] = halved(pack[272:288, :])
+
+
+def halved(x):
+    width = x.shape[1] // 2
+    a, b = x[:, :width], x[:, width:]
+    lane = lax.broadcasted_iota(I32, a.shape, 1)
+
+    def picked(odd):
+        index = ((2 * lane) & (width - 1)) + odd
+        first = jnp.take_along_axis(a, index, axis=1, mode="promise_in_bounds")
+        second = jnp.take_along_axis(b, index, axis=1, mode="promise_in_bounds")
+        return jnp.where(lane < width // 2, first, second)
+
+    return jnp.concatenate([picked(0), picked(1)], 1)
+
+
+def unhalved(a, b):
+    lane = lax.broadcasted_iota(I32, a.shape, 1)
+    width = a.shape[1]
+
+    def picked(first):
+        index = lax.shift_right_logical(lane, 1) + first
+        even = jnp.take_along_axis(a, index, axis=1, mode="promise_in_bounds")
+        odd = jnp.take_along_axis(b, index, axis=1, mode="promise_in_bounds")
+        return jnp.where((lane & 1) == 0, even, odd)
+
+    return jnp.concatenate([picked(0), picked(width // 2)], 1)
+
+
+def renumbered(cell):
+    return (cell & ~255) + lax.shift_left(cell & 1, 7) + lax.shift_right_logical(cell & 255, 1)
 
 
 def block_of(ref, k):
@@ -242,7 +279,7 @@
 
 def trace_kernel(
     pack, other, inverse, own, near, fifth, sixth, p1, p2, p3, p4, m1, m2, m3, m4,
-    send, keep, rhs, inv, code, code_up, code_down, eta,
+    send, keep, rhs, inv, code, code_up, code_down, even, odd,
 ):
     rows, width = rhs.shape
     groups = rows // 8
@@ -276,10 +313,10 @@
         return ref[8 * g : 8 * g + 8, :]
 
     def from_above(here, above):
-        return jnp.where(line == 0, above, here)
+        return jnp.where(line[:, : here.shape[1]] == 0, above, here)
 
     def from_below(here, below):
-        return jnp.where(line == 7, below, here)
+        return jnp.where(line[:, : here.shape[1]] == 7, below, here)
 
     downward = [pltpu.roll(group(code, g), 1, 0) for g in range(groups)]
     for g in range(groups):
@@ -287,26 +324,37 @@
     upward = [pltpu.roll(group(code, g), 7, 0) for g in range(groups)]
     for g in range(groups):
         code_up[8 * g : 8 * g + 8, :] = from_below(upward[g], upward[min(g + 1, groups - 1)])
+    half = width // 2
     for g in range(groups):
-        eta[8 * g : 8 * g + 8, :] = group(rhs, g) * group(inv, g)
+        first = group(rhs, g) * group(inv, g)
+        even[8 * g : 8 * g + 8, :] = first[:, :half]
+        odd[8 * g : 8 * g + 8, :] = first[:, half:]
 
     def sweep(first, last):
         beside, above, below = {}, {}, {}
 
+        def chosen(code, zero, left, here, right):
+            return jnp.where(code == zero, left, jnp.where(code == zero + 1.0, here, right))
+
         def read(g):
-            here = group(eta, g)
-            left = pltpu.roll(here, 1, 1)
-            right = pltpu.roll(here, width - 1, 1)
-            beside[g] = left + right
+            e, o = group(even, g), group(odd, g)
+            left = pltpu.roll(o, 1, 1)
+            right = pltpu.roll(e, half - 1, 1)
+            beside[g] = left + o, e + right
             u, d = group(code_up, g), group(code_down, g)
-            above[g] = pltpu.roll(jnp.where(u == 0.0, left, jnp.where(u == 1.0, here, right)), 1, 0)
-            below[g] = pltpu.roll(jnp.where(d == 3.0, left, jnp.where(d == 4.0, here, right)), 7, 0)
+            up = (chosen(u[:, :half], 0.0, left, e, o), chosen(u[:, half:], 0.0, e, o, right))
+            down = (chosen(d[:, :half], 3.0, left, e, o), chosen(d[:, half:], 3.0, e, o, right))
+            above[g] = [pltpu.roll(x, 1, 0) for x in up]
+            below[g] = [pltpu.roll(x, 7, 0) for x in down]
 
         def write(g):
-            up = from_above(above[g], above[max(g - 1, first)])
-            down = from_below(below[g], below[min(g + 1, last - 1)])
-            third = jnp.where(group(code, g) >= 3.0, down, up)
-            eta[8 * g : 8 * g + 8, :] = (group(rhs, g) + (beside[g] + third)) * group(inv, g)
+            for k, ref in enumerate((even, odd)):
+                lanes = slice(k * half, k * half + half)
+                up = from_above(above[g][k], above[max(g - 1, first)][k])
+                down = from_below(below[g][k], below[min(g + 1, last - 1)][k])
+                third = jnp.where(group(code, g)[:, lanes] >= 3.0, down, up)
+                total = group(rhs, g)[:, lanes] + (beside[g][k] + third)
+                ref[8 * g : 8 * g + 8, :] = total * group(inv, g)[:, lanes]
 
         for g in range(first, last):
             read(g)
@@ -316,14 +364,14 @@
 
     def repeat(count, skip):
         def several(_, carry):
-            for _ in range(4):
+            for _ in range(8):
                 sweep(skip, groups - skip)
             return carry
 
-        for _ in range(count % 4):
+        for _ in range(count % 8):
             sweep(skip, groups - skip)
-        if count >= 4:
-            lax.fori_loop(0, count // 4, several, 0)
+        if count >= 8:
+            lax.fori_loop(0, count // 8, several, 0)
 
     done = 1
     for skip in range(3):
@@ -341,13 +389,14 @@
     total = jnp.zeros((128, 64), F32)
     for i in range(4):
         at = 24 + 16 * i
-        sst = 1.25 * sea[i] + 0.5 * eta[at : at + 16, :] - 0.25 * rhs[at : at + 16, :]
+        eta = jnp.concatenate([even[at : at + 16, :], odd[at : at + 16, :]], 1)
+        sst = 1.25 * sea[i] + 0.5 * eta - 0.25 * rhs[at : at + 16, :]
         picked = gather_cells(sst, slots[i].astype(I32))
         cell = jnp.where(atmosphere, block_of(pack, 4 + i), block_of(other, i)).astype(I32)
         weight = jnp.where(atmosphere, block_of(pack, 12 + i), block_of(other, 8 + i))
         total = scatter_add(total, weight * picked, cell)
     part = as_rows(total)
-    send[...] = jnp.where(atmosphere, eta[24:40, :], part)
+    send[...] = jnp.where(atmosphere, unhalved(even[24:40, :], odd[24:40, :]), part)
     keep[...] = jnp.where(atmosphere, part * inverse[...], 0.0)
 
 
@@ -398,7 +447,8 @@
     send, keep = call(
         trace_kernel, [block, block],
         pack, other, inverse, fifth, swap(near), fifth_in, sixth_in, p1_in, p2_in, p3_in, p4_in, *messages_in,
-        scratch=[pltpu.VMEM(window, F32)] * 6,
+        scratch=[pltpu.VMEM(window, F32)] * 5
+        + [pltpu.VMEM((window[0], width // 2), F32)] * 2,
     )
     return (keep + swap(send) * inverse)[None]
 

time: 40.6 us -> 39.8 us (0.980)
  Pallas kernels: 10.4 us -> 9.59 us
    pallas_call x8, Pallas kernels: 10.4 us -> 9.59 us  [call(): pl.pallas_call(kernel, out_shape=out, in_specs=[pl.BlockSpec(memory_space...]
where the time goes in v4:
time: 39.8 us; the launch traced here: 39.5 us
  starting transfers between devices  21.6 us (54%)
  Pallas kernels  9.59 us (24%)
  waiting for transfers between devices  7.54 us (19%)
  other arithmetic  0.61 us (2%)
    ppermute x10, starting transfers between devices, move(): return lax.ppermute(x, GRID, pairs)  18.8 us
    pallas_call x8, Pallas kernels, call(): pl.pallas_call(kernel, out_shape=out, in_specs=[pl.BlockSpec(memory_space...  9.59 us
    ppermute x10, waiting for transfers between devices, move(): return lax.ppermute(x, GRID, pairs)  4.32 us
    ppermute x4, waiting for transfers between devices, swap(): return lax.ppermute(x, 'comp', [(0, 1), (1, 0)])  3.22 us
    ppermute x4, starting transfers between devices, swap(): return lax.ppermute(x, 'comp', [(0, 1), (1, 0)])  2.22 us
  transfers between devices with their start and end apart: 15, of which 6 were waited for; matrix products, arithmetic and copies ran while one was open for 0% of the time, Pallas kernels for 6%

profile of v4, /device:TPU:0, one launch (start us, length us, event | category | flops | bytes accessed | tf_op | source)
XLA Modules:
  0.0 39.5 jit_solution(2921822367283132538)
XLA Ops:
  0.0 1.2 %shard_map.64 = (f32[288,256]{1,0:T(8,128)S(1)}, f32[16,256]{1,0:T(8,128)S(1)}) custom-call(s32[8,4096]{1,0:T(8,128)} %cells.1, f32[8,4096]{1,0:T(8,128)} %weights.1, s32[8,4096]{1,0:T(8,128)} %slots.1, f32[1,16,256]{2,1,0:T(8,128)} %state.1, f32[1,16,256]{2,1,0:T(8,128)} %coeff.1, s32[16,256]{1,0:T(8,128)} %vertical.1), custom_call_target="tpu_custom_call" | custom-call | tf_op jit(solution)/shard_map/pallas_call | solution.py:23
  1.2 0.5 %collective-permute-start = (f32[288,256]{1,0:T(8,128)S(1)}, f32[288,256]{1,0:T(8,128)S(1)}, u32[]{:S(2)}, u32[]{:S(2)}) collective-permute-start(f32[288,256]{1,0:T(8,128)S(1)} %get-tuple-element.17.pack), channel_id=1, source_target_pairs={{0,16},{16,0},{1,17},{17,1},{2,18},{18,2},{3,19},{19,3},{4,20},{20... | collective-permute-start | bytes 884744 | tf_op jit(solution)/shard_map/ppermute | solution.py:409
  1.7 1.2 %collective-permute-done.other = f32[288,256]{1,0:T(8,128)S(1)} collective-permute-done((f32[288,256]{1,0:T(8,128)S(1)}, f32[288,256]{1,0:T(8,128)S(1)}, u32[]{:S(2)}, u32[]{:S(2)}) %collective-permute-start) | collective-permute-done | bytes 294944 | tf_op jit(solution)/shard_map/ppermute | solution.py:409
  3.0 0.1 shard_map.66
  3.0 6.0 %collective-permute-start.3 = (f32[120,256]{1,0:T(8,128)S(1)}, f32[120,256]{1,0:T(8,128)S(1)}, u32[]{:S(2)}, u32[]{:S(2)}) collective-permute-start(f32[120,256]{1,0:T(8,128)S(1)} %get-tuple-element.21.own), channel_id=1, source_target_pairs={{2,0},{3,1},{4,2},{5,3},{6,4},{7,5},{8,6},{9,7},{10,8},{11,9},{12,... | collective-permute-start | bytes 368648 | tf_op jit(solution)/shard_map/ppermute | solution.py:414
  9.0 1.4 %collective-permute-start.2 = (f32[120,256]{1,0:T(8,128)S(1)}, f32[120,256]{1,0:T(8,128)S(1)}, u32[]{:S(2)}, u32[]{:S(2)}) collective-permute-start(f32[120,256]{1,0:T(8,128)S(1)} %get-tuple-element.20), channel_id=1, source_target_pairs={{1,0},{2,1},{3,2},{4,3},{5,4},{6,5},{7,6},{8,7},{9,8},{10,9},{11,1... | collective-permute-start | bytes 368648 | tf_op jit(solution)/shard_map/ppermute | solution.py:414
  10.5 0.5 %collective-permute-start.4 = (f32[120,256]{1,0:T(8,128)S(1)}, f32[120,256]{1,0:T(8,128)S(1)}, u32[]{:S(2)}, u32[]{:S(2)}) collective-permute-start(f32[120,256]{1,0:T(8,128)S(1)} %get-tuple-element.22), channel_id=1, source_target_pairs={{3,0},{4,1},{5,2},{6,3},{7,4},{8,5},{9,6},{10,7},{11,8},{12,9},{13... | collective-permute-start | bytes 368648 | tf_op jit(solution)/shard_map/ppermute | solution.py:414
  10.9 1.3 %collective-permute-start.1 = (f32[8,256]{1,0:T(8,128)S(1)}, f32[8,256]{1,0:T(8,128)S(1)}, u32[]{:S(2)}, u32[]{:S(2)}) collective-permute-start(f32[8,256]{1,0:T(8,128)S(1)} %get-tuple-element.19), channel_id=1, source_target_pairs={{5,0},{6,1},{7,2},{8,3},{9,4},{10,5},{11,6},{12,7},{13,8},{14,9},{... | collective-permute-start | bytes 24584 | tf_op jit(solution)/shard_map/ppermute | solution.py:414
  12.3 1.3 %collective-permute-start.5 = (f32[88,256]{1,0:T(8,128)S(1)}, f32[88,256]{1,0:T(8,128)S(1)}, u32[]{:S(2)}, u32[]{:S(2)}) collective-permute-start(f32[88,256]{1,0:T(8,128)S(1)} %get-tuple-element.23), channel_id=1, source_target_pairs={{4,0},{5,1},{6,2},{7,3},{8,4},{9,5},{10,6},{11,7},{12,8},{13,9},{1... | collective-permute-start | bytes 270344 | tf_op jit(solution)/shard_map/ppermute | solution.py:414
  13.6 4.1 %collective-permute-done.1.edge = f32[8,256]{1,0:T(8,128)S(1)} collective-permute-done((f32[8,256]{1,0:T(8,128)S(1)}, f32[8,256]{1,0:T(8,128)S(1)}, u32[]{:S(2)}, u32[]{:S(2)}) %collective-permute-start.1) | collective-permute-done | bytes 8224 | tf_op jit(solution)/shard_map/ppermute | solution.py:414
  17.7 0.1 collective-permute-done.5.m4
  17.8 0.0 collective-permute-done.3.m2
  17.8 0.0 collective-permute-done.2.m1
  17.9 0.0 collective-permute-done.4.m3
  17.9 2.1 %shard_map.68.partial = f32[16,256]{1,0:T(8,128)S(1)} custom-call(f32[8,256]{1,0:T(8,128)S(1)} %shard_map.67.edge, f32[120,256]{1,0:T(8,128)S(1)} %collective-permute-done.2.m1, f32[120,256]{1,0:T(8,128)S(1)} %collective-permute-done.3.m2, f32[120,256]{1,0:T(8,128)S(1)} %collective-permute-done.4.m3, f32[88,256]{1,0:T(8,128)S(1)} %collective-permute-done.5.m4, ...), custom_call_target="tpu_custom_call" | custom-call | flops 1000000000 | tf_op jit(solution)/shard_map/pallas_call | solution.py:23
  20.0 0.0 collective-permute-start.6
  20.0 1.2 %collective-permute-done.6.partial_sw = f32[16,256]{1,0:T(8,128)S(1)} collective-permute-done((f32[16,256]{1,0:T(8,128)S(1)}, f32[16,256]{1,0:T(8,128)S(1)}, u32[]{:S(2)}, u32[]{:S(2)}) %collective-permute-start.6) | collective-permute-done | bytes 16416 | tf_op jit(solution)/shard_map/ppermute | solution.py:409
  21.2 2.2 %collective-permute-start.7 = (f32[16,256]{1,0:T(8,128)S(1)}, f32[16,256]{1,0:T(8,128)S(1)}, u32[]{:S(2)}, u32[]{:S(2)}) collective-permute-start(f32[16,256]{1,0:T(8,128)S(1)} %get-tuple-element.25), channel_id=1, source_target_pairs={{1,0},{2,1},{3,2},{4,3},{5,4},{6,5},{7,6},{8,7},{9,8},{10,9},{11,1... | collective-permute-start | bytes 49160 | tf_op jit(solution)/shard_map/ppermute | solution.py:414
  23.4 2.0 %collective-permute-start.8 = (f32[16,256]{1,0:T(8,128)S(1)}, f32[16,256]{1,0:T(8,128)S(1)}, u32[]{:S(2)}, u32[]{:S(2)}) collective-permute-start(f32[16,256]{1,0:T(8,128)S(1)} %get-tuple-element.25), channel_id=1, source_target_pairs={{2,0},{3,1},{4,2},{5,3},{6,4},{7,5},{8,6},{9,7},{10,8},{11,9},{12,... | collective-permute-start | bytes 49160 | tf_op jit(solution)/shard_map/ppermute | solution.py:414
  25.4 2.2 %collective-permute-start.12 = (f32[16,256]{1,0:T(8,128)S(1)}, f32[16,256]{1,0:T(8,128)S(1)}, u32[]{:S(2)}, u32[]{:S(2)}) collective-permute-start(f32[16,256]{1,0:T(8,128)S(1)} %get-tuple-element.25), channel_id=1, source_target_pairs={{3,0},{4,1},{5,2},{6,3},{7,4},{8,5},{9,6},{10,7},{11,8},{12,9},{13... | collective-permute-start | bytes 49160 | tf_op jit(solution)/shard_map/ppermute | solution.py:414
  27.6 0.5 %collective-permute-start.13 = (f32[16,256]{1,0:T(8,128)S(1)}, f32[16,256]{1,0:T(8,128)S(1)}, u32[]{:S(2)}, u32[]{:S(2)}) collective-permute-start(f32[16,256]{1,0:T(8,128)S(1)} %get-tuple-element.25), channel_id=1, source_target_pairs={{4,0},{5,1},{6,2},{7,3},{8,4},{9,5},{10,6},{11,7},{12,8},{13,9},{1... | collective-permute-start | bytes 49160 | tf_op jit(solution)/shard_map/ppermute | solution.py:414
  28.0 1.4 %collective-permute-start.10 = (f32[48,256]{1,0:T(8,128)S(1)}, f32[48,256]{1,0:T(8,128)S(1)}, u32[]{:S(2)}, u32[]{:S(2)}) collective-permute-start(f32[48,256]{1,0:T(8,128)S(1)} %get-tuple-element.24.own), channel_id=1, source_target_pairs={{5,0},{6,1},{7,2},{8,3},{9,4},{10,5},{11,6},{12,7},{13,8},{14,9},{... | collective-permute-start | bytes 147464 | tf_op jit(solution)/shard_map/ppermute | solution.py:414
  29.4 0.0 collective-permute-done.7.p1
  29.4 0.7 %collective-permute-start.11 = (f32[24,256]{1,0:T(8,128)S(1)}, f32[24,256]{1,0:T(8,128)S(1)}, u32[]{:S(2)}, u32[]{:S(2)}) collective-permute-start(f32[24,256]{1,0:T(8,128)S(1)} %get-tuple-element.26), channel_id=1, source_target_pairs={{16,22},{17,23},{18,24},{19,25},{20,26},{21,27},{22,28},{23,29},{2... | collective-permute-start | bytes 73736 | tf_op jit(solution)/shard_map/ppermute | solution.py:444
  30.1 0.0 collective-permute-done.8.p2
  30.1 0.9 %collective-permute-start.9 = (f32[72,256]{1,0:T(8,128)S(1)}, f32[72,256]{1,0:T(8,128)S(1)}, u32[]{:S(2)}, u32[]{:S(2)}) collective-permute-start(f32[72,256]{1,0:T(8,128)S(1)} %shard_map.70), channel_id=1, source_target_pairs={{0,16},{16,0},{1,17},{17,1},{2,18},{18,2},{3,19},{19,3},{4,20},{20... | collective-permute-start | bytes 221192 | tf_op jit(solution)/shard_map/ppermute | solution.py:409
  31.0 2.4 %shard_map.65.inverse = f32[16,256]{1,0:T(8,128)S(1)} custom-call(f32[288,256]{1,0:T(8,128)S(1)} %get-tuple-element.17.pack), custom_call_target="tpu_custom_call" | custom-call | flops 1000000000 | tf_op jit(solution)/shard_map/pallas_call | solution.py:23
  33.4 0.0 collective-permute-done.12.p3
  33.5 0.0 collective-permute-done.13.p4
  33.5 0.0 collective-permute-done.11.sixth
  33.5 0.1 collective-permute-done.10.fifth
  33.5 0.0 collective-permute-done.9.near
  33.5 3.7 %shard_map.71 = (f32[16,256]{1,0:T(8,128)S(1)}, f32[16,256]{1,0:T(8,128)S(1)}) custom-call(f32[288,256]{1,0:T(8,128)S(1)} %get-tuple-element.17.pack, f32[288,256]{1,0:T(8,128)S(1)} %collective-permute-done.other, f32[16,256]{1,0:T(8,128)S(1)} %shard_map.65.inverse, f32[48,256]{1,0:T(8,128)S(1)} %get-tuple-element.24.own, ...), custom_call_target="tpu_custom_call" | custom-call | tf_op jit(solution)/shard_map/pallas_call | solution.py:23
  37.3 0.8 %collective-permute-start.14 = (f32[16,256]{1,0:T(8,128)S(1)}, f32[16,256]{1,0:T(8,128)S(1)}, u32[]{:S(2)}, u32[]{:S(2)}) collective-permute-start(f32[16,256]{1,0:T(8,128)S(1)} %get-tuple-element.28), channel_id=1, source_target_pairs={{0,16},{16,0},{1,17},{17,1},{2,18},{18,2},{3,19},{19,3},{4,20},{20... | collective-permute-start | bytes 49160 | tf_op jit(solution)/shard_map/ppermute | solution.py:409
  38.0 0.8 %collective-permute-done.14 = f32[16,256]{1,0:T(8,128)S(1)} collective-permute-done((f32[16,256]{1,0:T(8,128)S(1)}, f32[16,256]{1,0:T(8,128)S(1)}, u32[]{:S(2)}, u32[]{:S(2)}) %collective-permute-start.14) | collective-permute-done | bytes 16416 | tf_op jit(solution)/shard_map/ppermute | solution.py:409
  38.9 0.6 %add_bitcast_fusion = f32[1,16,256]{2,1,0:T(8,128)} fusion(f32[16,256]{1,0:T(8,128)S(1)} %get-tuple-element.27, f32[16,256]{1,0:T(8,128)S(1)} %collective-permute-done.14, f32[16,256]{1,0:T(8,128)S(1)} %shard_map.65.inverse), kind=kLoop, calls=%fused_computation | loop fusion | flops 8192 | bytes 65536 | tf_op jit(solution)/shard_map/broadcast_in_dim | solution.py:453
  (3 shorter events, 0.0 us)
Async XLA Ops:
  1.2 1.7 %collective-permute-start = (f32[288,256]{1,0:T(8,128)S(1)}, f32[288,256]{1,0:T(8,128)S(1)}, u32[]{:S(2)}, u32[]{:S(2)}) collective-permute-start(f32[288,256]{1,0:T(8,128)S(1)} %get-tuple-element.17.pack), channel_id=1, source_target_pairs={{0,16},{16,0},{1,17},{17,1},{2,18},{18,2},{3,19},{19,3},{4,20},{20... | collective-permute-start | bytes 884744 | tf_op jit(solution)/shard_map/ppermute | solution.py:409
  3.0 14.8 %collective-permute-start.3 = (f32[120,256]{1,0:T(8,128)S(1)}, f32[120,256]{1,0:T(8,128)S(1)}, u32[]{:S(2)}, u32[]{:S(2)}) collective-permute-start(f32[120,256]{1,0:T(8,128)S(1)} %get-tuple-element.21.own), channel_id=1, source_target_pairs={{2,0},{3,1},{4,2},{5,3},{6,4},{7,5},{8,6},{9,7},{10,8},{11,9},{12,... | collective-permute-start | bytes 368648 | tf_op jit(solution)/shard_map/ppermute | solution.py:414
  9.0 8.8 %collective-permute-start.2 = (f32[120,256]{1,0:T(8,128)S(1)}, f32[120,256]{1,0:T(8,128)S(1)}, u32[]{:S(2)}, u32[]{:S(2)}) collective-permute-start(f32[120,256]{1,0:T(8,128)S(1)} %get-tuple-element.20), channel_id=1, source_target_pairs={{1,0},{2,1},{3,2},{4,3},{5,4},{6,5},{7,6},{8,7},{9,8},{10,9},{11,1... | collective-permute-start | bytes 368648 | tf_op jit(solution)/shard_map/ppermute | solution.py:414
  10.5 7.4 %collective-permute-start.4 = (f32[120,256]{1,0:T(8,128)S(1)}, f32[120,256]{1,0:T(8,128)S(1)}, u32[]{:S(2)}, u32[]{:S(2)}) collective-permute-start(f32[120,256]{1,0:T(8,128)S(1)} %get-tuple-element.22), channel_id=1, source_target_pairs={{3,0},{4,1},{5,2},{6,3},{7,4},{8,5},{9,6},{10,7},{11,8},{12,9},{13... | collective-permute-start | bytes 368648 | tf_op jit(solution)/shard_map/ppermute | solution.py:414
  10.9 6.8 %collective-permute-start.1 = (f32[8,256]{1,0:T(8,128)S(1)}, f32[8,256]{1,0:T(8,128)S(1)}, u32[]{:S(2)}, u32[]{:S(2)}) collective-permute-start(f32[8,256]{1,0:T(8,128)S(1)} %get-tuple-element.19), channel_id=1, source_target_pairs={{5,0},{6,1},{7,2},{8,3},{9,4},{10,5},{11,6},{12,7},{13,8},{14,9},{... | collective-permute-start | bytes 24584 | tf_op jit(solution)/shard_map/ppermute | solution.py:414
  12.3 5.6 %collective-permute-start.5 = (f32[88,256]{1,0:T(8,128)S(1)}, f32[88,256]{1,0:T(8,128)S(1)}, u32[]{:S(2)}, u32[]{:S(2)}) collective-permute-start(f32[88,256]{1,0:T(8,128)S(1)} %get-tuple-element.23), channel_id=1, source_target_pairs={{4,0},{5,1},{6,2},{7,3},{8,4},{9,5},{10,6},{11,7},{12,8},{13,9},{1... | collective-permute-start | bytes 270344 | tf_op jit(solution)/shard_map/ppermute | solution.py:414
  20.0 1.2 %collective-permute-start.6 = (f32[16,256]{1,0:T(8,128)S(1)}, f32[16,256]{1,0:T(8,128)S(1)}, u32[]{:S(2)}, u32[]{:S(2)}) collective-permute-start(f32[16,256]{1,0:T(8,128)S(1)} %shard_map.68.partial), channel_id=1, source_target_pairs={{0,16},{16,0},{1,17},{17,1},{2,18},{18,2},{3,19},{19,3},{4,20},{20... | collective-permute-start | bytes 49160 | tf_op jit(solution)/shard_map/ppermute | solution.py:409
  21.2 8.2 %collective-permute-start.7 = (f32[16,256]{1,0:T(8,128)S(1)}, f32[16,256]{1,0:T(8,128)S(1)}, u32[]{:S(2)}, u32[]{:S(2)}) collective-permute-start(f32[16,256]{1,0:T(8,128)S(1)} %get-tuple-element.25), channel_id=1, source_target_pairs={{1,0},{2,1},{3,2},{4,3},{5,4},{6,5},{7,6},{8,7},{9,8},{10,9},{11,1... | collective-permute-start | bytes 49160 | tf_op jit(solution)/shard_map/ppermute | solution.py:414
  23.4 6.7 %collective-permute-start.8 = (f32[16,256]{1,0:T(8,128)S(1)}, f32[16,256]{1,0:T(8,128)S(1)}, u32[]{:S(2)}, u32[]{:S(2)}) collective-permute-start(f32[16,256]{1,0:T(8,128)S(1)} %get-tuple-element.25), channel_id=1, source_target_pairs={{2,0},{3,1},{4,2},{5,3},{6,4},{7,5},{8,6},{9,7},{10,8},{11,9},{12,... | collective-permute-start | bytes 49160 | tf_op jit(solution)/shard_map/ppermute | solution.py:414
  25.4 8.1 %collective-permute-start.12 = (f32[16,256]{1,0:T(8,128)S(1)}, f32[16,256]{1,0:T(8,128)S(1)}, u32[]{:S(2)}, u32[]{:S(2)}) collective-permute-start(f32[16,256]{1,0:T(8,128)S(1)} %get-tuple-element.25), channel_id=1, source_target_pairs={{3,0},{4,1},{5,2},{6,3},{7,4},{8,5},{9,6},{10,7},{11,8},{12,9},{13... | collective-permute-start | bytes 49160 | tf_op jit(solution)/shard_map/ppermute | solution.py:414
  27.6 5.9 %collective-permute-start.13 = (f32[16,256]{1,0:T(8,128)S(1)}, f32[16,256]{1,0:T(8,128)S(1)}, u32[]{:S(2)}, u32[]{:S(2)}) collective-permute-start(f32[16,256]{1,0:T(8,128)S(1)} %get-tuple-element.25), channel_id=1, source_target_pairs={{4,0},{5,1},{6,2},{7,3},{8,4},{9,5},{10,6},{11,7},{12,8},{13,9},{1... | collective-permute-start | bytes 49160 | tf_op jit(solution)/shard_map/ppermute | solution.py:414
  28.0 5.5 %collective-permute-start.10 = (f32[48,256]{1,0:T(8,128)S(1)}, f32[48,256]{1,0:T(8,128)S(1)}, u32[]{:S(2)}, u32[]{:S(2)}) collective-permute-start(f32[48,256]{1,0:T(8,128)S(1)} %get-tuple-element.24.own), channel_id=1, source_target_pairs={{5,0},{6,1},{7,2},{8,3},{9,4},{10,5},{11,6},{12,7},{13,8},{14,9},{... | collective-permute-start | bytes 147464 | tf_op jit(solution)/shard_map/ppermute | solution.py:414
  29.4 4.1 %collective-permute-start.11 = (f32[24,256]{1,0:T(8,128)S(1)}, f32[24,256]{1,0:T(8,128)S(1)}, u32[]{:S(2)}, u32[]{:S(2)}) collective-permute-start(f32[24,256]{1,0:T(8,128)S(1)} %get-tuple-element.26), channel_id=1, source_target_pairs={{16,22},{17,23},{18,24},{19,25},{20,26},{21,27},{22,28},{23,29},{2... | collective-permute-start | bytes 73736 | tf_op jit(solution)/shard_map/ppermute | solution.py:444
  30.1 3.5 %collective-permute-start.9 = (f32[72,256]{1,0:T(8,128)S(1)}, f32[72,256]{1,0:T(8,128)S(1)}, u32[]{:S(2)}, u32[]{:S(2)}) collective-permute-start(f32[72,256]{1,0:T(8,128)S(1)} %shard_map.70), channel_id=1, source_target_pairs={{0,16},{16,0},{1,17},{17,1},{2,18},{18,2},{3,19},{19,3},{4,20},{20... | collective-permute-start | bytes 221192 | tf_op jit(solution)/shard_map/ppermute | solution.py:409
  37.3 1.6 %collective-permute-start.14 = (f32[16,256]{1,0:T(8,128)S(1)}, f32[16,256]{1,0:T(8,128)S(1)}, u32[]{:S(2)}, u32[]{:S(2)}) collective-permute-start(f32[16,256]{1,0:T(8,128)S(1)} %get-tuple-element.28), channel_id=1, source_target_pairs={{0,16},{16,0},{1,17},{17,1},{2,18},{18,2},{3,19},{19,3},{4,20},{20... | collective-permute-start | bytes 49160 | tf_op jit(solution)/shard_map/ppermute | solution.py:409

commit v5 on v4

--- a/solution.py
+++ b/solution.py
@@ -37,17 +37,18 @@
     pl.when(comp != 0)(ocean)
 
 
-def fold(source, target, first):
-    width = target.shape[1]
-    lines = source.shape[1] // width
-    for row in range(SPAN):
+def fold(source, target, first, halves):
+    width = halves.shape[1]
+    rows = halves.shape[0]
+    lines = rows // SPAN
+    for h in range(target.shape[1] // width):
         for j in range(lines):
-            piece = source[row : row + 1, j * width : (j + 1) * width]
-            at = first + row * lines + j
-            target[at : at + 1, :] = piece.astype(F32)
-
-
-def gather_cells(table, index):
+            at = j * target.shape[1] + h * width
+            halves[pl.ds(j, SPAN, stride=lines), :] = source[:, at : at + width].astype(F32)
+        target[first : first + rows, h * width : h * width + width] = halves[...]
+
+
+def gather_steps(table, index, out):
     rows, width = index.shape
     tiles = [(r, h) for r in range(0, rows, 8) for h in range(0, width, 128)]
     pieces = [index[r : r + 8, h : h + 128] for r, h in tiles]
@@ -60,13 +61,13 @@
         for k in range(len(tiles)):
             picked = jnp.take_along_axis(line, low[k], axis=1, mode="promise_in_bounds")
             found[k] = jnp.where(high[k] == i, picked, found[k])
+        yield
     across = width // 128
-    return jnp.concatenate(
-        [jnp.concatenate(found[k : k + across], 1) for k in range(0, len(found), across)], 0
-    )
-
-
-def scatter_add(total, values, index):
+    lines = [jnp.concatenate(found[k : k + across], 1) for k in range(0, len(found), across)]
+    out.append(jnp.concatenate(lines, 0))
+
+
+def scatter_steps(totals, values, index):
     rows, width = index.shape
     place = lax.broadcasted_iota(I32, (64, width), 0)
     for r in range(rows):
@@ -84,10 +85,34 @@
             0,
         )
         chosen = jnp.where(column_here, 1.0, 0.0).astype(BF16)
-        total = total + lax.dot_general(
-            spread, chosen, CONTRACT_LANES, preferred_element_type=F32
+        totals.append(
+            totals.pop()
+            + lax.dot_general(spread, chosen, CONTRACT_LANES, preferred_element_type=F32)
         )
-    return total
+        yield
+
+
+def remap(parts):
+    totals = [jnp.zeros((128, 64), F32)]
+    adding = iter(())
+    for table, cells, weights, targets in parts:
+        found = []
+        for step, _ in enumerate(gather_steps(table, cells, found)):
+            if step % 2:
+                next(adding, None)
+        for _ in adding:
+            pass
+        adding = scatter_steps(totals, weights * found[0], targets)
+    for _ in adding:
+        pass
+    return as_rows(totals[0])
+
+
+def scatter_add(total, values, index):
+    totals = [total]
+    for _ in scatter_steps(totals, values, index):
+        pass
+    return totals[0]
 
 
 def as_rows(total):
@@ -96,7 +121,7 @@
     return jnp.concatenate([cells[:, q, :] for q in range(4)], 1)
 
 
-def pack_kernel(cells, weights, slots, state, coeff, vertical, pack, code, ints, reals, codes, sems):
+def pack_kernel(cells, weights, slots, state, coeff, vertical, pack, code, ints, reals, codes, halves, sems):
     copies = [
         pltpu.make_async_copy(state.at[0], pack.at[256:272], sems.at[0]),
         pltpu.make_async_copy(coeff.at[0], pack.at[272:288], sems.at[1]),
@@ -111,9 +136,9 @@
         first.start()
         second.start()
         first.wait()
-        fold(ints, pack, 0)
+        fold(ints, pack, 0, halves)
         second.wait()
-        fold(reals, pack, 128)
+        fold(reals, pack, 128, halves)
 
     def ocean():
         first = pltpu.make_async_copy(slots, ints, sems.at[3])
@@ -121,7 +146,7 @@
         pack[128:256, :] = jnp.zeros((128, pack.shape[1]), F32)
         first.wait()
         ints[...] = renumbered(ints[...])
-        fold(ints, pack, 0)
+        fold(ints, pack, 0, halves)
 
     on_each_component(atmosphere, ocean)
     for copy in copies:
@@ -223,11 +248,10 @@
     out[...] = edge[...]
 
 
-def add_fluxes(total, cells, weights, flux, ends, before, after, slots):
+def whole_flux(flux, ends, before, after):
     first = flux[0:1] + ends[0:1] * (0.2 * before)
     last = flux[15:16] + ends[1:2] * (0.2 * after)
-    flux = jnp.concatenate([first, flux[1:15], last], 0)
-    return scatter_add(total, weights * gather_cells(flux, cells.astype(I32)), slots.astype(I32))
+    return jnp.concatenate([first, flux[1:15], last], 0)
 
 
 def flux_kernel(edge, m1, m2, m3, m4, own, pack, other, partial):
@@ -236,26 +260,30 @@
     def either(a, b):
         return jnp.where(atmosphere, a, b)
 
-    def part(m):
+    def part(cells, weights, flux, ends, before, after, slots):
+        return whole_flux(flux, ends, before, after), cells.astype(I32), weights, slots.astype(I32)
+
+    def sent(m):
         return m[0:16, :], m[16:32, :], m[32:48, :], m[64:72, :]
 
-    total = jnp.zeros((128, 64), F32)
+    parts = []
     before = either(pack[271:272, :], m2[67:68, :])
     after = either(m2[66:67, :], other[256:257, :])
-    total = add_fluxes(total, *part(m1), before, after, either(block_of(other, 3), block_of(pack, 5)))
+    parts.append(part(*sent(m1), before, after, either(block_of(other, 3), block_of(pack, 5))))
     before = either(m1[67:68, :], m3[67:68, :])
     after = either(m3[66:67, :], m1[66:67, :])
-    total = add_fluxes(total, *part(m2), before, after, either(block_of(other, 2), block_of(pack, 6)))
+    parts.append(part(*sent(m2), before, after, either(block_of(other, 2), block_of(pack, 6))))
     before = either(m2[67:68, :], m4[51:52, :])
     after = either(m4[50:51, :], m2[66:67, :])
-    total = add_fluxes(total, *part(m3), before, after, either(block_of(other, 1), block_of(pack, 7)))
+    parts.append(part(*sent(m3), before, after, either(block_of(other, 1), block_of(pack, 7))))
     before = either(m3[67:68, :], m1[67:68, :])
     cells = either(m4[0:16, :], block_of(other, 4))
     weights = either(m4[16:32, :], block_of(other, 12))
     flux = either(m4[32:48, :], own[32:48, :])
     ends = either(m4[48:56, :], own[64:72, :])
     slots = either(block_of(other, 0), block_of(pack, 4))
-    partial[...] = as_rows(add_fluxes(total, cells, weights, flux, ends, before, edge[0:1, :], slots))
+    parts.append(part(cells, weights, flux, ends, before, edge[0:1, :], slots))
+    partial[...] = remap(parts)
 
 
 def source_kernel(partial, partial_sw, pack, other, code, rhs, fifth, sixth):
@@ -386,16 +414,15 @@
     slots = [jnp.where(atmosphere, block_of(other, 4), m4[0:16, :])]
     for a, b in ((m1, m3), (m2, m2), (m3, m1)):
         slots.append(jnp.where(atmosphere, a[48:64, :], b[48:64, :]))
-    total = jnp.zeros((128, 64), F32)
+    parts = []
     for i in range(4):
         at = 24 + 16 * i
         eta = jnp.concatenate([even[at : at + 16, :], odd[at : at + 16, :]], 1)
         sst = 1.25 * sea[i] + 0.5 * eta - 0.25 * rhs[at : at + 16, :]
-        picked = gather_cells(sst, slots[i].astype(I32))
         cell = jnp.where(atmosphere, block_of(pack, 4 + i), block_of(other, i)).astype(I32)
         weight = jnp.where(atmosphere, block_of(pack, 12 + i), block_of(other, 8 + i))
-        total = scatter_add(total, weight * picked, cell)
-    part = as_rows(total)
+        parts.append((sst, slots[i].astype(I32), weight, cell))
+    part = remap(parts)
     send[...] = jnp.where(atmosphere, unhalved(even[24:40, :], odd[24:40, :]), part)
     keep[...] = jnp.where(atmosphere, part * inverse[...], 0.0)
 
@@ -421,6 +448,7 @@
             pltpu.VMEM(send_cell.shape, I32),
             pltpu.VMEM(send_cell.shape, F32),
             pltpu.VMEM(block, I32),
+            pltpu.VMEM((SPAN * lines, 128), F32),
             pltpu.SemaphoreType.DMA((5,)),
         ],
         where=pltpu.HBM,

time: 39.8 us -> 39.7 us (level)
  no operation moved by 1% of the time
where the time goes in v5:
time: 39.7 us; the launch traced here: 39.4 us
  starting transfers between devices  21.6 us (54%)
  Pallas kernels  9.57 us (24%)
  waiting for transfers between devices  7.54 us (19%)
  other arithmetic  0.61 us (2%)
    ppermute x10, starting transfers between devices, move(): return lax.ppermute(x, GRID, pairs)  18.8 us
    pallas_call x8, Pallas kernels, call(): pl.pallas_call(kernel, out_shape=out, in_specs=[pl.BlockSpec(memory_space...  9.57 us
    ppermute x10, waiting for transfers between devices, move(): return lax.ppermute(x, GRID, pairs)  4.31 us
    ppermute x4, waiting for transfers between devices, swap(): return lax.ppermute(x, 'comp', [(0, 1), (1, 0)])  3.22 us
    ppermute x4, starting transfers between devices, swap(): return lax.ppermute(x, 'comp', [(0, 1), (1, 0)])  2.23 us
  transfers between devices with their start and end apart: 15, of which 6 were waited for; matrix products, arithmetic and copies ran while one was open for 0% of the time, Pallas kernels for 6%

profile of v5, /device:TPU:0, one launch (start us, length us, event | category | flops | bytes accessed | tf_op | source)
XLA Modules:
  0.0 39.4 jit_solution(4077661248408531306)
XLA Ops:
  0.0 1.2 %shard_map.64 = (f32[288,256]{1,0:T(8,128)S(1)}, f32[16,256]{1,0:T(8,128)S(1)}) custom-call(s32[8,4096]{1,0:T(8,128)} %cells.1, f32[8,4096]{1,0:T(8,128)} %weights.1, s32[8,4096]{1,0:T(8,128)} %slots.1, f32[1,16,256]{2,1,0:T(8,128)} %state.1, f32[1,16,256]{2,1,0:T(8,128)} %coeff.1, s32[16,256]{1,0:T(8,128)} %vertical.1), custom_call_target="tpu_custom_call" | custom-call | tf_op jit(solution)/shard_map/pallas_call | solution.py:23
  1.2 0.5 %collective-permute-start = (f32[288,256]{1,0:T(8,128)S(1)}, f32[288,256]{1,0:T(8,128)S(1)}, u32[]{:S(2)}, u32[]{:S(2)}) collective-permute-start(f32[288,256]{1,0:T(8,128)S(1)} %get-tuple-element.17.pack), channel_id=1, source_target_pairs={{0,16},{16,0},{1,17},{17,1},{2,18},{18,2},{3,19},{19,3},{4,20},{20... | collective-permute-start | bytes 884744 | tf_op jit(solution)/shard_map/ppermute | solution.py:436
  1.7 1.2 %collective-permute-done.other = f32[288,256]{1,0:T(8,128)S(1)} collective-permute-done((f32[288,256]{1,0:T(8,128)S(1)}, f32[288,256]{1,0:T(8,128)S(1)}, u32[]{:S(2)}, u32[]{:S(2)}) %collective-permute-start) | collective-permute-done | bytes 294944 | tf_op jit(solution)/shard_map/ppermute | solution.py:436
  2.9 0.1 shard_map.66
  3.0 6.0 %collective-permute-start.3 = (f32[120,256]{1,0:T(8,128)S(1)}, f32[120,256]{1,0:T(8,128)S(1)}, u32[]{:S(2)}, u32[]{:S(2)}) collective-permute-start(f32[120,256]{1,0:T(8,128)S(1)} %get-tuple-element.21.own), channel_id=1, source_target_pairs={{2,0},{3,1},{4,2},{5,3},{6,4},{7,5},{8,6},{9,7},{10,8},{11,9},{12,... | collective-permute-start | bytes 368648 | tf_op jit(solution)/shard_map/ppermute | solution.py:441
  9.0 1.4 %collective-permute-start.2 = (f32[120,256]{1,0:T(8,128)S(1)}, f32[120,256]{1,0:T(8,128)S(1)}, u32[]{:S(2)}, u32[]{:S(2)}) collective-permute-start(f32[120,256]{1,0:T(8,128)S(1)} %get-tuple-element.20), channel_id=1, source_target_pairs={{1,0},{2,1},{3,2},{4,3},{5,4},{6,5},{7,6},{8,7},{9,8},{10,9},{11,1... | collective-permute-start | bytes 368648 | tf_op jit(solution)/shard_map/ppermute | solution.py:441
  10.4 0.5 %collective-permute-start.4 = (f32[120,256]{1,0:T(8,128)S(1)}, f32[120,256]{1,0:T(8,128)S(1)}, u32[]{:S(2)}, u32[]{:S(2)}) collective-permute-start(f32[120,256]{1,0:T(8,128)S(1)} %get-tuple-element.22), channel_id=1, source_target_pairs={{3,0},{4,1},{5,2},{6,3},{7,4},{8,5},{9,6},{10,7},{11,8},{12,9},{13... | collective-permute-start | bytes 368648 | tf_op jit(solution)/shard_map/ppermute | solution.py:441
  10.9 1.3 %collective-permute-start.1 = (f32[8,256]{1,0:T(8,128)S(1)}, f32[8,256]{1,0:T(8,128)S(1)}, u32[]{:S(2)}, u32[]{:S(2)}) collective-permute-start(f32[8,256]{1,0:T(8,128)S(1)} %get-tuple-element.19), channel_id=1, source_target_pairs={{5,0},{6,1},{7,2},{8,3},{9,4},{10,5},{11,6},{12,7},{13,8},{14,9},{... | collective-permute-start | bytes 24584 | tf_op jit(solution)/shard_map/ppermute | solution.py:441
  12.2 1.3 %collective-permute-start.5 = (f32[88,256]{1,0:T(8,128)S(1)}, f32[88,256]{1,0:T(8,128)S(1)}, u32[]{:S(2)}, u32[]{:S(2)}) collective-permute-start(f32[88,256]{1,0:T(8,128)S(1)} %get-tuple-element.23), channel_id=1, source_target_pairs={{4,0},{5,1},{6,2},{7,3},{8,4},{9,5},{10,6},{11,7},{12,8},{13,9},{1... | collective-permute-start | bytes 270344 | tf_op jit(solution)/shard_map/ppermute | solution.py:441
  13.6 4.1 %collective-permute-done.1.edge = f32[8,256]{1,0:T(8,128)S(1)} collective-permute-done((f32[8,256]{1,0:T(8,128)S(1)}, f32[8,256]{1,0:T(8,128)S(1)}, u32[]{:S(2)}, u32[]{:S(2)}) %collective-permute-start.1) | collective-permute-done | bytes 8224 | tf_op jit(solution)/shard_map/ppermute | solution.py:441
  17.7 0.1 collective-permute-done.5.m4
  17.8 0.0 collective-permute-done.3.m2
  17.8 0.0 collective-permute-done.2.m1
  17.8 0.0 collective-permute-done.4.m3
  17.8 2.1 %shard_map.68.partial = f32[16,256]{1,0:T(8,128)S(1)} custom-call(f32[8,256]{1,0:T(8,128)S(1)} %shard_map.67.edge, f32[120,256]{1,0:T(8,128)S(1)} %collective-permute-done.2.m1, f32[120,256]{1,0:T(8,128)S(1)} %collective-permute-done.3.m2, f32[120,256]{1,0:T(8,128)S(1)} %collective-permute-done.4.m3, f32[88,256]{1,0:T(8,128)S(1)} %collective-permute-done.5.m4, ...), custom_call_target="tpu_custom_call" | custom-call | flops 1000000000 | tf_op jit(solution)/shard_map/pallas_call | solution.py:23
  20.0 0.0 collective-permute-start.6
  20.0 1.2 %collective-permute-done.6.partial_sw = f32[16,256]{1,0:T(8,128)S(1)} collective-permute-done((f32[16,256]{1,0:T(8,128)S(1)}, f32[16,256]{1,0:T(8,128)S(1)}, u32[]{:S(2)}, u32[]{:S(2)}) %collective-permute-start.6) | collective-permute-done | bytes 16416 | tf_op jit(solution)/shard_map/ppermute | solution.py:436
  21.2 2.2 %collective-permute-start.7 = (f32[16,256]{1,0:T(8,128)S(1)}, f32[16,256]{1,0:T(8,128)S(1)}, u32[]{:S(2)}, u32[]{:S(2)}) collective-permute-start(f32[16,256]{1,0:T(8,128)S(1)} %get-tuple-element.25), channel_id=1, source_target_pairs={{1,0},{2,1},{3,2},{4,3},{5,4},{6,5},{7,6},{8,7},{9,8},{10,9},{11,1... | collective-permute-start | bytes 49160 | tf_op jit(solution)/shard_map/ppermute | solution.py:441
  23.4 2.0 %collective-permute-start.8 = (f32[16,256]{1,0:T(8,128)S(1)}, f32[16,256]{1,0:T(8,128)S(1)}, u32[]{:S(2)}, u32[]{:S(2)}) collective-permute-start(f32[16,256]{1,0:T(8,128)S(1)} %get-tuple-element.25), channel_id=1, source_target_pairs={{2,0},{3,1},{4,2},{5,3},{6,4},{7,5},{8,6},{9,7},{10,8},{11,9},{12,... | collective-permute-start | bytes 49160 | tf_op jit(solution)/shard_map/ppermute | solution.py:441
  25.4 2.2 %collective-permute-start.12 = (f32[16,256]{1,0:T(8,128)S(1)}, f32[16,256]{1,0:T(8,128)S(1)}, u32[]{:S(2)}, u32[]{:S(2)}) collective-permute-start(f32[16,256]{1,0:T(8,128)S(1)} %get-tuple-element.25), channel_id=1, source_target_pairs={{3,0},{4,1},{5,2},{6,3},{7,4},{8,5},{9,6},{10,7},{11,8},{12,9},{13... | collective-permute-start | bytes 49160 | tf_op jit(solution)/shard_map/ppermute | solution.py:441
  27.5 0.4 %collective-permute-start.13 = (f32[16,256]{1,0:T(8,128)S(1)}, f32[16,256]{1,0:T(8,128)S(1)}, u32[]{:S(2)}, u32[]{:S(2)}) collective-permute-start(f32[16,256]{1,0:T(8,128)S(1)} %get-tuple-element.25), channel_id=1, source_target_pairs={{4,0},{5,1},{6,2},{7,3},{8,4},{9,5},{10,6},{11,7},{12,8},{13,9},{1... | collective-permute-start | bytes 49160 | tf_op jit(solution)/shard_map/ppermute | solution.py:441
  28.0 1.4 %collective-permute-start.10 = (f32[48,256]{1,0:T(8,128)S(1)}, f32[48,256]{1,0:T(8,128)S(1)}, u32[]{:S(2)}, u32[]{:S(2)}) collective-permute-start(f32[48,256]{1,0:T(8,128)S(1)} %get-tuple-element.24.own), channel_id=1, source_target_pairs={{5,0},{6,1},{7,2},{8,3},{9,4},{10,5},{11,6},{12,7},{13,8},{14,9},{... | collective-permute-start | bytes 147464 | tf_op jit(solution)/shard_map/ppermute | solution.py:441
  29.4 0.0 collective-permute-done.7.p1
  29.4 0.7 %collective-permute-start.11 = (f32[24,256]{1,0:T(8,128)S(1)}, f32[24,256]{1,0:T(8,128)S(1)}, u32[]{:S(2)}, u32[]{:S(2)}) collective-permute-start(f32[24,256]{1,0:T(8,128)S(1)} %get-tuple-element.26), channel_id=1, source_target_pairs={{16,22},{17,23},{18,24},{19,25},{20,26},{21,27},{22,28},{23,29},{2... | collective-permute-start | bytes 73736 | tf_op jit(solution)/shard_map/ppermute | solution.py:472
  30.0 0.0 collective-permute-done.8.p2
  30.1 0.9 %collective-permute-start.9 = (f32[72,256]{1,0:T(8,128)S(1)}, f32[72,256]{1,0:T(8,128)S(1)}, u32[]{:S(2)}, u32[]{:S(2)}) collective-permute-start(f32[72,256]{1,0:T(8,128)S(1)} %shard_map.70), channel_id=1, source_target_pairs={{0,16},{16,0},{1,17},{17,1},{2,18},{18,2},{3,19},{19,3},{4,20},{20... | collective-permute-start | bytes 221192 | tf_op jit(solution)/shard_map/ppermute | solution.py:436
  31.0 2.4 %shard_map.65.inverse = f32[16,256]{1,0:T(8,128)S(1)} custom-call(f32[288,256]{1,0:T(8,128)S(1)} %get-tuple-element.17.pack), custom_call_target="tpu_custom_call" | custom-call | flops 1000000000 | tf_op jit(solution)/shard_map/pallas_call | solution.py:23
  33.4 0.0 collective-permute-done.12.p3
  33.4 0.0 collective-permute-done.13.p4
  33.4 0.0 collective-permute-done.11.sixth
  33.4 0.1 collective-permute-done.10.fifth
  33.5 0.0 collective-permute-done.9.near
  33.5 3.7 %shard_map.71 = (f32[16,256]{1,0:T(8,128)S(1)}, f32[16,256]{1,0:T(8,128)S(1)}) custom-call(f32[288,256]{1,0:T(8,128)S(1)} %get-tuple-element.17.pack, f32[288,256]{1,0:T(8,128)S(1)} %collective-permute-done.other, f32[16,256]{1,0:T(8,128)S(1)} %shard_map.65.inverse, f32[48,256]{1,0:T(8,128)S(1)} %get-tuple-element.24.own, ...), custom_call_target="tpu_custom_call" | custom-call | tf_op jit(solution)/shard_map/pallas_call | solution.py:23
  37.2 0.8 %collective-permute-start.14 = (f32[16,256]{1,0:T(8,128)S(1)}, f32[16,256]{1,0:T(8,128)S(1)}, u32[]{:S(2)}, u32[]{:S(2)}) collective-permute-start(f32[16,256]{1,0:T(8,128)S(1)} %get-tuple-element.28), channel_id=1, source_target_pairs={{0,16},{16,0},{1,17},{17,1},{2,18},{18,2},{3,19},{19,3},{4,20},{20... | collective-permute-start | bytes 49160 | tf_op jit(solution)/shard_map/ppermute | solution.py:436
  38.0 0.8 %collective-permute-done.14 = f32[16,256]{1,0:T(8,128)S(1)} collective-permute-done((f32[16,256]{1,0:T(8,128)S(1)}, f32[16,256]{1,0:T(8,128)S(1)}, u32[]{:S(2)}, u32[]{:S(2)}) %collective-permute-start.14) | collective-permute-done | bytes 16416 | tf_op jit(solution)/shard_map/ppermute | solution.py:436
  38.8 0.6 %add_bitcast_fusion = f32[1,16,256]{2,1,0:T(8,128)} fusion(f32[16,256]{1,0:T(8,128)S(1)} %get-tuple-element.27, f32[16,256]{1,0:T(8,128)S(1)} %collective-permute-done.14, f32[16,256]{1,0:T(8,128)S(1)} %shard_map.65.inverse), kind=kLoop, calls=%fused_computation | loop fusion | flops 8192 | bytes 65536 | tf_op jit(solution)/shard_map/broadcast_in_dim | solution.py:481
  (3 shorter events, 0.0 us)
Async XLA Ops:
  1.2 1.7 %collective-permute-start = (f32[288,256]{1,0:T(8,128)S(1)}, f32[288,256]{1,0:T(8,128)S(1)}, u32[]{:S(2)}, u32[]{:S(2)}) collective-permute-start(f32[288,256]{1,0:T(8,128)S(1)} %get-tuple-element.17.pack), channel_id=1, source_target_pairs={{0,16},{16,0},{1,17},{17,1},{2,18},{18,2},{3,19},{19,3},{4,20},{20... | collective-permute-start | bytes 884744 | tf_op jit(solution)/shard_map/ppermute | solution.py:436
  3.0 14.8 %collective-permute-start.3 = (f32[120,256]{1,0:T(8,128)S(1)}, f32[120,256]{1,0:T(8,128)S(1)}, u32[]{:S(2)}, u32[]{:S(2)}) collective-permute-start(f32[120,256]{1,0:T(8,128)S(1)} %get-tuple-element.21.own), channel_id=1, source_target_pairs={{2,0},{3,1},{4,2},{5,3},{6,4},{7,5},{8,6},{9,7},{10,8},{11,9},{12,... | collective-permute-start | bytes 368648 | tf_op jit(solution)/shard_map/ppermute | solution.py:441
  9.0 8.8 %collective-permute-start.2 = (f32[120,256]{1,0:T(8,128)S(1)}, f32[120,256]{1,0:T(8,128)S(1)}, u32[]{:S(2)}, u32[]{:S(2)}) collective-permute-start(f32[120,256]{1,0:T(8,128)S(1)} %get-tuple-element.20), channel_id=1, source_target_pairs={{1,0},{2,1},{3,2},{4,3},{5,4},{6,5},{7,6},{8,7},{9,8},{10,9},{11,1... | collective-permute-start | bytes 368648 | tf_op jit(solution)/shard_map/ppermute | solution.py:441
  10.4 7.4 %collective-permute-start.4 = (f32[120,256]{1,0:T(8,128)S(1)}, f32[120,256]{1,0:T(8,128)S(1)}, u32[]{:S(2)}, u32[]{:S(2)}) collective-permute-start(f32[120,256]{1,0:T(8,128)S(1)} %get-tuple-element.22), channel_id=1, source_target_pairs={{3,0},{4,1},{5,2},{6,3},{7,4},{8,5},{9,6},{10,7},{11,8},{12,9},{13... | collective-permute-start | bytes 368648 | tf_op jit(solution)/shard_map/ppermute | solution.py:441
  10.9 6.8 %collective-permute-start.1 = (f32[8,256]{1,0:T(8,128)S(1)}, f32[8,256]{1,0:T(8,128)S(1)}, u32[]{:S(2)}, u32[]{:S(2)}) collective-permute-start(f32[8,256]{1,0:T(8,128)S(1)} %get-tuple-element.19), channel_id=1, source_target_pairs={{5,0},{6,1},{7,2},{8,3},{9,4},{10,5},{11,6},{12,7},{13,8},{14,9},{... | collective-permute-start | bytes 24584 | tf_op jit(solution)/shard_map/ppermute | solution.py:441
  12.2 5.6 %collective-permute-start.5 = (f32[88,256]{1,0:T(8,128)S(1)}, f32[88,256]{1,0:T(8,128)S(1)}, u32[]{:S(2)}, u32[]{:S(2)}) collective-permute-start(f32[88,256]{1,0:T(8,128)S(1)} %get-tuple-element.23), channel_id=1, source_target_pairs={{4,0},{5,1},{6,2},{7,3},{8,4},{9,5},{10,6},{11,7},{12,8},{13,9},{1... | collective-permute-start | bytes 270344 | tf_op jit(solution)/shard_map/ppermute | solution.py:441
  20.0 1.2 %collective-permute-start.6 = (f32[16,256]{1,0:T(8,128)S(1)}, f32[16,256]{1,0:T(8,128)S(1)}, u32[]{:S(2)}, u32[]{:S(2)}) collective-permute-start(f32[16,256]{1,0:T(8,128)S(1)} %shard_map.68.partial), channel_id=1, source_target_pairs={{0,16},{16,0},{1,17},{17,1},{2,18},{18,2},{3,19},{19,3},{4,20},{20... | collective-permute-start | bytes 49160 | tf_op jit(solution)/shard_map/ppermute | solution.py:436
  21.2 8.2 %collective-permute-start.7 = (f32[16,256]{1,0:T(8,128)S(1)}, f32[16,256]{1,0:T(8,128)S(1)}, u32[]{:S(2)}, u32[]{:S(2)}) collective-permute-start(f32[16,256]{1,0:T(8,128)S(1)} %get-tuple-element.25), channel_id=1, source_target_pairs={{1,0},{2,1},{3,2},{4,3},{5,4},{6,5},{7,6},{8,7},{9,8},{10,9},{11,1... | collective-permute-start | bytes 49160 | tf_op jit(solution)/shard_map/ppermute | solution.py:441
  23.4 6.7 %collective-permute-start.8 = (f32[16,256]{1,0:T(8,128)S(1)}, f32[16,256]{1,0:T(8,128)S(1)}, u32[]{:S(2)}, u32[]{:S(2)}) collective-permute-start(f32[16,256]{1,0:T(8,128)S(1)} %get-tuple-element.25), channel_id=1, source_target_pairs={{2,0},{3,1},{4,2},{5,3},{6,4},{7,5},{8,6},{9,7},{10,8},{11,9},{12,... | collective-permute-start | bytes 49160 | tf_op jit(solution)/shard_map/ppermute | solution.py:441
  25.4 8.1 %collective-permute-start.12 = (f32[16,256]{1,0:T(8,128)S(1)}, f32[16,256]{1,0:T(8,128)S(1)}, u32[]{:S(2)}, u32[]{:S(2)}) collective-permute-start(f32[16,256]{1,0:T(8,128)S(1)} %get-tuple-element.25), channel_id=1, source_target_pairs={{3,0},{4,1},{5,2},{6,3},{7,4},{8,5},{9,6},{10,7},{11,8},{12,9},{13... | collective-permute-start | bytes 49160 | tf_op jit(solution)/shard_map/ppermute | solution.py:441
  27.5 5.9 %collective-permute-start.13 = (f32[16,256]{1,0:T(8,128)S(1)}, f32[16,256]{1,0:T(8,128)S(1)}, u32[]{:S(2)}, u32[]{:S(2)}) collective-permute-start(f32[16,256]{1,0:T(8,128)S(1)} %get-tuple-element.25), channel_id=1, source_target_pairs={{4,0},{5,1},{6,2},{7,3},{8,4},{9,5},{10,6},{11,7},{12,8},{13,9},{1... | collective-permute-start | bytes 49160 | tf_op jit(solution)/shard_map/ppermute | solution.py:441
  28.0 5.5 %collective-permute-start.10 = (f32[48,256]{1,0:T(8,128)S(1)}, f32[48,256]{1,0:T(8,128)S(1)}, u32[]{:S(2)}, u32[]{:S(2)}) collective-permute-start(f32[48,256]{1,0:T(8,128)S(1)} %get-tuple-element.24.own), channel_id=1, source_target_pairs={{5,0},{6,1},{7,2},{8,3},{9,4},{10,5},{11,6},{12,7},{13,8},{14,9},{... | collective-permute-start | bytes 147464 | tf_op jit(solution)/shard_map/ppermute | solution.py:441
  29.4 4.1 %collective-permute-start.11 = (f32[24,256]{1,0:T(8,128)S(1)}, f32[24,256]{1,0:T(8,128)S(1)}, u32[]{:S(2)}, u32[]{:S(2)}) collective-permute-start(f32[24,256]{1,0:T(8,128)S(1)} %get-tuple-element.26), channel_id=1, source_target_pairs={{16,22},{17,23},{18,24},{19,25},{20,26},{21,27},{22,28},{23,29},{2... | collective-permute-start | bytes 73736 | tf_op jit(solution)/shard_map/ppermute | solution.py:472
  30.1 3.5 %collective-permute-start.9 = (f32[72,256]{1,0:T(8,128)S(1)}, f32[72,256]{1,0:T(8,128)S(1)}, u32[]{:S(2)}, u32[]{:S(2)}) collective-permute-start(f32[72,256]{1,0:T(8,128)S(1)} %shard_map.70), channel_id=1, source_target_pairs={{0,16},{16,0},{1,17},{17,1},{2,18},{18,2},{3,19},{19,3},{4,20},{20... | collective-permute-start | bytes 221192 | tf_op jit(solution)/shard_map/ppermute | solution.py:436
  37.2 1.6 %collective-permute-start.14 = (f32[16,256]{1,0:T(8,128)S(1)}, f32[16,256]{1,0:T(8,128)S(1)}, u32[]{:S(2)}, u32[]{:S(2)}) collective-permute-start(f32[16,256]{1,0:T(8,128)S(1)} %get-tuple-element.28), channel_id=1, source_target_pairs={{0,16},{16,0},{1,17},{17,1},{2,18},{18,2},{3,19},{19,3},{4,20},{20... | collective-permute-start | bytes 49160 | tf_op jit(solution)/shard_map/ppermute | solution.py:436

commit v6 on v5

--- a/solution.py
+++ b/solution.py
@@ -92,8 +92,8 @@
         yield
 
 
-def remap(parts):
-    totals = [jnp.zeros((128, 64), F32)]
+def remap(parts, total):
+    totals = [total]
     adding = iter(())
     for table, cells, weights, targets in parts:
         found = []
@@ -105,7 +105,7 @@
         adding = scatter_steps(totals, weights * found[0], targets)
     for _ in adding:
         pass
-    return as_rows(totals[0])
+    return totals[0]
 
 
 def scatter_add(total, values, index):
@@ -231,21 +231,19 @@
     on_each_component(atmosphere, ocean)
 
 
-def share_kernel(pack, inverse):
-    def atmosphere():
+def share_kernel(pack, other, share):
+    def fill(air, first):
         total = jnp.zeros((128, 64), F32)
-        for d in range(SPAN):
-            total = scatter_add(total, block_of(pack, 8 + d), block_of(pack, d).astype(I32))
-        inverse[...] = 1.0 / as_rows(total)
-
-    def ocean():
-        inverse[...] = jnp.ones_like(inverse)
-
-    on_each_component(atmosphere, ocean)
-
-
-def edge_kernel(edge, out):
+        for d in range(first, first + SPAN // 2):
+            total = scatter_add(total, block_of(air, 8 + d), block_of(air, d).astype(I32))
+        share[...] = as_rows(total)
+
+    on_each_component(lambda: fill(pack, 4), lambda: fill(other, 0))
+
+
+def edge_kernel(edge, total, out, same):
     out[...] = edge[...]
+    same[...] = total[...]
 
 
 def whole_flux(flux, ends, before, after):
@@ -254,51 +252,65 @@
     return jnp.concatenate([first, flux[1:15], last], 0)
 
 
-def flux_kernel(edge, m1, m2, m3, m4, own, pack, other, partial):
+def flux_part(cells, weights, flux, ends, before, after, slots):
+    return whole_flux(flux, ends, before, after), cells.astype(I32), weights, slots.astype(I32)
+
+
+def sent(m):
+    return m[0:16, :], m[16:32, :], m[32:48, :], m[64:72, :]
+
+
+def first_flux_kernel(m1, m2, m3, pack, other, total):
     atmosphere = lax.axis_index("comp") == 0
 
     def either(a, b):
         return jnp.where(atmosphere, a, b)
-
-    def part(cells, weights, flux, ends, before, after, slots):
-        return whole_flux(flux, ends, before, after), cells.astype(I32), weights, slots.astype(I32)
-
-    def sent(m):
-        return m[0:16, :], m[16:32, :], m[32:48, :], m[64:72, :]
 
     parts = []
     before = either(pack[271:272, :], m2[67:68, :])
     after = either(m2[66:67, :], other[256:257, :])
-    parts.append(part(*sent(m1), before, after, either(block_of(other, 3), block_of(pack, 5))))
+    parts.append(flux_part(*sent(m1), before, after, either(block_of(other, 3), block_of(pack, 5))))
     before = either(m1[67:68, :], m3[67:68, :])
     after = either(m3[66:67, :], m1[66:67, :])
-    parts.append(part(*sent(m2), before, after, either(block_of(other, 2), block_of(pack, 6))))
-    before = either(m2[67:68, :], m4[51:52, :])
-    after = either(m4[50:51, :], m2[66:67, :])
-    parts.append(part(*sent(m3), before, after, either(block_of(other, 1), block_of(pack, 7))))
+    parts.append(flux_part(*sent(m2), before, after, either(block_of(other, 2), block_of(pack, 6))))
+    total[...] = remap(parts, jnp.zeros((128, 64), F32))
+
+
+def second_flux_kernel(edge, m4, m1, m2, m3, own, pack, other, total, partial):
+    atmosphere = lax.axis_index("comp") == 0
+
+    def either(a, b):
+        return jnp.where(atmosphere, a, b)
+
+    parts = []
     before = either(m3[67:68, :], m1[67:68, :])
     cells = either(m4[0:16, :], block_of(other, 4))
     weights = either(m4[16:32, :], block_of(other, 12))
     flux = either(m4[32:48, :], own[32:48, :])
     ends = either(m4[48:56, :], own[64:72, :])
     slots = either(block_of(other, 0), block_of(pack, 4))
-    parts.append(part(cells, weights, flux, ends, before, edge[0:1, :], slots))
-    partial[...] = remap(parts)
-
-
-def source_kernel(partial, partial_sw, pack, other, code, rhs, fifth, sixth):
+    parts.append(flux_part(cells, weights, flux, ends, before, edge[0:1, :], slots))
+    before = either(m2[67:68, :], m4[51:52, :])
+    after = either(m4[50:51, :], m2[66:67, :])
+    parts.append(flux_part(*sent(m3), before, after, either(block_of(other, 1), block_of(pack, 7))))
+    partial[...] = as_rows(remap(parts, total[...]))
+
+
+def source_kernel(partial, partial_sw, pack, other, code, m4, rhs, first, second, sixth):
     atmosphere = lax.axis_index("comp") == 0
     sea = jnp.where(atmosphere, other[256:272, :], pack[256:272, :])
-    diagonal = jnp.where(atmosphere, other[272:288, :], pack[272:288, :])
     total = partial[...] + partial_sw[...] + sea
     rhs[...] = total
-    for k, part in enumerate((total, diagonal, code[...])):
-        fifth[16 * k : 16 * k + 16, :] = part
-        sixth[8 * k : 8 * k + 8, :] = part[8:16]
+    first[0:16, :] = total
+    first[16:48, :] = m4[56:88, :]
+    second[0:16, :] = total
+    second[16:24, :] = m4[64:72, :]
+    second[24:32, :] = m4[80:88, :]
+    sixth[...] = total[8:16]
 
 
 def near_kernel(p1, p2, m1, m2, out):
-    out[0:16, :] = p1[...]
+    out[0:16, :] = p1[0:16, :]
     out[16:48, :] = m1[72:104, :]
     out[48:56, :] = p2[8:16, :]
     out[56:64, :] = m2[80:88, :]
@@ -306,7 +318,7 @@
 
 
 def trace_kernel(
-    pack, other, inverse, own, near, fifth, sixth, p1, p2, p3, p4, m1, m2, m3, m4,
+    pack, other, share, code_own, own, near, fifth, sixth, p1, p2, p3, p4, m1, m2, m3, m4,
     send, keep, rhs, inv, code, code_up, code_down, even, odd,
 ):
     rows, width = rhs.shape
@@ -324,15 +336,19 @@
     def thirds(ref, first, step, size):
         return [ref.at[first + k * step : first + k * step + size] for k in range(3)]
 
-    others = [(p, m.at[72:88], m.at[88:104]) for p, m in ((p1, m1), (p2, m2), (p3, m3))]
+    others = [(p.at[0:16], m.at[72:88], m.at[88:104]) for p, m in ((p1, m1), (p2, m2), (p3, m3))]
     others.append((p4, m4.at[56:72], m4.at[72:88]))
-    here = thirds(own, 0, 16, 16)
+    further = p1.at[16:24], p1.at[32:40]
+    whole = p1.at[16:32], p1.at[32:48]
+    last = p2.at[16:24], p2.at[24:32]
     on_each_component(
         lambda: place(
-            [thirds(near, 48, 8, 8), thirds(near, 0, 16, 16), here, *others, thirds(fifth, 0, 16, 8)]
+            [thirds(near, 48, 8, 8), thirds(near, 0, 16, 16), (own, other.at[272:288], code_own), *others,
+             (fifth.at[0:8], *further)]
         ),
         lambda: place(
-            [thirds(sixth, 0, 8, 8), thirds(fifth, 0, 16, 16), *others[::-1], here, thirds(near, 0, 16, 8)]
+            [(sixth, *last), (fifth, *whole), *others[::-1], (own, pack.at[272:288], code_own),
+             thirds(near, 0, 16, 8)]
         ),
     )
     line = lax.broadcasted_iota(I32, (8, width), 0)
@@ -422,9 +438,11 @@
         cell = jnp.where(atmosphere, block_of(pack, 4 + i), block_of(other, i)).astype(I32)
         weight = jnp.where(atmosphere, block_of(pack, 12 + i), block_of(other, 8 + i))
         parts.append((sst, slots[i].astype(I32), weight, cell))
-    part = remap(parts)
-    send[...] = jnp.where(atmosphere, unhalved(even[24:40, :], odd[24:40, :]), part)
-    keep[...] = jnp.where(atmosphere, part * inverse[...], 0.0)
+    part = as_rows(remap(parts, jnp.zeros((128, 64), F32)))
+    send[0:16, :] = jnp.where(atmosphere, unhalved(even[24:40, :], odd[24:40, :]), part)
+    send[16:32, :] = jnp.where(atmosphere, 1.0, share[...])
+    keep[0:16, :] = jnp.where(atmosphere, part, 0.0)
+    keep[16:32, :] = jnp.where(atmosphere, share[...], 0.0)
 
 
 def shards(state, coeff, vertical, send_cell, incoming_marine_slot, remap_weight):
@@ -460,25 +478,33 @@
         [(tall + 3 * lines, width)] * 3 + [(tall + lines, width), (8, width)],
         pack, other, code,
     )
-    (edge_in,) = call(edge_kernel, [(8, width)], move(edge, 5, 1), flops=10**9)
+    edge_in = move(edge, 5, 1)
     m1_in, m2_in, m3_in, m4_in = messages_in = [move(m, j, -j) for j, m in enumerate(messages, 1)]
-    (inverse,) = call(share_kernel, [block], pack, flops=10**9)
-    (partial,) = call(flux_kernel, [block], edge_in, *messages_in, messages[1], pack, other, flops=10**9)
-    rhs, fifth, sixth = call(
-        source_kernel, [block, (3 * lines, width), (24, width)], partial, swap(partial), pack, other, code
-    )
-    p1_in, p2_in, p3_in, p4_in = (move(rhs, j, -j) for j in range(1, 5))
-    fifth_in = move(fifth, 5, -5)
+    (share,) = call(share_kernel, [block], pack, other, flops=10**9)
+    (total,) = call(first_flux_kernel, [(128, 64)], m1_in, m2_in, m3_in, pack, other, flops=None)
+    edge_in, total = call(edge_kernel, [(8, width), (128, 64)], edge_in, total, flops=10**8)
+    (partial,) = call(
+        second_flux_kernel, [block],
+        edge_in, m4_in, m1_in, m2_in, m3_in, messages[1], pack, other, total, flops=10**9,
+    )
+    rhs, first, second, sixth = call(
+        source_kernel,
+        [block, (3 * lines, width), (2 * lines, width), (8, width)],
+        partial, swap(partial), pack, other, code, m4_in,
+    )
+    p1_in, p2_in = move(first, 1, -1), move(second, 2, -2)
+    p3_in, p4_in, fifth_in = (move(rhs, j, -j) for j in range(3, 6))
     sixth_in = lax.ppermute(sixth, GRID, [(tiles + t, tiles + (t + 6) % tiles) for t in range(tiles)])
     (near,) = call(near_kernel, [(72, width)], p1_in, p2_in, m1_in, m2_in)
     window = (6 * lines + 16, width)
     send, keep = call(
-        trace_kernel, [block, block],
-        pack, other, inverse, fifth, swap(near), fifth_in, sixth_in, p1_in, p2_in, p3_in, p4_in, *messages_in,
+        trace_kernel, [(2 * lines, width)] * 2,
+        pack, other, share, code, rhs, swap(near), fifth_in, sixth_in, p1_in, p2_in, p3_in, p4_in, *messages_in,
         scratch=[pltpu.VMEM(window, F32)] * 5
         + [pltpu.VMEM((window[0], width // 2), F32)] * 2,
     )
-    return (keep + swap(send) * inverse)[None]
+    both = keep + swap(send)
+    return (both[:lines] / both[lines:])[None]
 
 
 def solution(mesh):

time: 39.7 us -> 39.5 us (level)
  Pallas kernels: 9.57 us -> 8.94 us
  waiting for transfers between devices: 7.54 us -> 8.06 us
    ppermute x10, starting transfers between devices: 18.8 us -> 17.2 us  [move(): return lax.ppermute(x, GRID, pairs)]
    ppermute x4, starting transfers between devices: 2.23 us -> 3.69 us  [swap(): return lax.ppermute(x, 'comp', [(0, 1), (1, 0)])]
    pallas_call x8 -> x9, Pallas kernels: 9.57 us -> 8.94 us  [call(): pl.pallas_call(kernel, out_shape=out, in_specs=[pl.BlockSpec(memory_space...]
    ppermute x10, waiting for transfers between devices: 4.31 us -> 4.81 us  [move(): return lax.ppermute(x, GRID, pairs)]
  transfers between devices with their start and end apart: 15 -> 15, of which waited for: 6 -> 7; matrix products, arithmetic and copies ran while one was open for 0% -> 0% of each run, Pallas kernels for 6% -> 7%
where the time goes in v6:
time: 39.5 us; the launch traced here: 39.3 us
  starting transfers between devices  21.6 us (55%)
  Pallas kernels  8.94 us (23%)
  waiting for transfers between devices  8.06 us (20%)
  other arithmetic  0.62 us (2%)
    ppermute x10, starting transfers between devices, move(): return lax.ppermute(x, GRID, pairs)  17.2 us
    pallas_call x9, Pallas kernels, call(): pl.pallas_call(kernel, out_shape=out, in_specs=[pl.BlockSpec(memory_space...  8.94 us
    ppermute x10, waiting for transfers between devices, move(): return lax.ppermute(x, GRID, pairs)  4.81 us
    ppermute x4, starting transfers between devices, swap(): return lax.ppermute(x, 'comp', [(0, 1), (1, 0)])  3.69 us
    ppermute x4, waiting for transfers between devices, swap(): return lax.ppermute(x, 'comp', [(0, 1), (1, 0)])  3.24 us
  transfers between devices with their start and end apart: 15, of which 7 were waited for; matrix products, arithmetic and copies ran while one was open for 0% of the time, Pallas kernels for 7%

profile of v6, /device:TPU:0, one launch (start us, length us, event | category | flops | bytes accessed | tf_op | source)
XLA Modules:
  0.0 39.3 jit_solution(13760662429347240935)
XLA Ops:
  0.0 1.2 %shard_map.64 = (f32[288,256]{1,0:T(8,128)S(1)}, f32[16,256]{1,0:T(8,128)S(1)}) custom-call(s32[8,4096]{1,0:T(8,128)} %cells.1, f32[8,4096]{1,0:T(8,128)} %weights.1, s32[8,4096]{1,0:T(8,128)} %slots.1, f32[1,16,256]{2,1,0:T(8,128)} %state.1, f32[1,16,256]{2,1,0:T(8,128)} %coeff.1, s32[16,256]{1,0:T(8,128)} %vertical.1), custom_call_target="tpu_custom_call" | custom-call | tf_op jit(solution)/shard_map/pallas_call | solution.py:23
  1.2 0.5 %collective-permute-start = (f32[288,256]{1,0:T(8,128)S(1)}, f32[288,256]{1,0:T(8,128)S(1)}, u32[]{:S(2)}, u32[]{:S(2)}) collective-permute-start(f32[288,256]{1,0:T(8,128)S(1)} %get-tuple-element.20.pack), channel_id=1, source_target_pairs={{0,16},{16,0},{1,17},{17,1},{2,18},{18,2},{3,19},{19,3},{4,20},{20... | collective-permute-start | bytes 884744 | tf_op jit(solution)/shard_map/ppermute | solution.py:454
  1.7 1.2 %collective-permute-done.other = f32[288,256]{1,0:T(8,128)S(1)} collective-permute-done((f32[288,256]{1,0:T(8,128)S(1)}, f32[288,256]{1,0:T(8,128)S(1)}, u32[]{:S(2)}, u32[]{:S(2)}) %collective-permute-start) | collective-permute-done | bytes 294944 | tf_op jit(solution)/shard_map/ppermute | solution.py:454
  2.9 0.1 shard_map.66
  3.0 6.0 %collective-permute-start.3 = (f32[120,256]{1,0:T(8,128)S(1)}, f32[120,256]{1,0:T(8,128)S(1)}, u32[]{:S(2)}, u32[]{:S(2)}) collective-permute-start(f32[120,256]{1,0:T(8,128)S(1)} %get-tuple-element.24.own), channel_id=1, source_target_pairs={{2,0},{3,1},{4,2},{5,3},{6,4},{7,5},{8,6},{9,7},{10,8},{11,9},{12,... | collective-permute-start | bytes 368648 | tf_op jit(solution)/shard_map/ppermute | solution.py:459
  9.0 1.4 %collective-permute-start.2 = (f32[120,256]{1,0:T(8,128)S(1)}, f32[120,256]{1,0:T(8,128)S(1)}, u32[]{:S(2)}, u32[]{:S(2)}) collective-permute-start(f32[120,256]{1,0:T(8,128)S(1)} %get-tuple-element.23), channel_id=1, source_target_pairs={{1,0},{2,1},{3,2},{4,3},{5,4},{6,5},{7,6},{8,7},{9,8},{10,9},{11,1... | collective-permute-start | bytes 368648 | tf_op jit(solution)/shard_map/ppermute | solution.py:459
  10.4 0.5 %collective-permute-start.4 = (f32[120,256]{1,0:T(8,128)S(1)}, f32[120,256]{1,0:T(8,128)S(1)}, u32[]{:S(2)}, u32[]{:S(2)}) collective-permute-start(f32[120,256]{1,0:T(8,128)S(1)} %get-tuple-element.25), channel_id=1, source_target_pairs={{3,0},{4,1},{5,2},{6,3},{7,4},{8,5},{9,6},{10,7},{11,8},{12,9},{13... | collective-permute-start | bytes 368648 | tf_op jit(solution)/shard_map/ppermute | solution.py:459
  10.9 0.4 %collective-permute-start.5 = (f32[88,256]{1,0:T(8,128)S(1)}, f32[88,256]{1,0:T(8,128)S(1)}, u32[]{:S(2)}, u32[]{:S(2)}) collective-permute-start(f32[88,256]{1,0:T(8,128)S(1)} %get-tuple-element.27), channel_id=1, source_target_pairs={{4,0},{5,1},{6,2},{7,3},{8,4},{9,5},{10,6},{11,7},{12,8},{13,9},{1... | collective-permute-start | bytes 270344 | tf_op jit(solution)/shard_map/ppermute | solution.py:459
  11.4 1.3 %collective-permute-start.1 = (f32[8,256]{1,0:T(8,128)S(1)}, f32[8,256]{1,0:T(8,128)S(1)}, u32[]{:S(2)}, u32[]{:S(2)}) collective-permute-start(f32[8,256]{1,0:T(8,128)S(1)} %get-tuple-element.22), channel_id=1, source_target_pairs={{5,0},{6,1},{7,2},{8,3},{9,4},{10,5},{11,6},{12,7},{13,8},{14,9},{... | collective-permute-start | bytes 24584 | tf_op jit(solution)/shard_map/ppermute | solution.py:459
  12.7 0.0 collective-permute-done.3.m2
  12.7 2.4 %collective-permute-done.2.m1 = f32[120,256]{1,0:T(8,128)S(1)} collective-permute-done((f32[120,256]{1,0:T(8,128)S(1)}, f32[120,256]{1,0:T(8,128)S(1)}, u32[]{:S(2)}, u32[]{:S(2)}) %collective-permute-start.2) | collective-permute-done | bytes 122912 | tf_op jit(solution)/shard_map/ppermute | solution.py:459
  15.1 1.1 %collective-permute-done.4.m3 = f32[120,256]{1,0:T(8,128)S(1)} collective-permute-done((f32[120,256]{1,0:T(8,128)S(1)}, f32[120,256]{1,0:T(8,128)S(1)}, u32[]{:S(2)}, u32[]{:S(2)}) %collective-permute-start.4) | collective-permute-done | bytes 122912 | tf_op jit(solution)/shard_map/ppermute | solution.py:459
  16.3 1.3 %shard_map.67.total = f32[128,64]{1,0:T(8,128)S(1)} custom-call(f32[120,256]{1,0:T(8,128)S(1)} %collective-permute-done.2.m1, f32[120,256]{1,0:T(8,128)S(1)} %collective-permute-done.3.m2, f32[120,256]{1,0:T(8,128)S(1)} %collective-permute-done.4.m3, f32[288,256]{1,0:T(8,128)S(1)} %get-tuple-element.20.pack, f32[288,256]{1,0:T(8,128)S(1)} %collective-permute-done.other), custom_call_target="tpu_custom_call" | custom-call | tf_op jit(solution)/shard_map/pallas_call | solution.py:23
  17.5 0.9 %collective-permute-done.1.edge = f32[8,256]{1,0:T(8,128)S(1)} collective-permute-done((f32[8,256]{1,0:T(8,128)S(1)}, f32[8,256]{1,0:T(8,128)S(1)}, u32[]{:S(2)}, u32[]{:S(2)}) %collective-permute-start.1) | collective-permute-done | bytes 8224 | tf_op jit(solution)/shard_map/ppermute | solution.py:459
  18.4 0.0 collective-permute-done.5.m4
  18.4 1.3 %shard_map.69.partial = f32[16,256]{1,0:T(8,128)S(1)} custom-call(f32[8,256]{1,0:T(8,128)S(1)} %get-tuple-element.26.edge, f32[88,256]{1,0:T(8,128)S(1)} %collective-permute-done.5.m4, f32[120,256]{1,0:T(8,128)S(1)} %collective-permute-done.2.m1, f32[120,256]{1,0:T(8,128)S(1)} %collective-permute-done.3.m2, f32[120,256]{1,0:T(8,128)S(1)} %collective-permute-done.4.m3, ...), custom_call_target="tpu_custom_call" | custom-call | flops 1000000000 | tf_op jit(solution)/shard_map/pallas_call | solution.py:23
  19.7 0.0 collective-permute-start.6
  19.8 1.2 %collective-permute-done.6.partial_sw = f32[16,256]{1,0:T(8,128)S(1)} collective-permute-done((f32[16,256]{1,0:T(8,128)S(1)}, f32[16,256]{1,0:T(8,128)S(1)}, u32[]{:S(2)}, u32[]{:S(2)}) %collective-permute-start.6) | collective-permute-done | bytes 16416 | tf_op jit(solution)/shard_map/ppermute | solution.py:454
  21.0 4.0 %collective-permute-start.7 = (f32[48,256]{1,0:T(8,128)S(1)}, f32[48,256]{1,0:T(8,128)S(1)}, u32[]{:S(2)}, u32[]{:S(2)}) collective-permute-start(f32[48,256]{1,0:T(8,128)S(1)} %get-tuple-element.30), channel_id=1, source_target_pairs={{1,0},{2,1},{3,2},{4,3},{5,4},{6,5},{7,6},{8,7},{9,8},{10,9},{11,1... | collective-permute-start | bytes 147464 | tf_op jit(solution)/shard_map/ppermute | solution.py:459
  25.0 0.7 %collective-permute-start.8 = (f32[32,256]{1,0:T(8,128)S(1)}, f32[32,256]{1,0:T(8,128)S(1)}, u32[]{:S(2)}, u32[]{:S(2)}) collective-permute-start(f32[32,256]{1,0:T(8,128)S(1)} %get-tuple-element.31), channel_id=1, source_target_pairs={{2,0},{3,1},{4,2},{5,3},{6,4},{7,5},{8,6},{9,7},{10,8},{11,9},{12,... | collective-permute-start | bytes 98312 | tf_op jit(solution)/shard_map/ppermute | solution.py:459
  25.7 0.0 collective-permute-start.10
  25.7 2.4 %collective-permute-start.12 = (f32[16,256]{1,0:T(8,128)S(1)}, f32[16,256]{1,0:T(8,128)S(1)}, u32[]{:S(2)}, u32[]{:S(2)}) collective-permute-start(f32[16,256]{1,0:T(8,128)S(1)} %get-tuple-element.29.own), channel_id=1, source_target_pairs={{3,0},{4,1},{5,2},{6,3},{7,4},{8,5},{9,6},{10,7},{11,8},{12,9},{13... | collective-permute-start | bytes 49160 | tf_op jit(solution)/shard_map/ppermute | solution.py:459
  28.1 0.5 %collective-permute-start.13 = (f32[16,256]{1,0:T(8,128)S(1)}, f32[16,256]{1,0:T(8,128)S(1)}, u32[]{:S(2)}, u32[]{:S(2)}) collective-permute-start(f32[16,256]{1,0:T(8,128)S(1)} %get-tuple-element.29.own), channel_id=1, source_target_pairs={{4,0},{5,1},{6,2},{7,3},{8,4},{9,5},{10,6},{11,7},{12,8},{13,9},{1... | collective-permute-start | bytes 49160 | tf_op jit(solution)/shard_map/ppermute | solution.py:459
  28.5 0.3 collective-permute-done.8.p2
  28.9 0.7 %collective-permute-start.11 = (f32[8,256]{1,0:T(8,128)S(1)}, f32[8,256]{1,0:T(8,128)S(1)}, u32[]{:S(2)}, u32[]{:S(2)}) collective-permute-start(f32[8,256]{1,0:T(8,128)S(1)} %get-tuple-element.32), channel_id=1, source_target_pairs={{16,22},{17,23},{18,24},{19,25},{20,26},{21,27},{22,28},{23,29},{2... | collective-permute-start | bytes 24584 | tf_op jit(solution)/shard_map/ppermute | solution.py:497
  29.5 0.0 collective-permute-done.7.p1
  29.6 1.9 %collective-permute-start.9 = (f32[72,256]{1,0:T(8,128)S(1)}, f32[72,256]{1,0:T(8,128)S(1)}, u32[]{:S(2)}, u32[]{:S(2)}) collective-permute-start(f32[72,256]{1,0:T(8,128)S(1)} %shard_map.71), channel_id=1, source_target_pairs={{0,16},{16,0},{1,17},{17,1},{2,18},{18,2},{3,19},{19,3},{4,20},{20... | collective-permute-start | bytes 221192 | tf_op jit(solution)/shard_map/ppermute | solution.py:454
  31.5 1.3 %shard_map.65.share = f32[16,256]{1,0:T(8,128)S(1)} custom-call(f32[288,256]{1,0:T(8,128)S(1)} %get-tuple-element.20.pack, f32[288,256]{1,0:T(8,128)S(1)} %collective-permute-done.other), custom_call_target="tpu_custom_call" | custom-call | flops 1000000000 | tf_op jit(solution)/shard_map/pallas_call | solution.py:23
  32.8 0.0 collective-permute-done.11.sixth
  32.8 0.0 collective-permute-done.10.fifth
  32.8 0.0 collective-permute-done.12.p3
  32.8 0.0 collective-permute-done.13.p4
  32.9 0.0 collective-permute-done.9.near
  32.9 3.7 %shard_map.72 = (f32[32,256]{1,0:T(8,128)S(1)}, f32[32,256]{1,0:T(8,128)S(1)}) custom-call(f32[288,256]{1,0:T(8,128)S(1)} %get-tuple-element.20.pack, f32[288,256]{1,0:T(8,128)S(1)} %collective-permute-done.other, f32[16,256]{1,0:T(8,128)S(1)} %shard_map.65.share, f32[16,256]{1,0:T(8,128)S(1)} %get-tuple-element.21.code.code_own, ...), custom_call_target="tpu_custom_call" | custom-call | tf_op jit(solution)/shard_map/pallas_call | solution.py:23
  36.6 1.2 %collective-permute-start.14 = (f32[32,256]{1,0:T(8,128)S(1)}, f32[32,256]{1,0:T(8,128)S(1)}, u32[]{:S(2)}, u32[]{:S(2)}) collective-permute-start(f32[32,256]{1,0:T(8,128)S(1)} %get-tuple-element.34), channel_id=1, source_target_pairs={{0,16},{16,0},{1,17},{17,1},{2,18},{18,2},{3,19},{19,3},{4,20},{20... | collective-permute-start | bytes 98312 | tf_op jit(solution)/shard_map/ppermute | solution.py:454
  37.8 0.9 %collective-permute-done.14 = f32[32,256]{1,0:T(8,128)S(1)} collective-permute-done((f32[32,256]{1,0:T(8,128)S(1)}, f32[32,256]{1,0:T(8,128)S(1)}, u32[]{:S(2)}, u32[]{:S(2)}) %collective-permute-start.14) | collective-permute-done | bytes 32800 | tf_op jit(solution)/shard_map/ppermute | solution.py:454
  38.7 0.6 %fusion = f32[1,16,256]{2,1,0:T(8,128)} fusion(f32[32,256]{1,0:T(8,128)S(1)} %add.3), kind=kLoop, calls=%fused_computation.1 | loop fusion | flops 4096 | bytes 49152 | tf_op jit(solution)/shard_map/broadcast_in_dim | solution.py:507
  (4 shorter events, 0.0 us)
Async XLA Ops:
  1.2 1.7 %collective-permute-start = (f32[288,256]{1,0:T(8,128)S(1)}, f32[288,256]{1,0:T(8,128)S(1)}, u32[]{:S(2)}, u32[]{:S(2)}) collective-permute-start(f32[288,256]{1,0:T(8,128)S(1)} %get-tuple-element.20.pack), channel_id=1, source_target_pairs={{0,16},{16,0},{1,17},{17,1},{2,18},{18,2},{3,19},{19,3},{4,20},{20... | collective-permute-start | bytes 884744 | tf_op jit(solution)/shard_map/ppermute | solution.py:454
  3.0 9.7 %collective-permute-start.3 = (f32[120,256]{1,0:T(8,128)S(1)}, f32[120,256]{1,0:T(8,128)S(1)}, u32[]{:S(2)}, u32[]{:S(2)}) collective-permute-start(f32[120,256]{1,0:T(8,128)S(1)} %get-tuple-element.24.own), channel_id=1, source_target_pairs={{2,0},{3,1},{4,2},{5,3},{6,4},{7,5},{8,6},{9,7},{10,8},{11,9},{12,... | collective-permute-start | bytes 368648 | tf_op jit(solution)/shard_map/ppermute | solution.py:459
  9.0 6.1 %collective-permute-start.2 = (f32[120,256]{1,0:T(8,128)S(1)}, f32[120,256]{1,0:T(8,128)S(1)}, u32[]{:S(2)}, u32[]{:S(2)}) collective-permute-start(f32[120,256]{1,0:T(8,128)S(1)} %get-tuple-element.23), channel_id=1, source_target_pairs={{1,0},{2,1},{3,2},{4,3},{5,4},{6,5},{7,6},{8,7},{9,8},{10,9},{11,1... | collective-permute-start | bytes 368648 | tf_op jit(solution)/shard_map/ppermute | solution.py:459
  10.4 5.8 %collective-permute-start.4 = (f32[120,256]{1,0:T(8,128)S(1)}, f32[120,256]{1,0:T(8,128)S(1)}, u32[]{:S(2)}, u32[]{:S(2)}) collective-permute-start(f32[120,256]{1,0:T(8,128)S(1)} %get-tuple-element.25), channel_id=1, source_target_pairs={{3,0},{4,1},{5,2},{6,3},{7,4},{8,5},{9,6},{10,7},{11,8},{12,9},{13... | collective-permute-start | bytes 368648 | tf_op jit(solution)/shard_map/ppermute | solution.py:459
  10.9 7.5 %collective-permute-start.5 = (f32[88,256]{1,0:T(8,128)S(1)}, f32[88,256]{1,0:T(8,128)S(1)}, u32[]{:S(2)}, u32[]{:S(2)}) collective-permute-start(f32[88,256]{1,0:T(8,128)S(1)} %get-tuple-element.27), channel_id=1, source_target_pairs={{4,0},{5,1},{6,2},{7,3},{8,4},{9,5},{10,6},{11,7},{12,8},{13,9},{1... | collective-permute-start | bytes 270344 | tf_op jit(solution)/shard_map/ppermute | solution.py:459
  11.4 7.1 %collective-permute-start.1 = (f32[8,256]{1,0:T(8,128)S(1)}, f32[8,256]{1,0:T(8,128)S(1)}, u32[]{:S(2)}, u32[]{:S(2)}) collective-permute-start(f32[8,256]{1,0:T(8,128)S(1)} %get-tuple-element.22), channel_id=1, source_target_pairs={{5,0},{6,1},{7,2},{8,3},{9,4},{10,5},{11,6},{12,7},{13,8},{14,9},{... | collective-permute-start | bytes 24584 | tf_op jit(solution)/shard_map/ppermute | solution.py:459
  19.7 1.2 %collective-permute-start.6 = (f32[16,256]{1,0:T(8,128)S(1)}, f32[16,256]{1,0:T(8,128)S(1)}, u32[]{:S(2)}, u32[]{:S(2)}) collective-permute-start(f32[16,256]{1,0:T(8,128)S(1)} %shard_map.69.partial), channel_id=1, source_target_pairs={{0,16},{16,0},{1,17},{17,1},{2,18},{18,2},{3,19},{19,3},{4,20},{20... | collective-permute-start | bytes 49160 | tf_op jit(solution)/shard_map/ppermute | solution.py:454
  21.0 8.6 %collective-permute-start.7 = (f32[48,256]{1,0:T(8,128)S(1)}, f32[48,256]{1,0:T(8,128)S(1)}, u32[]{:S(2)}, u32[]{:S(2)}) collective-permute-start(f32[48,256]{1,0:T(8,128)S(1)} %get-tuple-element.30), channel_id=1, source_target_pairs={{1,0},{2,1},{3,2},{4,3},{5,4},{6,5},{7,6},{8,7},{9,8},{10,9},{11,1... | collective-permute-start | bytes 147464 | tf_op jit(solution)/shard_map/ppermute | solution.py:459
  25.0 3.9 %collective-permute-start.8 = (f32[32,256]{1,0:T(8,128)S(1)}, f32[32,256]{1,0:T(8,128)S(1)}, u32[]{:S(2)}, u32[]{:S(2)}) collective-permute-start(f32[32,256]{1,0:T(8,128)S(1)} %get-tuple-element.31), channel_id=1, source_target_pairs={{2,0},{3,1},{4,2},{5,3},{6,4},{7,5},{8,6},{9,7},{10,8},{11,9},{12,... | collective-permute-start | bytes 98312 | tf_op jit(solution)/shard_map/ppermute | solution.py:459
  25.7 7.1 %collective-permute-start.10 = (f32[16,256]{1,0:T(8,128)S(1)}, f32[16,256]{1,0:T(8,128)S(1)}, u32[]{:S(2)}, u32[]{:S(2)}) collective-permute-start(f32[16,256]{1,0:T(8,128)S(1)} %get-tuple-element.29.own), channel_id=1, source_target_pairs={{5,0},{6,1},{7,2},{8,3},{9,4},{10,5},{11,6},{12,7},{13,8},{14,9},{... | collective-permute-start | bytes 49160 | tf_op jit(solution)/shard_map/ppermute | solution.py:459
  25.7 7.1 %collective-permute-start.12 = (f32[16,256]{1,0:T(8,128)S(1)}, f32[16,256]{1,0:T(8,128)S(1)}, u32[]{:S(2)}, u32[]{:S(2)}) collective-permute-start(f32[16,256]{1,0:T(8,128)S(1)} %get-tuple-element.29.own), channel_id=1, source_target_pairs={{3,0},{4,1},{5,2},{6,3},{7,4},{8,5},{9,6},{10,7},{11,8},{12,9},{13... | collective-permute-start | bytes 49160 | tf_op jit(solution)/shard_map/ppermute | solution.py:459
  28.1 4.8 %collective-permute-start.13 = (f32[16,256]{1,0:T(8,128)S(1)}, f32[16,256]{1,0:T(8,128)S(1)}, u32[]{:S(2)}, u32[]{:S(2)}) collective-permute-start(f32[16,256]{1,0:T(8,128)S(1)} %get-tuple-element.29.own), channel_id=1, source_target_pairs={{4,0},{5,1},{6,2},{7,3},{8,4},{9,5},{10,6},{11,7},{12,8},{13,9},{1... | collective-permute-start | bytes 49160 | tf_op jit(solution)/shard_map/ppermute | solution.py:459
  28.9 3.9 %collective-permute-start.11 = (f32[8,256]{1,0:T(8,128)S(1)}, f32[8,256]{1,0:T(8,128)S(1)}, u32[]{:S(2)}, u32[]{:S(2)}) collective-permute-start(f32[8,256]{1,0:T(8,128)S(1)} %get-tuple-element.32), channel_id=1, source_target_pairs={{16,22},{17,23},{18,24},{19,25},{20,26},{21,27},{22,28},{23,29},{2... | collective-permute-start | bytes 24584 | tf_op jit(solution)/shard_map/ppermute | solution.py:497
  29.6 3.3 %collective-permute-start.9 = (f32[72,256]{1,0:T(8,128)S(1)}, f32[72,256]{1,0:T(8,128)S(1)}, u32[]{:S(2)}, u32[]{:S(2)}) collective-permute-start(f32[72,256]{1,0:T(8,128)S(1)} %shard_map.71), channel_id=1, source_target_pairs={{0,16},{16,0},{1,17},{17,1},{2,18},{18,2},{3,19},{19,3},{4,20},{20... | collective-permute-start | bytes 221192 | tf_op jit(solution)/shard_map/ppermute | solution.py:454
  36.6 2.1 %collective-permute-start.14 = (f32[32,256]{1,0:T(8,128)S(1)}, f32[32,256]{1,0:T(8,128)S(1)}, u32[]{:S(2)}, u32[]{:S(2)}) collective-permute-start(f32[32,256]{1,0:T(8,128)S(1)} %get-tuple-element.34), channel_id=1, source_target_pairs={{0,16},{16,0},{1,17},{17,1},{2,18},{18,2},{3,19},{19,3},{4,20},{20... | collective-permute-start | bytes 98312 | tf_op jit(solution)/shard_map/ppermute | solution.py:454

commit v7 on v6

--- a/solution.py
+++ b/solution.py
@@ -407,15 +407,8 @@
         write(last - 1)
 
     def repeat(count, skip):
-        def several(_, carry):
-            for _ in range(8):
-                sweep(skip, groups - skip)
-            return carry
-
-        for _ in range(count % 8):
+        for _ in range(count):
             sweep(skip, groups - skip)
-        if count >= 8:
-            lax.fori_loop(0, count // 8, several, 0)
 
     done = 1
     for skip in range(3):

time: 39.5 us -> 39.5 us (level)
  no operation moved by 1% of the time
where the time goes in v7:
time: 39.5 us; the launch traced here: 39.3 us
  starting transfers between devices  21.6 us (55%)
  Pallas kernels  8.94 us (23%)
  waiting for transfers between devices  8.06 us (20%)
  other arithmetic  0.62 us (2%)
    ppermute x10, starting transfers between devices, move(): return lax.ppermute(x, GRID, pairs)  17.2 us
    pallas_call x9, Pallas kernels, call(): pl.pallas_call(kernel, out_shape=out, in_specs=[pl.BlockSpec(memory_space...  8.94 us
    ppermute x10, waiting for transfers between devices, move(): return lax.ppermute(x, GRID, pairs)  4.81 us
    ppermute x4, starting transfers between devices, swap(): return lax.ppermute(x, 'comp', [(0, 1), (1, 0)])  3.69 us
    ppermute x4, waiting for transfers between devices, swap(): return lax.ppermute(x, 'comp', [(0, 1), (1, 0)])  3.24 us
  transfers between devices with their start and end apart: 15, of which 7 were waited for; matrix products, arithmetic and copies ran while one was open for 0% of the time, Pallas kernels for 7%

profile of v7, /device:TPU:0, one launch (start us, length us, event | category | flops | bytes accessed | tf_op | source)
XLA Modules:
  0.0 39.3 jit_solution(13760662429347240935)
XLA Ops:
  0.0 1.2 %shard_map.64 = (f32[288,256]{1,0:T(8,128)S(1)}, f32[16,256]{1,0:T(8,128)S(1)}) custom-call(s32[8,4096]{1,0:T(8,128)} %cells.1, f32[8,4096]{1,0:T(8,128)} %weights.1, s32[8,4096]{1,0:T(8,128)} %slots.1, f32[1,16,256]{2,1,0:T(8,128)} %state.1, f32[1,16,256]{2,1,0:T(8,128)} %coeff.1, s32[16,256]{1,0:T(8,128)} %vertical.1), custom_call_target="tpu_custom_call" | custom-call | tf_op jit(solution)/shard_map/pallas_call | solution.py:23
  1.2 0.5 %collective-permute-start = (f32[288,256]{1,0:T(8,128)S(1)}, f32[288,256]{1,0:T(8,128)S(1)}, u32[]{:S(2)}, u32[]{:S(2)}) collective-permute-start(f32[288,256]{1,0:T(8,128)S(1)} %get-tuple-element.20.pack), channel_id=1, source_target_pairs={{0,16},{16,0},{1,17},{17,1},{2,18},{18,2},{3,19},{19,3},{4,20},{20... | collective-permute-start | bytes 884744 | tf_op jit(solution)/shard_map/ppermute | solution.py:447
  1.7 1.2 %collective-permute-done.other = f32[288,256]{1,0:T(8,128)S(1)} collective-permute-done((f32[288,256]{1,0:T(8,128)S(1)}, f32[288,256]{1,0:T(8,128)S(1)}, u32[]{:S(2)}, u32[]{:S(2)}) %collective-permute-start) | collective-permute-done | bytes 294944 | tf_op jit(solution)/shard_map/ppermute | solution.py:447
  2.9 0.1 shard_map.66
  3.0 6.0 %collective-permute-start.3 = (f32[120,256]{1,0:T(8,128)S(1)}, f32[120,256]{1,0:T(8,128)S(1)}, u32[]{:S(2)}, u32[]{:S(2)}) collective-permute-start(f32[120,256]{1,0:T(8,128)S(1)} %get-tuple-element.24.own), channel_id=1, source_target_pairs={{2,0},{3,1},{4,2},{5,3},{6,4},{7,5},{8,6},{9,7},{10,8},{11,9},{12,... | collective-permute-start | bytes 368648 | tf_op jit(solution)/shard_map/ppermute | solution.py:452
  9.0 1.4 %collective-permute-start.2 = (f32[120,256]{1,0:T(8,128)S(1)}, f32[120,256]{1,0:T(8,128)S(1)}, u32[]{:S(2)}, u32[]{:S(2)}) collective-permute-start(f32[120,256]{1,0:T(8,128)S(1)} %get-tuple-element.23), channel_id=1, source_target_pairs={{1,0},{2,1},{3,2},{4,3},{5,4},{6,5},{7,6},{8,7},{9,8},{10,9},{11,1... | collective-permute-start | bytes 368648 | tf_op jit(solution)/shard_map/ppermute | solution.py:452
  10.4 0.5 %collective-permute-start.4 = (f32[120,256]{1,0:T(8,128)S(1)}, f32[120,256]{1,0:T(8,128)S(1)}, u32[]{:S(2)}, u32[]{:S(2)}) collective-permute-start(f32[120,256]{1,0:T(8,128)S(1)} %get-tuple-element.25), channel_id=1, source_target_pairs={{3,0},{4,1},{5,2},{6,3},{7,4},{8,5},{9,6},{10,7},{11,8},{12,9},{13... | collective-permute-start | bytes 368648 | tf_op jit(solution)/shard_map/ppermute | solution.py:452
  10.9 0.4 %collective-permute-start.5 = (f32[88,256]{1,0:T(8,128)S(1)}, f32[88,256]{1,0:T(8,128)S(1)}, u32[]{:S(2)}, u32[]{:S(2)}) collective-permute-start(f32[88,256]{1,0:T(8,128)S(1)} %get-tuple-element.27), channel_id=1, source_target_pairs={{4,0},{5,1},{6,2},{7,3},{8,4},{9,5},{10,6},{11,7},{12,8},{13,9},{1... | collective-permute-start | bytes 270344 | tf_op jit(solution)/shard_map/ppermute | solution.py:452
  11.4 1.3 %collective-permute-start.1 = (f32[8,256]{1,0:T(8,128)S(1)}, f32[8,256]{1,0:T(8,128)S(1)}, u32[]{:S(2)}, u32[]{:S(2)}) collective-permute-start(f32[8,256]{1,0:T(8,128)S(1)} %get-tuple-element.22), channel_id=1, source_target_pairs={{5,0},{6,1},{7,2},{8,3},{9,4},{10,5},{11,6},{12,7},{13,8},{14,9},{... | collective-permute-start | bytes 24584 | tf_op jit(solution)/shard_map/ppermute | solution.py:452
  12.7 0.0 collective-permute-done.3.m2
  12.7 2.4 %collective-permute-done.2.m1 = f32[120,256]{1,0:T(8,128)S(1)} collective-permute-done((f32[120,256]{1,0:T(8,128)S(1)}, f32[120,256]{1,0:T(8,128)S(1)}, u32[]{:S(2)}, u32[]{:S(2)}) %collective-permute-start.2) | collective-permute-done | bytes 122912 | tf_op jit(solution)/shard_map/ppermute | solution.py:452
  15.1 1.1 %collective-permute-done.4.m3 = f32[120,256]{1,0:T(8,128)S(1)} collective-permute-done((f32[120,256]{1,0:T(8,128)S(1)}, f32[120,256]{1,0:T(8,128)S(1)}, u32[]{:S(2)}, u32[]{:S(2)}) %collective-permute-start.4) | collective-permute-done | bytes 122912 | tf_op jit(solution)/shard_map/ppermute | solution.py:452
  16.3 1.3 %shard_map.67.total = f32[128,64]{1,0:T(8,128)S(1)} custom-call(f32[120,256]{1,0:T(8,128)S(1)} %collective-permute-done.2.m1, f32[120,256]{1,0:T(8,128)S(1)} %collective-permute-done.3.m2, f32[120,256]{1,0:T(8,128)S(1)} %collective-permute-done.4.m3, f32[288,256]{1,0:T(8,128)S(1)} %get-tuple-element.20.pack, f32[288,256]{1,0:T(8,128)S(1)} %collective-permute-done.other), custom_call_target="tpu_custom_call" | custom-call | tf_op jit(solution)/shard_map/pallas_call | solution.py:23
  17.5 0.9 %collective-permute-done.1.edge = f32[8,256]{1,0:T(8,128)S(1)} collective-permute-done((f32[8,256]{1,0:T(8,128)S(1)}, f32[8,256]{1,0:T(8,128)S(1)}, u32[]{:S(2)}, u32[]{:S(2)}) %collective-permute-start.1) | collective-permute-done | bytes 8224 | tf_op jit(solution)/shard_map/ppermute | solution.py:452
  18.4 0.0 collective-permute-done.5.m4
  18.4 1.3 %shard_map.69.partial = f32[16,256]{1,0:T(8,128)S(1)} custom-call(f32[8,256]{1,0:T(8,128)S(1)} %get-tuple-element.26.edge, f32[88,256]{1,0:T(8,128)S(1)} %collective-permute-done.5.m4, f32[120,256]{1,0:T(8,128)S(1)} %collective-permute-done.2.m1, f32[120,256]{1,0:T(8,128)S(1)} %collective-permute-done.3.m2, f32[120,256]{1,0:T(8,128)S(1)} %collective-permute-done.4.m3, ...), custom_call_target="tpu_custom_call" | custom-call | flops 1000000000 | tf_op jit(solution)/shard_map/pallas_call | solution.py:23
  19.7 0.0 collective-permute-start.6
  19.8 1.2 %collective-permute-done.6.partial_sw = f32[16,256]{1,0:T(8,128)S(1)} collective-permute-done((f32[16,256]{1,0:T(8,128)S(1)}, f32[16,256]{1,0:T(8,128)S(1)}, u32[]{:S(2)}, u32[]{:S(2)}) %collective-permute-start.6) | collective-permute-done | bytes 16416 | tf_op jit(solution)/shard_map/ppermute | solution.py:447
  21.0 4.0 %collective-permute-start.7 = (f32[48,256]{1,0:T(8,128)S(1)}, f32[48,256]{1,0:T(8,128)S(1)}, u32[]{:S(2)}, u32[]{:S(2)}) collective-permute-start(f32[48,256]{1,0:T(8,128)S(1)} %get-tuple-element.30), channel_id=1, source_target_pairs={{1,0},{2,1},{3,2},{4,3},{5,4},{6,5},{7,6},{8,7},{9,8},{10,9},{11,1... | collective-permute-start | bytes 147464 | tf_op jit(solution)/shard_map/ppermute | solution.py:452
  25.0 0.7 %collective-permute-start.8 = (f32[32,256]{1,0:T(8,128)S(1)}, f32[32,256]{1,0:T(8,128)S(1)}, u32[]{:S(2)}, u32[]{:S(2)}) collective-permute-start(f32[32,256]{1,0:T(8,128)S(1)} %get-tuple-element.31), channel_id=1, source_target_pairs={{2,0},{3,1},{4,2},{5,3},{6,4},{7,5},{8,6},{9,7},{10,8},{11,9},{12,... | collective-permute-start | bytes 98312 | tf_op jit(solution)/shard_map/ppermute | solution.py:452
  25.7 0.0 collective-permute-start.10
  25.7 2.4 %collective-permute-start.12 = (f32[16,256]{1,0:T(8,128)S(1)}, f32[16,256]{1,0:T(8,128)S(1)}, u32[]{:S(2)}, u32[]{:S(2)}) collective-permute-start(f32[16,256]{1,0:T(8,128)S(1)} %get-tuple-element.29.own), channel_id=1, source_target_pairs={{3,0},{4,1},{5,2},{6,3},{7,4},{8,5},{9,6},{10,7},{11,8},{12,9},{13... | collective-permute-start | bytes 49160 | tf_op jit(solution)/shard_map/ppermute | solution.py:452
  28.1 0.5 %collective-permute-start.13 = (f32[16,256]{1,0:T(8,128)S(1)}, f32[16,256]{1,0:T(8,128)S(1)}, u32[]{:S(2)}, u32[]{:S(2)}) collective-permute-start(f32[16,256]{1,0:T(8,128)S(1)} %get-tuple-element.29.own), channel_id=1, source_target_pairs={{4,0},{5,1},{6,2},{7,3},{8,4},{9,5},{10,6},{11,7},{12,8},{13,9},{1... | collective-permute-start | bytes 49160 | tf_op jit(solution)/shard_map/ppermute | solution.py:452
  28.5 0.3 collective-permute-done.8.p2
  28.9 0.7 %collective-permute-start.11 = (f32[8,256]{1,0:T(8,128)S(1)}, f32[8,256]{1,0:T(8,128)S(1)}, u32[]{:S(2)}, u32[]{:S(2)}) collective-permute-start(f32[8,256]{1,0:T(8,128)S(1)} %get-tuple-element.32), channel_id=1, source_target_pairs={{16,22},{17,23},{18,24},{19,25},{20,26},{21,27},{22,28},{23,29},{2... | collective-permute-start | bytes 24584 | tf_op jit(solution)/shard_map/ppermute | solution.py:490
  29.5 0.0 collective-permute-done.7.p1
  29.6 1.9 %collective-permute-start.9 = (f32[72,256]{1,0:T(8,128)S(1)}, f32[72,256]{1,0:T(8,128)S(1)}, u32[]{:S(2)}, u32[]{:S(2)}) collective-permute-start(f32[72,256]{1,0:T(8,128)S(1)} %shard_map.71), channel_id=1, source_target_pairs={{0,16},{16,0},{1,17},{17,1},{2,18},{18,2},{3,19},{19,3},{4,20},{20... | collective-permute-start | bytes 221192 | tf_op jit(solution)/shard_map/ppermute | solution.py:447
  31.5 1.3 %shard_map.65.share = f32[16,256]{1,0:T(8,128)S(1)} custom-call(f32[288,256]{1,0:T(8,128)S(1)} %get-tuple-element.20.pack, f32[288,256]{1,0:T(8,128)S(1)} %collective-permute-done.other), custom_call_target="tpu_custom_call" | custom-call | flops 1000000000 | tf_op jit(solution)/shard_map/pallas_call | solution.py:23
  32.8 0.0 collective-permute-done.11.sixth
  32.8 0.0 collective-permute-done.10.fifth
  32.8 0.0 collective-permute-done.12.p3
  32.8 0.0 collective-permute-done.13.p4
  32.9 0.0 collective-permute-done.9.near
  32.9 3.7 %shard_map.72 = (f32[32,256]{1,0:T(8,128)S(1)}, f32[32,256]{1,0:T(8,128)S(1)}) custom-call(f32[288,256]{1,0:T(8,128)S(1)} %get-tuple-element.20.pack, f32[288,256]{1,0:T(8,128)S(1)} %collective-permute-done.other, f32[16,256]{1,0:T(8,128)S(1)} %shard_map.65.share, f32[16,256]{1,0:T(8,128)S(1)} %get-tuple-element.21.code.code_own, ...), custom_call_target="tpu_custom_call" | custom-call | tf_op jit(solution)/shard_map/pallas_call | solution.py:23
  36.6 1.2 %collective-permute-start.14 = (f32[32,256]{1,0:T(8,128)S(1)}, f32[32,256]{1,0:T(8,128)S(1)}, u32[]{:S(2)}, u32[]{:S(2)}) collective-permute-start(f32[32,256]{1,0:T(8,128)S(1)} %get-tuple-element.34), channel_id=1, source_target_pairs={{0,16},{16,0},{1,17},{17,1},{2,18},{18,2},{3,19},{19,3},{4,20},{20... | collective-permute-start | bytes 98312 | tf_op jit(solution)/shard_map/ppermute | solution.py:447
  37.8 0.9 %collective-permute-done.14 = f32[32,256]{1,0:T(8,128)S(1)} collective-permute-done((f32[32,256]{1,0:T(8,128)S(1)}, f32[32,256]{1,0:T(8,128)S(1)}, u32[]{:S(2)}, u32[]{:S(2)}) %collective-permute-start.14) | collective-permute-done | bytes 32800 | tf_op jit(solution)/shard_map/ppermute | solution.py:447
  38.7 0.6 %fusion = f32[1,16,256]{2,1,0:T(8,128)} fusion(f32[32,256]{1,0:T(8,128)S(1)} %add.3), kind=kLoop, calls=%fused_computation.1 | loop fusion | flops 4096 | bytes 49152 | tf_op jit(solution)/shard_map/broadcast_in_dim | solution.py:500
  (4 shorter events, 0.0 us)
Async XLA Ops:
  1.2 1.7 %collective-permute-start = (f32[288,256]{1,0:T(8,128)S(1)}, f32[288,256]{1,0:T(8,128)S(1)}, u32[]{:S(2)}, u32[]{:S(2)}) collective-permute-start(f32[288,256]{1,0:T(8,128)S(1)} %get-tuple-element.20.pack), channel_id=1, source_target_pairs={{0,16},{16,0},{1,17},{17,1},{2,18},{18,2},{3,19},{19,3},{4,20},{20... | collective-permute-start | bytes 884744 | tf_op jit(solution)/shard_map/ppermute | solution.py:447
  3.0 9.7 %collective-permute-start.3 = (f32[120,256]{1,0:T(8,128)S(1)}, f32[120,256]{1,0:T(8,128)S(1)}, u32[]{:S(2)}, u32[]{:S(2)}) collective-permute-start(f32[120,256]{1,0:T(8,128)S(1)} %get-tuple-element.24.own), channel_id=1, source_target_pairs={{2,0},{3,1},{4,2},{5,3},{6,4},{7,5},{8,6},{9,7},{10,8},{11,9},{12,... | collective-permute-start | bytes 368648 | tf_op jit(solution)/shard_map/ppermute | solution.py:452
  9.0 6.1 %collective-permute-start.2 = (f32[120,256]{1,0:T(8,128)S(1)}, f32[120,256]{1,0:T(8,128)S(1)}, u32[]{:S(2)}, u32[]{:S(2)}) collective-permute-start(f32[120,256]{1,0:T(8,128)S(1)} %get-tuple-element.23), channel_id=1, source_target_pairs={{1,0},{2,1},{3,2},{4,3},{5,4},{6,5},{7,6},{8,7},{9,8},{10,9},{11,1... | collective-permute-start | bytes 368648 | tf_op jit(solution)/shard_map/ppermute | solution.py:452
  10.4 5.8 %collective-permute-start.4 = (f32[120,256]{1,0:T(8,128)S(1)}, f32[120,256]{1,0:T(8,128)S(1)}, u32[]{:S(2)}, u32[]{:S(2)}) collective-permute-start(f32[120,256]{1,0:T(8,128)S(1)} %get-tuple-element.25), channel_id=1, source_target_pairs={{3,0},{4,1},{5,2},{6,3},{7,4},{8,5},{9,6},{10,7},{11,8},{12,9},{13... | collective-permute-start | bytes 368648 | tf_op jit(solution)/shard_map/ppermute | solution.py:452
  10.9 7.5 %collective-permute-start.5 = (f32[88,256]{1,0:T(8,128)S(1)}, f32[88,256]{1,0:T(8,128)S(1)}, u32[]{:S(2)}, u32[]{:S(2)}) collective-permute-start(f32[88,256]{1,0:T(8,128)S(1)} %get-tuple-element.27), channel_id=1, source_target_pairs={{4,0},{5,1},{6,2},{7,3},{8,4},{9,5},{10,6},{11,7},{12,8},{13,9},{1... | collective-permute-start | bytes 270344 | tf_op jit(solution)/shard_map/ppermute | solution.py:452
  11.4 7.1 %collective-permute-start.1 = (f32[8,256]{1,0:T(8,128)S(1)}, f32[8,256]{1,0:T(8,128)S(1)}, u32[]{:S(2)}, u32[]{:S(2)}) collective-permute-start(f32[8,256]{1,0:T(8,128)S(1)} %get-tuple-element.22), channel_id=1, source_target_pairs={{5,0},{6,1},{7,2},{8,3},{9,4},{10,5},{11,6},{12,7},{13,8},{14,9},{... | collective-permute-start | bytes 24584 | tf_op jit(solution)/shard_map/ppermute | solution.py:452
  19.7 1.2 %collective-permute-start.6 = (f32[16,256]{1,0:T(8,128)S(1)}, f32[16,256]{1,0:T(8,128)S(1)}, u32[]{:S(2)}, u32[]{:S(2)}) collective-permute-start(f32[16,256]{1,0:T(8,128)S(1)} %shard_map.69.partial), channel_id=1, source_target_pairs={{0,16},{16,0},{1,17},{17,1},{2,18},{18,2},{3,19},{19,3},{4,20},{20... | collective-permute-start | bytes 49160 | tf_op jit(solution)/shard_map/ppermute | solution.py:447
  21.0 8.6 %collective-permute-start.7 = (f32[48,256]{1,0:T(8,128)S(1)}, f32[48,256]{1,0:T(8,128)S(1)}, u32[]{:S(2)}, u32[]{:S(2)}) collective-permute-start(f32[48,256]{1,0:T(8,128)S(1)} %get-tuple-element.30), channel_id=1, source_target_pairs={{1,0},{2,1},{3,2},{4,3},{5,4},{6,5},{7,6},{8,7},{9,8},{10,9},{11,1... | collective-permute-start | bytes 147464 | tf_op jit(solution)/shard_map/ppermute | solution.py:452
  25.0 3.9 %collective-permute-start.8 = (f32[32,256]{1,0:T(8,128)S(1)}, f32[32,256]{1,0:T(8,128)S(1)}, u32[]{:S(2)}, u32[]{:S(2)}) collective-permute-start(f32[32,256]{1,0:T(8,128)S(1)} %get-tuple-element.31), channel_id=1, source_target_pairs={{2,0},{3,1},{4,2},{5,3},{6,4},{7,5},{8,6},{9,7},{10,8},{11,9},{12,... | collective-permute-start | bytes 98312 | tf_op jit(solution)/shard_map/ppermute | solution.py:452
  25.7 7.1 %collective-permute-start.10 = (f32[16,256]{1,0:T(8,128)S(1)}, f32[16,256]{1,0:T(8,128)S(1)}, u32[]{:S(2)}, u32[]{:S(2)}) collective-permute-start(f32[16,256]{1,0:T(8,128)S(1)} %get-tuple-element.29.own), channel_id=1, source_target_pairs={{5,0},{6,1},{7,2},{8,3},{9,4},{10,5},{11,6},{12,7},{13,8},{14,9},{... | collective-permute-start | bytes 49160 | tf_op jit(solution)/shard_map/ppermute | solution.py:452
  25.7 7.1 %collective-permute-start.12 = (f32[16,256]{1,0:T(8,128)S(1)}, f32[16,256]{1,0:T(8,128)S(1)}, u32[]{:S(2)}, u32[]{:S(2)}) collective-permute-start(f32[16,256]{1,0:T(8,128)S(1)} %get-tuple-element.29.own), channel_id=1, source_target_pairs={{3,0},{4,1},{5,2},{6,3},{7,4},{8,5},{9,6},{10,7},{11,8},{12,9},{13... | collective-permute-start | bytes 49160 | tf_op jit(solution)/shard_map/ppermute | solution.py:452
  28.1 4.8 %collective-permute-start.13 = (f32[16,256]{1,0:T(8,128)S(1)}, f32[16,256]{1,0:T(8,128)S(1)}, u32[]{:S(2)}, u32[]{:S(2)}) collective-permute-start(f32[16,256]{1,0:T(8,128)S(1)} %get-tuple-element.29.own), channel_id=1, source_target_pairs={{4,0},{5,1},{6,2},{7,3},{8,4},{9,5},{10,6},{11,7},{12,8},{13,9},{1... | collective-permute-start | bytes 49160 | tf_op jit(solution)/shard_map/ppermute | solution.py:452
  28.9 3.9 %collective-permute-start.11 = (f32[8,256]{1,0:T(8,128)S(1)}, f32[8,256]{1,0:T(8,128)S(1)}, u32[]{:S(2)}, u32[]{:S(2)}) collective-permute-start(f32[8,256]{1,0:T(8,128)S(1)} %get-tuple-element.32), channel_id=1, source_target_pairs={{16,22},{17,23},{18,24},{19,25},{20,26},{21,27},{22,28},{23,29},{2... | collective-permute-start | bytes 24584 | tf_op jit(solution)/shard_map/ppermute | solution.py:490
  29.6 3.3 %collective-permute-start.9 = (f32[72,256]{1,0:T(8,128)S(1)}, f32[72,256]{1,0:T(8,128)S(1)}, u32[]{:S(2)}, u32[]{:S(2)}) collective-permute-start(f32[72,256]{1,0:T(8,128)S(1)} %shard_map.71), channel_id=1, source_target_pairs={{0,16},{16,0},{1,17},{17,1},{2,18},{18,2},{3,19},{19,3},{4,20},{20... | collective-permute-start | bytes 221192 | tf_op jit(solution)/shard_map/ppermute | solution.py:447
  36.6 2.1 %collective-permute-start.14 = (f32[32,256]{1,0:T(8,128)S(1)}, f32[32,256]{1,0:T(8,128)S(1)}, u32[]{:S(2)}, u32[]{:S(2)}) collective-permute-start(f32[32,256]{1,0:T(8,128)S(1)} %get-tuple-element.34), channel_id=1, source_target_pairs={{0,16},{16,0},{1,17},{17,1},{2,18},{18,2},{3,19},{19,3},{4,20},{20... | collective-permute-start | bytes 98312 | tf_op jit(solution)/shard_map/ppermute | solution.py:447
